TPU v7x, 256 devices: a whole 4x4x8 slice. The times are simulated.
256 devices in a mesh: gx: 16 (over x, z_lo, core), gy: 16 (over z_hi, y).
Axes of the slice: x: 4, y: 4, z: 8 (z_hi: 4, z_lo: 2; z = z_hi * 2 + z_lo), core: 2. Of those that a mesh axis runs over, the one named last changes fastest.
Arguments:
- p_now: float32 [256, 256, 128], P('gx', 'gy'), may hold values from -6 to 6
- p_prev: float32 [256, 256, 128], P('gx', 'gy'), may hold values from -6 to 6
- water_coef: float32 [256, 256, 128], P('gx', 'gy'), may hold values from 0.05 to 0.3
- seafloor: int32 [256, 512], P('gx', 'gy'), may hold values from -1 to 127, as said below
- u_now: float32 [3, 256, 512, 128], P(None, 'gx', 'gy'), may hold values from -6 to 6
- u_prev: float32 [3, 256, 512, 128], P(None, 'gx', 'gy'), may hold values from -6 to 6
- shear: float32 [256, 512, 128], P('gx', 'gy'), may hold values from 0.03 to 0.1
- bulk: float32 [256, 512, 128], P('gx', 'gy'), may hold values from 0.03 to 0.1
- recv_field: bfloat16 [4, 256, 512, 128], P(None, 'gx', 'gy'), may hold values from -6 to 6
Outputs:
- pressure_out: float32 [256, 256, 128], P('gx', 'gy')
- displacement_out: float32 [3, 256, 512, 128], P(None, 'gx', 'gy')
- image: bfloat16 [21, 256, 512, 128], P(None, 'gx', 'gy')
Inputs may be any that keep to these rules, and one draw needn't show every extreme that they name: For every column exactly one of its two rows (depth halves) is 0 or more (the seafloor cell within that half); the other is -1.
All inputs are finite; a program needn't handle non-finite values.
Results may differ from a plain program's by a relative error of at most 0.001.
Values sent between devices are 32-bit elements; how exact they have to be, the bound alone decides.
No kernel may reach another device: no remote copies, remote signals or barrier semaphores. Data moves between devices by JAX's collectives and lax.ppermute only.
A program may use at most 128 MiB of HBM per device.

v0:
```python
import jax
import jax.numpy as jnp
from jax import lax
from jax.experimental import pallas as pl
from jax.experimental.pallas import tpu as pltpu
from jax.sharding import PartitionSpec as P

LAG = 10
STEPS = 4
LOAD = 0.5
F32 = jnp.float32
XS = 16
SOLID = 40
WATER = 24
DEPTH = 128
VN_LANE = 96
PB_LANE = 112
VMEM = pl.BlockSpec(memory_space=pltpu.VMEM)
PARAMS = pltpu.CompilerParams(vmem_limit_bytes=40 * 1024 * 1024)


def iota(shape, dim):
    return lax.broadcasted_iota(jnp.int32, shape, dim)


def turned(value, shift, axis):
    return pltpu.roll(value, shift % value.shape[axis], axis)


def after_y(value):
    return turned(value, -1, 0)


def before_y(value):
    return turned(value, 1, 0)


def after_z(value, ghost):
    return jnp.where(iota(value.shape, 1) == DEPTH - 1, ghost, turned(value, -1, 1))


def before_z(value, ghost):
    return jnp.where(iota(value.shape, 1) == 0, ghost, turned(value, 1, 1))


def slot(component, x):
    return 32 * component + x + 1


def coordinates():
    gx = lax.axis_index("gx")
    gy = lax.axis_index("gy")
    return gx, gy // 2, gy % 2


def edge_plane(rows, half, solid_of, vn_of, water_of):
    lane = iota((SOLID, DEPTH), 1)
    lane_of_half = lane - half
    sub = iota((8, DEPTH), 0)
    packed = jnp.zeros((SOLID, DEPTH), F32)
    bottom = jnp.zeros((WATER, DEPTH), F32)
    lane_w = iota((WATER, DEPTH), 1)
    for x in range(XS):
        for component in range(3):
            at = slot(component, x)
            packed = jnp.where(lane_of_half == at, turned(solid_of(component, x), at + 1, 1), packed)
        packed = jnp.where(lane == VN_LANE + x, vn_of(x), packed)
        bottom = jnp.where(
            lane_w == PB_LANE + x, turned(water_of(x), PB_LANE + x + 1, 1), bottom
        )
    low = half == 0
    zero = jnp.zeros((8, DEPTH), F32)
    own0, own1, own2 = bottom[0:8], bottom[8:16], bottom[16:24]
    keep = (sub < 4) != low
    spread = jnp.concatenate(
        [
            jnp.where(low, own0, zero),
            jnp.where(low, own1, zero),
            jnp.where(low, zero, own0),
            jnp.where(low, zero, own1),
            jnp.where(keep, own2, zero),
        ],
        axis=0,
    )
    return packed + spread


def velocity_of(now, before, contact_field):
    return jnp.sum(
        jnp.where(contact_field == 1.0, now - before, 0.0), axis=1, keepdims=True
    )


def paired(first, second, swap):
    return jnp.where(swap, first, turned(second, 4, 0))


def pack_kernel(
    d_ref, un_hbm, up_hbm, s_hbm, b_hbm, pn_hbm, pp_hbm, c_hbm,
    ya_ref, yb_ref, wi_ref, wo_ref,
    un, up, s_v, b_v, pn, pp, c_v, sems,
):
    gx, block, half = coordinates()
    even = block % 2 == 0
    upper = half == 0
    copies = []
    for k, (src, dst, rows) in enumerate(
        ((un_hbm, un, 24), (up_hbm, up, 24), (s_hbm, s_v, 24), (b_hbm, b_v, 24),
         (pn_hbm, pn, 8), (pp_hbm, pp, 8), (c_hbm, c_v, 8))
    ):
        for side, start in enumerate((0, rows)):
            if k < 2:
                source = src.at[:, :, pl.ds(start, 8)]
            else:
                source = src.at[:, pl.ds(start, 8)]
            copy = pltpu.make_async_copy(source, dst.at[side], sems.at[2 * k + side])
            copy.start()
            copies.append(copy)
    for copy in copies:
        copy.wait()
    sub = iota((8, DEPTH), 0)
    low = sub < 4
    for x in range(XS):
        sides = []
        for side, rows in ((0, pl.ds(0, 8)), (1, pl.ds(24, 8))):
            d = d_ref[x, rows]
            inside = d >= 1.0
            u = [jnp.where(inside, un[side, c, x], 0.0) for c in range(3)]
            v = [jnp.where(inside, up[side, c, x], 0.0) for c in range(3)]
            spare = 3 if side == 0 else 4
            for c in range(3):
                row = c if side == 0 else 5 + c
                v[c] = jnp.where(sub == spare, turned(d, spare - row, 0), v[c])
            s = jnp.where(inside, s_v[side, x], 0.0)
            b = jnp.where(inside, b_v[side, x], 0.0)
            keep = low if side == 0 else jnp.logical_not(low)
            sides.append(
                [paired(u[0], u[1], keep), paired(u[2], v[0], keep),
                 paired(v[1], v[2], keep), paired(s, b, keep)]
            )
        for k in range(4):
            head, tail = sides[0][k], sides[1][k]
            ya_ref[k, x] = jnp.where(even, tail, head)
            yb_ref[k, x] = jnp.where(even, head, tail)

    def water(target, inner, write):
        keep = low == (upper != inner)
        for x in range(XS):
            def pick(ref, at):
                return jnp.where(upper == inner, ref[1, at], ref[0, at])

            write(target, x, paired(pick(pn, x), pick(pp, x), keep))
            if x < 8:
                write(target, XS + x, paired(pick(c_v, x), pick(c_v, x + 8), keep))

    def write(ref, at, value):
        ref[at] = value

    water(wi_ref, True, write)
    water(wo_ref, False, write)


def send_faces(solid_of, water_of, a_ref, b_ref):
    even = lax.axis_index("gx") % 2 == 0
    for c in range(3):
        head, tail = solid_of(c, 0), solid_of(c, XS - 1)
        a_ref[pl.ds(SOLID * c, SOLID)] = jnp.where(even, tail, head)
        b_ref[pl.ds(SOLID * c, SOLID)] = jnp.where(even, head, tail)
    head, tail = water_of(0), water_of(XS - 1)
    a_ref[pl.ds(3 * SOLID, WATER)] = jnp.where(even, tail, head)
    b_ref[pl.ds(3 * SOLID, WATER)] = jnp.where(even, head, tail)


def received(a_ref, b_ref, rows):
    gx = lax.axis_index("gx")
    even = gx % 2 == 0
    a, b = a_ref[rows], b_ref[rows]
    before = jnp.where(gx > 0, jnp.where(even, b, a), 0.0)
    after = jnp.where(gx < lax.axis_size("gx") - 1, jnp.where(even, a, b), 0.0)
    return before, after


def corner_kernel(edge_ref, a_ref, b_ref, out_ref):
    half = lax.axis_index("gy") % 2
    lane_of_half = iota((SOLID, DEPTH), 1) - half
    packed = edge_ref[...]
    for c in (0, 2):
        before, after = received(a_ref, b_ref, pl.ds(SOLID * c, SOLID))
        for value, x in ((before, -1), (after, XS)):
            at = slot(c, x)
            packed = jnp.where(lane_of_half == at, turned(value, at + 1, 1), packed)
    out_ref[...] = packed


def assemble_kernel(
    d_ref, un_ref, up_ref, s_ref, b_ref, pn_ref, pp_ref, c_ref, ya_ref, yb_ref, wi_ref, wo_ref,
    u_out, v_out, s_out, b_out, d_out, p_out, q_out, c_out, edge_out, xa_out, xb_out,
):
    gx, block, half = coordinates()
    even = block % 2 == 0
    sub = iota((8, DEPTH), 0)
    low = sub < 4
    has_before = block > 0
    has_after = block < lax.axis_size("gy") // 2 - 1
    outer = jnp.where(half == 0, has_before, has_after)
    own, beyond = pl.ds(0, 32), pl.ds(32, 8)
    for x in range(XS):
        d = d_ref[x]
        inside = d >= 1.0
        for c in range(3):
            u_out[c, x, own] = jnp.where(inside, un_ref[c, x], 0.0)
            v_out[c, x, own] = jnp.where(inside, up_ref[c, x], 0.0)
        s_out[x, own] = jnp.where(inside, s_ref[x], 0.0)
        b_out[x, own] = jnp.where(inside, b_ref[x], 0.0)
        d_out[x, own] = d
        halo = []
        for k in range(4):
            got_a, got_b = ya_ref[k, x], yb_ref[k, x]
            from_before = jnp.where(has_before, jnp.where(even, got_b, got_a), 0.0)
            from_after = jnp.where(has_after, jnp.where(even, got_a, got_b), 0.0)
            halo.append(jnp.where(low, from_after, from_before))
            halo.append(turned(jnp.where(low, from_before, from_after), 4, 0))
        contact_rows = jnp.zeros((8, DEPTH), F32)
        for c in range(3):
            v = halo[3 + c]
            contact_rows = jnp.where(sub == c, turned(v, c - 3, 0), contact_rows)
            contact_rows = jnp.where(sub == 5 + c, turned(v, 1 + c, 0), contact_rows)
        halo.append(contact_rows)
        for c in range(3):
            u_out[c, x, beyond] = halo[c]
            v_out[c, x, beyond] = halo[3 + c]
        s_out[x, beyond] = halo[6]
        b_out[x, beyond] = halo[7]
        d_out[x, beyond] = halo[8]
        from_partner = low == (half == 0)

        def water_halo(at, natural):
            inner, beyond_it = wi_ref[at], jnp.where(outer, wo_ref[at], 0.0)
            if not natural:
                inner, beyond_it = turned(inner, 4, 0), turned(beyond_it, 4, 0)
            return jnp.where(from_partner, inner, beyond_it)

        for ref, out, at, natural in (
            (pn_ref, p_out, x, True), (pp_ref, q_out, x, False), (c_ref, c_out, XS + x % 8, x < 8)
        ):
            out[x, pl.ds(0, 16)] = ref[x]
            out[x, pl.ds(16, 8)] = water_halo(at, natural)
    edge_out[...] = edge_plane(
        None,
        half,
        lambda c, x: u_out[c, x],
        lambda x: velocity_of(u_out[2, x], v_out[2, x], d_out[x]),
        lambda x: p_out[x],
    )
    send_faces(lambda c, x: u_out[c, x], lambda x: p_out[x], xa_out, xb_out)


def step_kernel(
    last, lags,
    u_ref, v_ref, s_ref, b_ref, d_ref, p_ref, q_ref, c_ref, edge_ref,
    xa_ref, xb_ref, edge_in,
    u_out, p_out, *more,
):
    gx, block, half = coordinates()
    low_half = half == 0
    shape = (SOLID, DEPTH)
    lane = iota(shape, 1)
    at_edge = lane == jnp.where(low_half, DEPTH - 1, 0)
    sub = iota((8, DEPTH), 0)
    partner = edge_in[...]
    both = partner + edge_ref[...]
    ghosts_here = turned_by(partner, 2 * half)

    def ghost(c, x):
        return jnp.where(at_edge, turned(ghosts_here, 126 - slot(c, x), 1), 0.0)

    faces = [received(xa_ref, xb_ref, pl.ds(SOLID * c, SOLID)) for c in range(3)]
    faces.append(received(xa_ref, xb_ref, pl.ds(3 * SOLID, WATER)))

    def solid(c, x):
        if x < 0:
            return faces[c][0]
        if x >= XS:
            return faces[c][1]
        return u_ref[c, x]

    def water(x):
        if x < 0:
            return faces[3][0]
        if x >= XS:
            return faces[3][1]
        return p_ref[x]

    def plane(x):
        uy, uz = solid(1, x), solid(2, x)
        gz = ghost(2, x)
        up, down = after_y(uy), before_y(uy)
        deep, shallow = after_z(uz, gz), before_z(uz, gz)
        return up - down, up + down, deep - shallow, deep + shallow

    behind = plane(-1)
    here = plane(0)
    ghost_x_behind, ghost_x_here = ghost(0, -1), ghost(0, 0)
    for x in range(XS):
        ahead = plane(x + 1)
        ghost_x_ahead = ghost(0, x + 1)
        qy, sy_y, qz, sz_z = here
        now = [solid(c, x) for c in range(3)]
        nxt = [solid(c, x + 1) for c in range(3)]
        prv = [solid(c, x - 1) for c in range(3)]
        qx = nxt[0] - prv[0]
        sum_x = [nxt[c] + prv[c] for c in range(3)]
        dx = (ahead[0] + ahead[2]) - (behind[0] + behind[2])
        wy = qx + qz
        dy = after_y(wy) - before_y(wy)
        gy_here = ghost(1, x)
        wz = qx + qy
        ghost_wz = (ghost_x_ahead - ghost_x_behind) + (after_y(gy_here) - before_y(gy_here))
        dz = after_z(wz, ghost_wz) - before_z(wz, ghost_wz)
        sum_y = [after_y(now[0]) + before_y(now[0]), sy_y, after_y(now[2]) + before_y(now[2])]
        sum_z = [
            after_z(now[0], ghost_x_here) + before_z(now[0], ghost_x_here),
            after_z(now[1], gy_here) + before_z(now[1], gy_here),
            sz_z,
        ]
        own_sums = [sum_x[0], sum_y[1], sum_z[2]]
        mixed = [dx, dy, dz]
        s, b = s_ref[x], b_ref[x]
        d = d_ref[x]
        contact = d == 1.0
        pb = jnp.broadcast_to(both[:, PB_LANE + x : PB_LANE + x + 1], shape)
        vn = jnp.broadcast_to(both[:, VN_LANE + x : VN_LANE + x + 1], shape)
        for c in range(3):
            u = now[c]
            two = u + u
            laplace = (sum_x[c] + sum_y[c] + sum_z[c]) - 6.0 * u
            grad = (own_sums[c] - two) + 0.25 * mixed[c]
            new = (two - v_ref[c, x]) + s * laplace + b * grad
            if c == 2:
                new = new - jnp.where(contact, LOAD * pb, 0.0)
            if last:
                u_out[c, x] = new[0:32]
            else:
                u_out[c, x] = new
        beyond = jnp.where(
            sub < 4,
            jnp.where(low_half, vn[16:24], vn[32:40]),
            jnp.where(low_half, vn[32:40], vn[8:16]),
        )
        vn_water = jnp.concatenate([jnp.where(low_half, vn[0:16], vn[16:32]), beyond], axis=0)
        p = water(x)
        lateral = water(x + 1) + water(x - 1) + after_y(p) + before_y(p)
        vertical = after_z(p, p - vn_water) + before_z(p, 0.0)
        p_new = (2.0 * p - q_ref[x]) + c_ref[x] * (lateral + vertical - 6.0 * p)
        if last:
            p_out[x] = p_new[0:16]
        else:
            p_out[x] = p_new
        behind, here = here, ahead
        ghost_x_behind, ghost_x_here = ghost_x_here, ghost_x_ahead
    if lags:
        lag_a, lag_b = more[-2:]
        even = gx % 2 == 0
        for n, ref in enumerate((u_ref, u_out)[2 - lags :]):
            for k in range(LAG):
                head = ref[2, k, pl.ds(0, 32)]
                tail = ref[2, k + XS - LAG, pl.ds(0, 32)]
                lag_a[n, k] = jnp.where(even, tail, head)
                lag_b[n, k] = jnp.where(even, head, tail)
    if not last:
        edge_out, xa_out, xb_out = more[:3]
        edge_out[...] = edge_plane(
            None,
            half,
            lambda c, x: u_out[c, x],
            lambda x: velocity_of(u_out[2, x], u_ref[2, x], d_ref[x]),
            lambda x: p_out[x],
        )
        send_faces(lambda c, x: u_out[c, x], lambda x: p_out[x], xa_out, xb_out)


def turned_by(value, amount):
    return jnp.where(amount > 0, turned(value, 2, 1), value)


def image_kernel(chunk, *refs):
    u_refs, lag_refs = refs[0:4], refs[4:10]
    recv_ref, out_ref, reach = refs[10], refs[11], refs[12]
    step = pl.program_id(0)

    @pl.when(step == 0)
    def _():
        gx = lax.axis_index("gx")
        even = gx % 2 == 0
        has_before = gx > 0
        has_after = gx < lax.axis_size("gx") - 1
        t = 0
        for at in range(3):
            a_ref, b_ref = lag_refs[2 * at], lag_refs[2 * at + 1]
            for n in range(a_ref.shape[0]):
                for k in range(LAG):
                    a, b = a_ref[n, k], b_ref[n, k]
                    reach[t, k] = jnp.where(has_before, jnp.where(even, b, a), 0.0)
                    reach[t, LAG + XS + k] = jnp.where(has_after, jnp.where(even, a, b), 0.0)
                t += 1
        for t in range(STEPS):
            for x in range(XS):
                reach[t, LAG + x] = u_refs[t][2, x, pl.ds(0, 32)]

    for k in range(chunk):
        for row in (0, 16):
            rows = pl.ds(row, 16)
            weights = [recv_ref[t, k, rows].astype(F32) for t in range(STEPS)]
            for lag in range(2 * LAG + 1):
                at = step * chunk + (k + lag)
                total = reach[0, at, rows] * weights[0]
                for t in range(1, STEPS):
                    total = total + reach[t, at, rows] * weights[t]
                out_ref[lag, k, rows] = total.astype(jnp.bfloat16)


def call(body, outs, *args, specs=None, scratch=()):
    return pl.pallas_call(
        body,
        out_shape=[jax.ShapeDtypeStruct(shape, F32) for shape in outs],
        in_specs=specs or [VMEM] * len(args),
        out_specs=[VMEM] * len(outs),
        scratch_shapes=list(scratch),
        compiler_params=PARAMS,
    )(*args)


def swapped(size, width):
    return [(i, i ^ width) for i in range(size)]


def crossed(size, width):
    return [(i, (((i + width) % size ^ width) - width) % size) for i in range(size)]


def on_device(p_now, p_prev, water_coef, seafloor, u_now, u_prev, shear, bulk, recv_field):
    size_x = lax.axis_size("gx")
    size_y = lax.axis_size("gy")
    half = lax.axis_index("gy") % 2
    far = jnp.where(half == 0, 4 * DEPTH, -4 * DEPTH)
    levels = jnp.where(seafloor >= 0, seafloor, far)[:, :, None]
    depth = jnp.arange(1, DEPTH + 1, dtype=jnp.int32)[None, None, :]
    field = (depth - levels).astype(F32)
    raw = (field, u_now, u_prev, shear, bulk, p_now, p_prev, water_coef)
    tile = (XS, 8, DEPTH)
    y_payload = (4,) + tile
    w_payload = (XS + XS // 2, 8, DEPTH)
    hbm = pl.BlockSpec(memory_space=pltpu.HBM)
    ya, yb, w_in, w_out = call(
        pack_kernel,
        [y_payload, y_payload, w_payload, w_payload],
        *raw,
        specs=[VMEM] + [hbm] * 7,
        scratch=[pltpu.VMEM((2, 3) + tile, F32)] * 2
        + [pltpu.VMEM((2,) + tile, F32)] * 5
        + [pltpu.SemaphoreType.DMA((14,))],
    )
    ya = lax.ppermute(ya, "gy", swapped(size_y, 2))
    yb = lax.ppermute(yb, "gy", crossed(size_y, 2))
    w_out = lax.ppermute(w_out, "gy", crossed(size_y, 1))
    w_in = lax.ppermute(w_in, "gy", swapped(size_y, 1))
    solid = (XS, SOLID, DEPTH)
    water = (XS, WATER, DEPTH)
    face = (3 * SOLID + WATER, DEPTH)
    plane = (SOLID, DEPTH)
    u, v, s, b, d, p, q, c, edge, xa, xb = call(
        assemble_kernel,
        [(3,) + solid, (3,) + solid, solid, solid, solid, water, water, water, plane, face, face],
        *raw, ya, yb, w_in, w_out,
    )
    verticals, reaches = [], []
    for t in range(STEPS):
        last = t == STEPS - 1
        lags = (0, 2, 1, 1)[t]
        xa = lax.ppermute(xa, "gx", swapped(size_x, 1))
        xb = lax.ppermute(xb, "gx", crossed(size_x, 1))
        edge_full, = call(corner_kernel, [plane], edge, xa, xb)
        edge_in = lax.ppermute(edge_full, "gy", swapped(size_y, 1))
        if last:
            outs = [(3, XS, 32, DEPTH), (XS, 16, DEPTH)]
        else:
            outs = [(3,) + solid, water, plane, face, face]
        outs = outs + [(lags, LAG, 32, DEPTH)] * (2 if lags else 0)

        def body(*refs, last=last, lags=lags):
            step_kernel(last, lags, *refs)

        u_new, p_new, *more = call(body, outs, u, v, s, b, d, p, q, c, edge, xa, xb, edge_in)
        v, u, q, p = u, u_new, p, p_new
        if not last:
            edge, xa, xb = more[:3]
        if lags:
            reaches.append(lax.ppermute(more[-2], "gx", swapped(size_x, 1)))
            reaches.append(lax.ppermute(more[-1], "gx", crossed(size_x, 1)))
        verticals.append(u)
    chunk = 4

    def image_body(*refs):
        image_kernel(chunk, *refs)

    image = pl.pallas_call(
        image_body,
        out_shape=jax.ShapeDtypeStruct((2 * LAG + 1, XS, 32, DEPTH), jnp.bfloat16),
        grid=(XS // chunk,),
        in_specs=[VMEM] * 10 + [pl.BlockSpec((STEPS, chunk, 32, DEPTH), lambda i: (0, i, 0, 0))],
        out_specs=pl.BlockSpec((2 * LAG + 1, chunk, 32, DEPTH), lambda i: (0, i, 0, 0)),
        scratch_shapes=[pltpu.VMEM((STEPS, XS + 2 * LAG, 32, DEPTH), F32)],
        compiler_params=PARAMS,
    )(*verticals, *reaches, recv_field)
    return (p, u, image)


def solution(mesh):
    return jax.shard_map(
        on_device,
        mesh=mesh,
        in_specs=(
            P("gx", "gy", None),
            P("gx", "gy", None),
            P("gx", "gy", None),
            P("gx", "gy"),
            P(None, "gx", "gy", None),
            P(None, "gx", "gy", None),
            P("gx", "gy", None),
            P("gx", "gy", None),
            P(None, "gx", "gy", None),
        ),
        out_specs=(P("gx", "gy", None), P(None, "gx", "gy", None), P(None, "gx", "gy", None)),
        check_vma=False,
    )
```

profile of v0, /device:TPU:8, one launch (start us, length us, event | category | flops | bytes accessed | tf_op | source)
XLA Modules:
  0.0 96.5 jit_solution(8699499571540004769)
XLA Ops:
  0.6 0.0 copy-start.9
  0.6 0.0 copy-start.7
  0.7 0.8 compare_select_fusion
  1.5 0.1 subtract_convert_fusion.d_ref
  1.6 0.0 copy-start
  1.6 1.1 %copy-done = f32[3,16,32,128]{3,2,1,0:T(8,128)S(1)} copy-done((f32[3,16,32,128]{3,2,1,0:T(8,128)S(1)}, f32[3,16,32,128]{3,2,1,0:T(8,128)}, u32[]{:S(2)}) %copy-start) | copy-done | bytes 786456
  2.7 1.1 %copy-done.1 = f32[3,16,32,128]{3,2,1,0:T(8,128)S(1)} copy-done((f32[3,16,32,128]{3,2,1,0:T(8,128)S(1)}, f32[3,16,32,128]{3,2,1,0:T(8,128)}, u32[]{:S(2)}) %copy-start.1) | copy-done | bytes 786456
  3.9 0.9 copy-done.2
  4.8 0.9 copy-done.3
  5.8 0.9 copy-done.6
  6.7 0.9 copy-done.8
  7.6 0.9 copy-done.10
  8.5 0.5 shard_map.112
  9.0 2.4 %collective-permute-start = (f32[4,16,8,128]{3,2,1,0:T(8,128)S(1)}, f32[4,16,8,128]{3,2,1,0:T(8,128)S(1)}, u32[]{:S(2)}, u32[]{:S(2)}) collective-permute-start(f32[4,16,8,128]{3,2,1,0:T(8,128)S(1)} %get-tuple-element.41), channel_id=1, source_target_pairs={{0,2},{1,3},{2,0},{3,1},{4,6},{5,7},{6,4},{7,5},{8,10},{9,11},{10,... | collective-permute-start | bytes 786440 | tf_op jit(solution)/shard_map/ppermute | solution.py:463
  11.4 7.0 %collective-permute-start.1 = (f32[4,16,8,128]{3,2,1,0:T(8,128)S(1)}, f32[4,16,8,128]{3,2,1,0:T(8,128)S(1)}, u32[]{:S(2)}, u32[]{:S(2)}) collective-permute-start(f32[4,16,8,128]{3,2,1,0:T(8,128)S(1)} %get-tuple-element.42), channel_id=1, source_target_pairs={{0,14},{1,15},{2,4},{3,5},{4,2},{5,3},{6,8},{7,9},{8,6},{9,7},{10,... | collective-permute-start | bytes 786440 | tf_op jit(solution)/shard_map/ppermute | solution.py:464
  18.3 0.4 collective-permute-start.2
  18.8 0.0 collective-permute-start.3
  18.8 4.6 %collective-permute-done.2.wi_ref = f32[24,8,128]{2,1,0:T(8,128)S(1)} collective-permute-done((f32[24,8,128]{2,1,0:T(8,128)S(1)}, f32[24,8,128]{2,1,0:T(8,128)S(1)}, u32[]{:S(2)}, u32[]{:S(2)}) %collective-permute-start.2) | collective-permute-done | bytes 98336 | tf_op jit(solution)/shard_map/ppermute | solution.py:466
  23.4 3.2 %collective-permute-done.3.wo_ref = f32[24,8,128]{2,1,0:T(8,128)S(1)} collective-permute-done((f32[24,8,128]{2,1,0:T(8,128)S(1)}, f32[24,8,128]{2,1,0:T(8,128)S(1)}, u32[]{:S(2)}, u32[]{:S(2)}) %collective-permute-start.3) | collective-permute-done | bytes 98336 | tf_op jit(solution)/shard_map/ppermute | solution.py:465
  26.6 0.0 collective-permute-done.ya_ref
  26.6 2.6 %collective-permute-done.1.yb_ref = f32[4,16,8,128]{3,2,1,0:T(8,128)S(1)} collective-permute-done((f32[4,16,8,128]{3,2,1,0:T(8,128)S(1)}, f32[4,16,8,128]{3,2,1,0:T(8,128)S(1)}, u32[]{:S(2)}, u32[]{:S(2)}) %collective-permute-start.1) | collective-permute-done | bytes 262176 | tf_op jit(solution)/shard_map/ppermute | solution.py:464
  29.3 0.9 shard_map.113
  30.1 0.1 collective-permute-start.4
  30.3 6.7 %collective-permute-start.5 = (f32[144,128]{1,0:T(8,128)S(1)}, f32[144,128]{1,0:T(8,128)S(1)}, u32[]{:S(2)}, u32[]{:S(2)}) collective-permute-start(f32[144,128]{1,0:T(8,128)S(1)} %get-tuple-element.55), channel_id=1, source_target_pairs={{0,240},{16,32},{32,16},{48,64},{64,48},{80,96},{96,80},{112,128},... | collective-permute-start | bytes 221192 | tf_op jit(solution)/shard_map/ppermute | solution.py:481
  37.0 0.0 collective-permute-done.4.a_ref.refs_9_
  37.0 2.5 %collective-permute-done.5.b_ref.refs_10_ = f32[144,128]{1,0:T(8,128)S(1)} collective-permute-done((f32[144,128]{1,0:T(8,128)S(1)}, f32[144,128]{1,0:T(8,128)S(1)}, u32[]{:S(2)}, u32[]{:S(2)}) %collective-permute-start.5) | collective-permute-done | bytes 73760 | tf_op jit(solution)/shard_map/ppermute | solution.py:481
  39.5 0.1 shard_map.114
  39.6 3.0 %collective-permute-start.6 = (f32[40,128]{1,0:T(8,128)S(1)}, f32[40,128]{1,0:T(8,128)S(1)}, u32[]{:S(2)}, u32[]{:S(2)}) collective-permute-start(f32[40,128]{1,0:T(8,128)S(1)} %shard_map.114), channel_id=1, source_target_pairs={{0,1},{1,0},{2,3},{3,2},{4,5},{5,4},{6,7},{7,6},{8,9},{9,8},{10,11... | collective-permute-start | bytes 61448 | tf_op jit(solution)/shard_map/ppermute | solution.py:483
  42.6 1.8 %collective-permute-done.6.refs_11_ = f32[40,128]{1,0:T(8,128)S(1)} collective-permute-done((f32[40,128]{1,0:T(8,128)S(1)}, f32[40,128]{1,0:T(8,128)S(1)}, u32[]{:S(2)}, u32[]{:S(2)}) %collective-permute-start.6) | collective-permute-done | bytes 20512 | tf_op jit(solution)/shard_map/ppermute | solution.py:483
  44.3 2.5 %shard_map.115 = (f32[3,16,40,128]{3,2,1,0:T(8,128)S(1)}, f32[16,24,128]{2,1,0:T(8,128)S(1)}, f32[40,128]{1,0:T(8,128)S(1)}, f32[144,128]{1,0:T(8,128)S(1)}, f32[144,128]{1,0:T(8,128)S(1)}) custom-call(f32[3,16,40,128]{3,2,1,0:T(8,128)S(1)} %get-tuple-element.45.refs_0_.refs_1_, f32[3,16,40,128]{3,2,1,0:T(8,128)S(1)} %get-tuple-element.46.refs_1_, ...), custom_call_target="tpu_custom_call" | custom-call | tf_op jit(solution)/shard_map/pallas_call | solution.py:423
  46.8 0.1 collective-permute-start.7
  46.9 2.6 %collective-permute-start.8 = (f32[144,128]{1,0:T(8,128)S(1)}, f32[144,128]{1,0:T(8,128)S(1)}, u32[]{:S(2)}, u32[]{:S(2)}) collective-permute-start(f32[144,128]{1,0:T(8,128)S(1)} %get-tuple-element.60), channel_id=1, source_target_pairs={{0,240},{16,32},{32,16},{48,64},{64,48},{80,96},{96,80},{112,128},... | collective-permute-start | bytes 221192 | tf_op jit(solution)/shard_map/ppermute | solution.py:481
  49.5 3.4 %collective-permute-done.8.b_ref.refs_10_ = f32[144,128]{1,0:T(8,128)S(1)} collective-permute-done((f32[144,128]{1,0:T(8,128)S(1)}, f32[144,128]{1,0:T(8,128)S(1)}, u32[]{:S(2)}, u32[]{:S(2)}) %collective-permute-start.8) | collective-permute-done | bytes 73760 | tf_op jit(solution)/shard_map/ppermute | solution.py:481
  52.9 0.1 shard_map.116
  53.0 2.1 %collective-permute-start.9 = (f32[40,128]{1,0:T(8,128)S(1)}, f32[40,128]{1,0:T(8,128)S(1)}, u32[]{:S(2)}, u32[]{:S(2)}) collective-permute-start(f32[40,128]{1,0:T(8,128)S(1)} %shard_map.116), channel_id=1, source_target_pairs={{0,1},{1,0},{2,3},{3,2},{4,5},{5,4},{6,7},{7,6},{8,9},{9,8},{10,11... | collective-permute-start | bytes 61448 | tf_op jit(solution)/shard_map/ppermute | solution.py:483
  55.1 1.8 %collective-permute-done.9.refs_11_ = f32[40,128]{1,0:T(8,128)S(1)} collective-permute-done((f32[40,128]{1,0:T(8,128)S(1)}, f32[40,128]{1,0:T(8,128)S(1)}, u32[]{:S(2)}, u32[]{:S(2)}) %collective-permute-start.9) | collective-permute-done | bytes 20512 | tf_op jit(solution)/shard_map/ppermute | solution.py:483
  56.9 2.5 %shard_map.117 = (f32[3,16,40,128]{3,2,1,0:T(8,128)S(1)}, f32[16,24,128]{2,1,0:T(8,128)S(1)}, f32[40,128]{1,0:T(8,128)S(1)}, f32[144,128]{1,0:T(8,128)S(1)}, f32...) custom-call(f32[3,16,40,128]{3,2,1,0:T(8,128)S(1)} %get-tuple-element.56.refs_0_.refs_1_, ...), custom_call_target="tpu_custom_call" | custom-call | tf_op jit(solution)/shard_map/pallas_call | solution.py:423
  59.3 0.1 collective-permute-start.10
  59.4 1.6 %collective-permute-start.11 = (f32[144,128]{1,0:T(8,128)S(1)}, f32[144,128]{1,0:T(8,128)S(1)}, u32[]{:S(2)}, u32[]{:S(2)}) collective-permute-start(f32[144,128]{1,0:T(8,128)S(1)} %get-tuple-element.65), channel_id=1, source_target_pairs={{0,240},{16,32},{32,16},{48,64},{64,48},{80,96},{96,80},{112,128},... | collective-permute-start | bytes 221192 | tf_op jit(solution)/shard_map/ppermute | solution.py:481
  61.0 4.6 %collective-permute-done.11.b_ref.refs_10_ = f32[144,128]{1,0:T(8,128)S(1)} collective-permute-done((f32[144,128]{1,0:T(8,128)S(1)}, f32[144,128]{1,0:T(8,128)S(1)}, u32[]{:S(2)}, u32[]{:S(2)}) %collective-permute-start.11) | collective-permute-done | bytes 73760 | tf_op jit(solution)/shard_map/ppermute | solution.py:481
  65.6 0.1 shard_map.118
  65.7 2.1 %collective-permute-start.12 = (f32[40,128]{1,0:T(8,128)S(1)}, f32[40,128]{1,0:T(8,128)S(1)}, u32[]{:S(2)}, u32[]{:S(2)}) collective-permute-start(f32[40,128]{1,0:T(8,128)S(1)} %shard_map.118), channel_id=1, source_target_pairs={{0,1},{1,0},{2,3},{3,2},{4,5},{5,4},{6,7},{7,6},{8,9},{9,8},{10,11... | collective-permute-start | bytes 61448 | tf_op jit(solution)/shard_map/ppermute | solution.py:483
  67.8 0.0 collective-permute-start.16
  67.8 0.8 collective-permute-start.17
  68.6 1.0 %collective-permute-done.12.refs_11_ = f32[40,128]{1,0:T(8,128)S(1)} collective-permute-done((f32[40,128]{1,0:T(8,128)S(1)}, f32[40,128]{1,0:T(8,128)S(1)}, u32[]{:S(2)}, u32[]{:S(2)}) %collective-permute-start.12) | collective-permute-done | bytes 20512 | tf_op jit(solution)/shard_map/ppermute | solution.py:483
  69.6 2.5 %shard_map.119 = (f32[3,16,40,128]{3,2,1,0:T(8,128)S(1)}, f32[16,24,128]{2,1,0:T(8,128)S(1)}, f32[40,128]{1,0:T(8,128)S(1)}, f32[144,128]{1,0:T(8,128)S(1)}, f32...) custom-call(f32[3,16,40,128]{3,2,1,0:T(8,128)S(1)} %get-tuple-element.61.refs_0_.refs_1_, ...), custom_call_target="tpu_custom_call" | custom-call | tf_op jit(solution)/shard_map/pallas_call | solution.py:423
  72.0 0.0 copy-start.5
  72.1 0.1 collective-permute-start.18
  72.2 0.5 collective-permute-start.13
  72.7 2.1 %collective-permute-start.14 = (f32[144,128]{1,0:T(8,128)S(1)}, f32[144,128]{1,0:T(8,128)S(1)}, u32[]{:S(2)}, u32[]{:S(2)}) collective-permute-start(f32[144,128]{1,0:T(8,128)S(1)} %get-tuple-element.70), channel_id=1, source_target_pairs={{0,240},{16,32},{32,16},{48,64},{64,48},{80,96},{96,80},{112,128},... | collective-permute-start | bytes 221192 | tf_op jit(solution)/shard_map/ppermute | solution.py:481
  74.8 0.0 collective-permute-done.13.a_ref.refs_9_
  74.8 4.3 %collective-permute-done.14.b_ref.refs_10_ = f32[144,128]{1,0:T(8,128)S(1)} collective-permute-done((f32[144,128]{1,0:T(8,128)S(1)}, f32[144,128]{1,0:T(8,128)S(1)}, u32[]{:S(2)}, u32[]{:S(2)}) %collective-permute-start.14) | collective-permute-done | bytes 73760 | tf_op jit(solution)/shard_map/ppermute | solution.py:481
  79.1 0.1 shard_map.120
  79.2 1.6 %collective-permute-start.15 = (f32[40,128]{1,0:T(8,128)S(1)}, f32[40,128]{1,0:T(8,128)S(1)}, u32[]{:S(2)}, u32[]{:S(2)}) collective-permute-start(f32[40,128]{1,0:T(8,128)S(1)} %shard_map.120), channel_id=1, source_target_pairs={{0,1},{1,0},{2,3},{3,2},{4,5},{5,4},{6,7},{7,6},{8,9},{9,8},{10,11... | collective-permute-start | bytes 61448 | tf_op jit(solution)/shard_map/ppermute | solution.py:483
  80.7 0.9 collective-permute-start.19
  81.6 1.5 %collective-permute-done.15.refs_11_ = f32[40,128]{1,0:T(8,128)S(1)} collective-permute-done((f32[40,128]{1,0:T(8,128)S(1)}, f32[40,128]{1,0:T(8,128)S(1)}, u32[]{:S(2)}, u32[]{:S(2)}) %collective-permute-start.15) | collective-permute-done | bytes 20512 | tf_op jit(solution)/shard_map/ppermute | solution.py:483
  83.1 2.3 %shard_map.121 = (f32[3,16,32,128]{3,2,1,0:T(8,128)}, f32[16,16,128]{2,1,0:T(8,128)}, f32[1,10,32,128]{3,2,1,0:T(8,128)S(1)}, f32[1,10,32,128]{3,2,1,0:T(8,128)S(1)}) custom-call(f32[3,16,40,128]{3,2,1,0:T(8,128)S(1)} %get-tuple-element.66.refs_0_.refs_2_, f32[3,16,40,128]{3,2,1,0:T(8,128)S(1)} %get-tuple-element.61.refs_0_.refs_1_, ...), custom_call_target="tpu_custom_call" | custom-call | tf_op jit(solution)/shard_map/pallas_call | solution.py:423
  85.3 1.6 %collective-permute-start.21 = (f32[1,10,32,128]{3,2,1,0:T(8,128)S(1)}, f32[1,10,32,128]{3,2,1,0:T(8,128)S(1)}, u32[]{:S(2)}, u32[]{:S(2)}) collective-permute-start(f32[1,10,32,128]{3,2,1,0:T(8,128)S(1)} %get-tuple-element.78), channel_id=1, source_target_pairs={{0,240},{16,32},{32,16},{48,64},{64,48},{80,96},{96,80},{112,128},... | collective-permute-start | bytes 491528 | tf_op jit(solution)/shard_map/ppermute | solution.py:499
  87.0 0.6 collective-permute-done.19.refs_7_
  87.6 0.0 collective-permute-done.17.refs_5_
  87.6 0.0 collective-permute-done.20.refs_8_
  87.6 4.7 %collective-permute-done.21.refs_9_ = f32[1,10,32,128]{3,2,1,0:T(8,128)S(1)} collective-permute-done((f32[1,10,32,128]{3,2,1,0:T(8,128)S(1)}, f32[1,10,32,128]{3,2,1,0:T(8,128)S(1)}, u32[]{:S(2)}, u32[]{:S(2)}) %collective-permute-start.21) | collective-permute-done | bytes 163872 | tf_op jit(solution)/shard_map/ppermute | solution.py:499
  92.3 1.1 %copy-done.4 = f32[3,16,32,128]{3,2,1,0:T(8,128)S(1)} copy-done((f32[3,16,32,128]{3,2,1,0:T(8,128)S(1)}, f32[3,16,32,128]{3,2,1,0:T(8,128)}, u32[]{:S(2)}) %copy-start.4) | copy-done | bytes 786456
  93.5 3.0 %shard_map.122 = bf16[21,16,32,128]{3,2,1,0:T(8,128)(2,1)} custom-call(f32[3,16,40,128]{3,2,1,0:T(8,128)S(1)} %get-tuple-element.56.refs_0_.refs_1_, f32[3,16,40,128]{3,2,1,0:T(8,128)S(1)} %get-tuple-element.61.refs_0_.refs_1_, f32[3,16,40,128]{3,2,1,0:T(8,128)S(1)} %get-tuple-element.66.refs_0_.refs_2_, f32[3,16,32,128]{3,2,1,0:T(8,128)S(1)} %copy-done.4, ...), custom_call_target="tpu_custom_call" | custom-call | tf_op jit(solution)/shard_map/pallas_call | solution.py:506
  (16 shorter events, 0.0 us)
Async XLA Ops:
  0.6 28.6 %copy-start.9 = (f32[16,16,128]{2,1,0:T(8,128)S(1)}, f32[16,16,128]{2,1,0:T(8,128)}, u32[]{:S(2)}) copy-start(f32[16,16,128]{2,1,0:T(8,128)} %pp_ref.1) | copy-start | bytes 393220
  0.6 28.6 %copy-start.7 = (f32[16,16,128]{2,1,0:T(8,128)S(1)}, f32[16,16,128]{2,1,0:T(8,128)}, u32[]{:S(2)}) copy-start(f32[16,16,128]{2,1,0:T(8,128)} %pn_ref.1) | copy-start | bytes 393220
  1.6 1.1 %copy-start = (f32[3,16,32,128]{3,2,1,0:T(8,128)S(1)}, f32[3,16,32,128]{3,2,1,0:T(8,128)}, u32[]{:S(2)}) copy-start(f32[3,16,32,128]{3,2,1,0:T(8,128)} %un_ref.1) | copy-start | bytes 2359300
  2.7 1.1 %copy-start.1 = (f32[3,16,32,128]{3,2,1,0:T(8,128)S(1)}, f32[3,16,32,128]{3,2,1,0:T(8,128)}, u32[]{:S(2)}) copy-start(f32[3,16,32,128]{3,2,1,0:T(8,128)} %up_ref.1) | copy-start | bytes 2359300
  3.9 0.9 copy-start.2
  4.8 0.9 copy-start.3
  5.8 0.9 copy-start.6
  6.7 0.9 copy-start.8
  7.6 0.9 copy-start.10
  9.0 17.7 %collective-permute-start = (f32[4,16,8,128]{3,2,1,0:T(8,128)S(1)}, f32[4,16,8,128]{3,2,1,0:T(8,128)S(1)}, u32[]{:S(2)}, u32[]{:S(2)}) collective-permute-start(f32[4,16,8,128]{3,2,1,0:T(8,128)S(1)} %get-tuple-element.41), channel_id=1, source_target_pairs={{0,2},{1,3},{2,0},{3,1},{4,6},{5,7},{6,4},{7,5},{8,10},{9,11},{10,... | collective-permute-start | bytes 786440 | tf_op jit(solution)/shard_map/ppermute | solution.py:463
  11.4 17.9 %collective-permute-start.1 = (f32[4,16,8,128]{3,2,1,0:T(8,128)S(1)}, f32[4,16,8,128]{3,2,1,0:T(8,128)S(1)}, u32[]{:S(2)}, u32[]{:S(2)}) collective-permute-start(f32[4,16,8,128]{3,2,1,0:T(8,128)S(1)} %get-tuple-element.42), channel_id=1, source_target_pairs={{0,14},{1,15},{2,4},{3,5},{4,2},{5,3},{6,8},{7,9},{8,6},{9,7},{10,... | collective-permute-start | bytes 786440 | tf_op jit(solution)/shard_map/ppermute | solution.py:464
  18.3 5.1 %collective-permute-start.2 = (f32[24,8,128]{2,1,0:T(8,128)S(1)}, f32[24,8,128]{2,1,0:T(8,128)S(1)}, u32[]{:S(2)}, u32[]{:S(2)}) collective-permute-start(f32[24,8,128]{2,1,0:T(8,128)S(1)} %get-tuple-element.43), channel_id=1, source_target_pairs={{0,1},{1,0},{2,3},{3,2},{4,5},{5,4},{6,7},{7,6},{8,9},{9,8},{10,11... | collective-permute-start | bytes 294920 | tf_op jit(solution)/shard_map/ppermute | solution.py:466
  18.8 7.9 %collective-permute-start.3 = (f32[24,8,128]{2,1,0:T(8,128)S(1)}, f32[24,8,128]{2,1,0:T(8,128)S(1)}, u32[]{:S(2)}, u32[]{:S(2)}) collective-permute-start(f32[24,8,128]{2,1,0:T(8,128)S(1)} %get-tuple-element.44), channel_id=1, source_target_pairs={{0,15},{1,2},{2,1},{3,4},{4,3},{5,6},{6,5},{7,8},{8,7},{9,10},{10,... | collective-permute-start | bytes 294920 | tf_op jit(solution)/shard_map/ppermute | solution.py:465
  30.1 6.8 %collective-permute-start.4 = (f32[144,128]{1,0:T(8,128)S(1)}, f32[144,128]{1,0:T(8,128)S(1)}, u32[]{:S(2)}, u32[]{:S(2)}) collective-permute-start(f32[144,128]{1,0:T(8,128)S(1)} %get-tuple-element.54), channel_id=1, source_target_pairs={{0,16},{16,0},{32,48},{48,32},{64,80},{80,64},{96,112},{112,96},{1... | collective-permute-start | bytes 221192 | tf_op jit(solution)/shard_map/ppermute | solution.py:480
  30.3 9.3 %collective-permute-start.5 = (f32[144,128]{1,0:T(8,128)S(1)}, f32[144,128]{1,0:T(8,128)S(1)}, u32[]{:S(2)}, u32[]{:S(2)}) collective-permute-start(f32[144,128]{1,0:T(8,128)S(1)} %get-tuple-element.55), channel_id=1, source_target_pairs={{0,240},{16,32},{32,16},{48,64},{64,48},{80,96},{96,80},{112,128},... | collective-permute-start | bytes 221192 | tf_op jit(solution)/shard_map/ppermute | solution.py:481
  39.6 4.7 %collective-permute-start.6 = (f32[40,128]{1,0:T(8,128)S(1)}, f32[40,128]{1,0:T(8,128)S(1)}, u32[]{:S(2)}, u32[]{:S(2)}) collective-permute-start(f32[40,128]{1,0:T(8,128)S(1)} %shard_map.114), channel_id=1, source_target_pairs={{0,1},{1,0},{2,3},{3,2},{4,5},{5,4},{6,7},{7,6},{8,9},{9,8},{10,11... | collective-permute-start | bytes 61448 | tf_op jit(solution)/shard_map/ppermute | solution.py:483
  46.8 2.7 %collective-permute-start.7 = (f32[144,128]{1,0:T(8,128)S(1)}, f32[144,128]{1,0:T(8,128)S(1)}, u32[]{:S(2)}, u32[]{:S(2)}) collective-permute-start(f32[144,128]{1,0:T(8,128)S(1)} %get-tuple-element.59), channel_id=1, source_target_pairs={{0,16},{16,0},{32,48},{48,32},{64,80},{80,64},{96,112},{112,96},{1... | collective-permute-start | bytes 221192 | tf_op jit(solution)/shard_map/ppermute | solution.py:480
  46.9 6.0 %collective-permute-start.8 = (f32[144,128]{1,0:T(8,128)S(1)}, f32[144,128]{1,0:T(8,128)S(1)}, u32[]{:S(2)}, u32[]{:S(2)}) collective-permute-start(f32[144,128]{1,0:T(8,128)S(1)} %get-tuple-element.60), channel_id=1, source_target_pairs={{0,240},{16,32},{32,16},{48,64},{64,48},{80,96},{96,80},{112,128},... | collective-permute-start | bytes 221192 | tf_op jit(solution)/shard_map/ppermute | solution.py:481
  53.0 3.9 %collective-permute-start.9 = (f32[40,128]{1,0:T(8,128)S(1)}, f32[40,128]{1,0:T(8,128)S(1)}, u32[]{:S(2)}, u32[]{:S(2)}) collective-permute-start(f32[40,128]{1,0:T(8,128)S(1)} %shard_map.116), channel_id=1, source_target_pairs={{0,1},{1,0},{2,3},{3,2},{4,5},{5,4},{6,7},{7,6},{8,9},{9,8},{10,11... | collective-permute-start | bytes 61448 | tf_op jit(solution)/shard_map/ppermute | solution.py:483
  59.3 1.7 %collective-permute-start.10 = (f32[144,128]{1,0:T(8,128)S(1)}, f32[144,128]{1,0:T(8,128)S(1)}, u32[]{:S(2)}, u32[]{:S(2)}) collective-permute-start(f32[144,128]{1,0:T(8,128)S(1)} %get-tuple-element.64), channel_id=1, source_target_pairs={{0,16},{16,0},{32,48},{48,32},{64,80},{80,64},{96,112},{112,96},{1... | collective-permute-start | bytes 221192 | tf_op jit(solution)/shard_map/ppermute | solution.py:480
  59.4 6.2 %collective-permute-start.11 = (f32[144,128]{1,0:T(8,128)S(1)}, f32[144,128]{1,0:T(8,128)S(1)}, u32[]{:S(2)}, u32[]{:S(2)}) collective-permute-start(f32[144,128]{1,0:T(8,128)S(1)} %get-tuple-element.65), channel_id=1, source_target_pairs={{0,240},{16,32},{32,16},{48,64},{64,48},{80,96},{96,80},{112,128},... | collective-permute-start | bytes 221192 | tf_op jit(solution)/shard_map/ppermute | solution.py:481
  65.7 3.9 %collective-permute-start.12 = (f32[40,128]{1,0:T(8,128)S(1)}, f32[40,128]{1,0:T(8,128)S(1)}, u32[]{:S(2)}, u32[]{:S(2)}) collective-permute-start(f32[40,128]{1,0:T(8,128)S(1)} %shard_map.118), channel_id=1, source_target_pairs={{0,1},{1,0},{2,3},{3,2},{4,5},{5,4},{6,7},{7,6},{8,9},{9,8},{10,11... | collective-permute-start | bytes 61448 | tf_op jit(solution)/shard_map/ppermute | solution.py:483
  67.8 19.8 %collective-permute-start.16 = (f32[2,10,32,128]{3,2,1,0:T(8,128)S(1)}, f32[2,10,32,128]{3,2,1,0:T(8,128)S(1)}, u32[]{:S(2)}, u32[]{:S(2)}) collective-permute-start(f32[2,10,32,128]{3,2,1,0:T(8,128)S(1)} %get-tuple-element.73), channel_id=1, source_target_pairs={{0,16},{16,0},{32,48},{48,32},{64,80},{80,64},{96,112},{112,96},{1... | collective-permute-start | bytes 983048 | tf_op jit(solution)/shard_map/ppermute | solution.py:498
  67.8 19.8 %collective-permute-start.17 = (f32[2,10,32,128]{3,2,1,0:T(8,128)S(1)}, f32[2,10,32,128]{3,2,1,0:T(8,128)S(1)}, u32[]{:S(2)}, u32[]{:S(2)}) collective-permute-start(f32[2,10,32,128]{3,2,1,0:T(8,128)S(1)} %get-tuple-element.74), channel_id=1, source_target_pairs={{0,240},{16,32},{32,16},{48,64},{64,48},{80,96},{96,80},{112,128},... | collective-permute-start | bytes 983048 | tf_op jit(solution)/shard_map/ppermute | solution.py:499
  72.0 20.3 %copy-start.5 = (bf16[4,16,32,128]{3,2,1,0:T(8,128)(2,1)S(1)}, bf16[4,16,32,128]{3,2,1,0:T(8,128)(2,1)}, u32[]{:S(2)}) copy-start(bf16[4,16,32,128]{3,2,1,0:T(8,128)(2,1)} %refs_10_.1) | copy-start | bytes 1572868
  72.1 13.3 %collective-permute-start.18 = (f32[1,10,32,128]{3,2,1,0:T(8,128)S(1)}, f32[1,10,32,128]{3,2,1,0:T(8,128)S(1)}, u32[]{:S(2)}, u32[]{:S(2)}) collective-permute-start(f32[1,10,32,128]{3,2,1,0:T(8,128)S(1)} %get-tuple-element.75), channel_id=1, source_target_pairs={{0,16},{16,0},{32,48},{48,32},{64,80},{80,64},{96,112},{112,96},{1... | collective-permute-start | bytes 491528 | tf_op jit(solution)/shard_map/ppermute | solution.py:498
  72.2 2.6 %collective-permute-start.13 = (f32[144,128]{1,0:T(8,128)S(1)}, f32[144,128]{1,0:T(8,128)S(1)}, u32[]{:S(2)}, u32[]{:S(2)}) collective-permute-start(f32[144,128]{1,0:T(8,128)S(1)} %get-tuple-element.69), channel_id=1, source_target_pairs={{0,16},{16,0},{32,48},{48,32},{64,80},{80,64},{96,112},{112,96},{1... | collective-permute-start | bytes 221192 | tf_op jit(solution)/shard_map/ppermute | solution.py:480
  72.7 6.4 %collective-permute-start.14 = (f32[144,128]{1,0:T(8,128)S(1)}, f32[144,128]{1,0:T(8,128)S(1)}, u32[]{:S(2)}, u32[]{:S(2)}) collective-permute-start(f32[144,128]{1,0:T(8,128)S(1)} %get-tuple-element.70), channel_id=1, source_target_pairs={{0,240},{16,32},{32,16},{48,64},{64,48},{80,96},{96,80},{112,128},... | collective-permute-start | bytes 221192 | tf_op jit(solution)/shard_map/ppermute | solution.py:481
  79.2 3.9 %collective-permute-start.15 = (f32[40,128]{1,0:T(8,128)S(1)}, f32[40,128]{1,0:T(8,128)S(1)}, u32[]{:S(2)}, u32[]{:S(2)}) collective-permute-start(f32[40,128]{1,0:T(8,128)S(1)} %shard_map.120), channel_id=1, source_target_pairs={{0,1},{1,0},{2,3},{3,2},{4,5},{5,4},{6,7},{7,6},{8,9},{9,8},{10,11... | collective-permute-start | bytes 61448 | tf_op jit(solution)/shard_map/ppermute | solution.py:483
  80.7 6.9 %collective-permute-start.19 = (f32[1,10,32,128]{3,2,1,0:T(8,128)S(1)}, f32[1,10,32,128]{3,2,1,0:T(8,128)S(1)}, u32[]{:S(2)}, u32[]{:S(2)}) collective-permute-start(f32[1,10,32,128]{3,2,1,0:T(8,128)S(1)} %get-tuple-element.76), channel_id=1, source_target_pairs={{0,240},{16,32},{32,16},{48,64},{64,48},{80,96},{96,80},{112,128},... | collective-permute-start | bytes 491528 | tf_op jit(solution)/shard_map/ppermute | solution.py:499
  85.3 2.3 %collective-permute-start.20 = (f32[1,10,32,128]{3,2,1,0:T(8,128)S(1)}, f32[1,10,32,128]{3,2,1,0:T(8,128)S(1)}, u32[]{:S(2)}, u32[]{:S(2)}) collective-permute-start(f32[1,10,32,128]{3,2,1,0:T(8,128)S(1)} %get-tuple-element.77), channel_id=1, source_target_pairs={{0,16},{16,0},{32,48},{48,32},{64,80},{80,64},{96,112},{112,96},{1... | collective-permute-start | bytes 491528 | tf_op jit(solution)/shard_map/ppermute | solution.py:498
  85.3 7.0 %collective-permute-start.21 = (f32[1,10,32,128]{3,2,1,0:T(8,128)S(1)}, f32[1,10,32,128]{3,2,1,0:T(8,128)S(1)}, u32[]{:S(2)}, u32[]{:S(2)}) collective-permute-start(f32[1,10,32,128]{3,2,1,0:T(8,128)S(1)} %get-tuple-element.78), channel_id=1, source_target_pairs={{0,240},{16,32},{32,16},{48,64},{64,48},{80,96},{96,80},{112,128},... | collective-permute-start | bytes 491528 | tf_op jit(solution)/shard_map/ppermute | solution.py:499
  92.3 1.1 %copy-start.4 = (f32[3,16,32,128]{3,2,1,0:T(8,128)S(1)}, f32[3,16,32,128]{3,2,1,0:T(8,128)}, u32[]{:S(2)}) copy-start(f32[3,16,32,128]{3,2,1,0:T(8,128)} %get-tuple-element.39.refs_3_) | copy-start | bytes 2359300
where the time goes:
time: 97.6 us; the launch traced here: 96.5 us
  waiting for transfers between devices  36.7 us (38%)
  starting transfers between devices  35.6 us (36%)
  Pallas kernels  14.4 us (15%)
  local copies, waits for them, and re-layouts  8.02 us (8%)
    ppermute x4, waiting for transfers between devices, on_device(): xb = lax.ppermute(xb, 'gx', crossed(size_x, 1))  14.8 us
    ppermute x4, starting transfers between devices, on_device(): xb = lax.ppermute(xb, 'gx', crossed(size_x, 1))  13 us
    pallas_call x10, Pallas kernels, call(): pl.pallas_call(body, out_shape=[jax.ShapeDtypeStruct(shape, F32) for shap...  11.4 us
    ppermute x4, starting transfers between devices, on_device(): edge_in = lax.ppermute(edge_full, 'gy', swapped(size_y, 1))  8.73 us
    unnamed x22, local copies, waits for them, and re-layouts  8.02 us
    ppermute x1, starting transfers between devices, on_device(): yb = lax.ppermute(yb, 'gy', crossed(size_y, 2))  6.97 us
    ppermute x4, waiting for transfers between devices, on_device(): edge_in = lax.ppermute(edge_full, 'gy', swapped(size_y, 1))  5.99 us
    ppermute x3, waiting for transfers between devices, on_device(): reaches.append(lax.ppermute(more[-1], 'gx', crossed(size_x, 1)))  5.37 us
  transfers between devices with their start and end apart: 22, of which 13 were waited for; matrix products, arithmetic and copies ran while one was open for 0% of the time, Pallas kernels for 5%

commit v1 on v0

v1 whole, which is shorter than its diff:
```python
import jax
import jax.numpy as jnp
from jax import lax
from jax.experimental import pallas as pl
from jax.experimental.pallas import tpu as pltpu
from jax.sharding import PartitionSpec as P

LAG = 10
STEPS = 4
LOAD = 0.5
F32 = jnp.float32
XS = 16
SOLID = 40
WATER = 24
DEPTH = 128
FACE = 3 * SOLID + WATER
OWN = 32
INNER = 192
VMEM = pl.BlockSpec(memory_space=pltpu.VMEM)
PACK_LIMIT = 50
PARAMS = pltpu.CompilerParams(vmem_limit_bytes=40 * 1024 * 1024)


def iota(shape, dim):
    return lax.broadcasted_iota(jnp.int32, shape, dim)


def turned(value, shift, axis):
    return pltpu.roll(value, shift % value.shape[axis], axis)


def after_y(value):
    return turned(value, -1, 0)


def before_y(value):
    return turned(value, 1, 0)


def after_z(value, ghost):
    return jnp.where(iota(value.shape, 1) == DEPTH - 1, ghost, turned(value, -1, 1))


def before_z(value, ghost):
    return jnp.where(iota(value.shape, 1) == 0, ghost, turned(value, 1, 1))


def coordinates():
    gx = lax.axis_index("gx")
    gy = lax.axis_index("gy")
    return gx, gy // 2, gy % 2


def coupling(half, vn_of, water_of):
    group = iota((SOLID, DEPTH), 1) // 8
    group_w = iota((WATER, DEPTH), 1) // 8
    sub = iota((8, DEPTH), 0)
    velocity = jnp.zeros((SOLID, DEPTH), F32)
    bottom = jnp.zeros((WATER, DEPTH), F32)
    for x in range(XS):
        velocity = jnp.where(group == x, vn_of(x), velocity)
        bottom = jnp.where(group_w == x, water_of(x)[:, DEPTH - 1 : DEPTH], bottom)
    low = half == 0
    zero = jnp.zeros((8, DEPTH), F32)
    own0, own1, own2 = bottom[0:8], bottom[8:16], bottom[16:24]
    keep = (sub < 4) != low
    spread = jnp.concatenate(
        [
            jnp.where(low, own0, zero),
            jnp.where(low, own1, zero),
            jnp.where(low, zero, own0),
            jnp.where(low, zero, own1),
            jnp.where(keep, own2, zero),
        ],
        axis=0,
    )
    return spread, velocity


def own_strip(half, plane_of):
    lane = iota((OWN, DEPTH), 1)
    group = lane // 8
    strip = jnp.zeros((OWN, DEPTH), F32)
    for x in range(XS):
        strip = jnp.where(group == x, turned(plane_of(x), 8 * x + 4, 1), strip)
    return jnp.where((lane % 8 < 4) == (half == 0), strip, 0.0)


def send_strip_faces(strips, a_ref, b_ref, rows):
    even = lax.axis_index("gx") % 2 == 0
    group = iota((SOLID, DEPTH), 1) // 8
    head = tail = jnp.zeros((SOLID, DEPTH), F32)
    for c in range(3):
        head = jnp.where(group == c, turned(strips[c], 8 * c, 1), head)
        tail = jnp.where(group == c, turned(strips[c], 8 * c + 8, 1), tail)
    a_ref[rows] = jnp.where(even, tail, head)
    b_ref[rows] = jnp.where(even, head, tail)


def strip_step(now, old, s, b, contact, pb, before, after):
    lane = iota((SOLID, DEPTH), 1)

    def next_x(value, face):
        return jnp.where(lane >= DEPTH - 8, turned(face, DEPTH - 8, 1), turned(value, -8, 1))

    def prev_x(value, face):
        return jnp.where(lane < 8, face, turned(value, 8, 1))

    def next_z(value):
        return turned(value, -1, 1)

    def prev_z(value):
        return turned(value, 1, 1)

    def x_weight(u1, u2):
        return (after_y(u1) - before_y(u1)) + (next_z(u2) - prev_z(u2))

    shifts = []
    for c in range(3):
        u = now[c]
        shifts.append((
            (next_x(u, after[c]), prev_x(u, before[c])),
            (after_y(u), before_y(u)),
            (next_z(u), prev_z(u)),
        ))
    q = [shifts[c][c][0] - shifts[c][c][1] for c in range(3)]
    wx, wy, wz = q[1] + q[2], q[0] + q[2], q[0] + q[1]
    mixed = [
        next_x(wx, x_weight(after[1], after[2])) - prev_x(wx, x_weight(before[1], before[2])),
        after_y(wy) - before_y(wy),
        next_z(wz) - prev_z(wz),
    ]
    new = []
    for c in range(3):
        u = now[c]
        two = u + u
        sums = [up + down for up, down in shifts[c]]
        laplace = (sums[0] + sums[1] + sums[2]) - 6.0 * u
        grad = (sums[c] - two) + 0.25 * mixed[c]
        value = (two - old[c]) + s * laplace + b * grad
        if c == 2:
            value = value - jnp.where(contact, LOAD * pb, 0.0)
        new.append(value)
    return new


def velocity_of(now, before, contact_field):
    return jnp.sum(
        jnp.where(contact_field == 1.0, now - before, 0.0), axis=1, keepdims=True
    )


def paired(first, second, swap):
    return jnp.where(swap, first, turned(second, 4, 0))


def pack_kernel(
    d_ref, un_hbm, up_hbm, elastic, pressures,
    un, up, s_v, b_v, ya_ref, yb_ref, wo_ref, partner_ref, sems,
):
    gx, block, half = coordinates()
    even = block % 2 == 0
    upper = half == 0
    copies = []
    for k, (src, dst) in enumerate(
        ((un_hbm, un), (up_hbm, up))
    ):
        copy = pltpu.make_async_copy(src, dst, sems.at[k])
        copy.start()
        copies.append(copy)
    for copy in copies:
        copy.wait()
    pn, pp, c_v = (pressures.at[k] for k in range(3))
    sub = iota((8, DEPTH), 0)
    low = sub < 4
    for x in range(XS):
        inside = d_ref[x] >= 1.0
        for ref in (un, up):
            for c in range(3):
                ref[c, x] = jnp.where(inside, ref[c, x], 0.0)
        s_v[x] = jnp.where(inside, elastic[0, x], 0.0)
        b_v[x] = jnp.where(inside, elastic[1, x], 0.0)
        sides = []
        for side, rows in ((0, pl.ds(0, 8)), (1, pl.ds(24, 8))):
            d = d_ref[x, rows]
            u = [un[c, x, rows] for c in range(3)]
            v = [up[c, x, rows] for c in range(3)]
            spare = 3 if side == 0 else 4
            for c in range(3):
                row = c if side == 0 else 5 + c
                v[c] = jnp.where(sub == spare, turned(d, spare - row, 0), v[c])
            keep = low if side == 0 else jnp.logical_not(low)
            sides.append(
                [paired(u[0], u[1], keep), paired(u[2], v[0], keep),
                 paired(v[1], v[2], keep), paired(s_v[x, rows], b_v[x, rows], keep)]
            )
        for k in range(4):
            head, tail = sides[0][k], sides[1][k]
            ya_ref[k, x] = jnp.where(even, tail, head)
            yb_ref[k, x] = jnp.where(even, head, tail)
    for inner in (True, False):
        keep = low == (upper != inner)

        def pick(ref, at):
            return jnp.where(upper == inner, ref[at, pl.ds(8, 8)], ref[at, pl.ds(0, 8)])

        tiles = [paired(pick(pn, x), pick(pp, x), keep) for x in range(XS)]
        tiles += [paired(pick(c_v, x), pick(c_v, x + 8), keep) for x in range(8)]
        for at, tile in enumerate(tiles):
            if inner:
                partner_ref[pl.ds(8 * at, 8)] = tile
            else:
                wo_ref[at] = tile
    planes = [lambda x, c=c: un[c, x] for c in range(3)]
    planes += [lambda x, c=c: up[c, x] for c in range(3)]
    planes += [lambda x: s_v[x], lambda x: b_v[x], lambda x: d_ref[x]]
    for k, plane_of in enumerate(planes):
        partner_ref[pl.ds(INNER + OWN * k, OWN)] = own_strip(half, plane_of)


def strip_kernel(own_ref, got_ref, full_ref, ya_ref, yb_ref):
    gx, block, half = coordinates()
    even = block % 2 == 0
    low = iota((8, DEPTH), 0) < 4
    full_ref[...] = own_ref[pl.ds(INNER, 9 * OWN)] + got_ref[pl.ds(INNER, 9 * OWN)]
    for pair in range(5):
        first, second = 2 * pair, min(2 * pair + 1, 8)
        sides = []
        for row, keep in ((0, low), (OWN - 8, jnp.logical_not(low))):
            sides.append(
                paired(full_ref[pl.ds(OWN * first + row, 8)], full_ref[pl.ds(OWN * second + row, 8)], keep)
            )
        ya_ref[pl.ds(8 * pair, 8)] = jnp.where(even, sides[1], sides[0])
        yb_ref[pl.ds(8 * pair, 8)] = jnp.where(even, sides[0], sides[1])


def send_faces(solid_of, water_of, a_ref, b_ref):
    even = lax.axis_index("gx") % 2 == 0
    for c in range(3):
        head, tail = solid_of(c, 0), solid_of(c, XS - 1)
        a_ref[pl.ds(SOLID * c, SOLID)] = jnp.where(even, tail, head)
        b_ref[pl.ds(SOLID * c, SOLID)] = jnp.where(even, head, tail)
    head, tail = water_of(0), water_of(XS - 1)
    a_ref[pl.ds(3 * SOLID, WATER)] = jnp.where(even, tail, head)
    b_ref[pl.ds(3 * SOLID, WATER)] = jnp.where(even, head, tail)


def received(a_ref, b_ref, rows):
    gx = lax.axis_index("gx")
    even = gx % 2 == 0
    a, b = a_ref[rows], b_ref[rows]
    before = jnp.where(gx > 0, jnp.where(even, b, a), 0.0)
    after = jnp.where(gx < lax.axis_size("gx") - 1, jnp.where(even, a, b), 0.0)
    return before, after


def assemble_kernel(
    d_ref, un_ref, up_ref, s_ref, b_ref, pressures,
    ya_ref, yb_ref, wo_ref, partner_ref, full_ref, ysa_ref, ysb_ref,
    u_out, v_out, s_out, b_out, d_out, p_out, q_out, c_out, now_out, old_out, static_out, coupling_out, xa_out, xb_out,
):
    gx, block, half = coordinates()
    even = block % 2 == 0
    sub = iota((8, DEPTH), 0)
    low = sub < 4
    has_before = block > 0
    has_after = block < lax.axis_size("gy") // 2 - 1
    outer = jnp.where(half == 0, has_before, has_after)
    own, beyond = pl.ds(0, OWN), pl.ds(OWN, 8)

    def halos(got_a, got_b):
        from_before = jnp.where(has_before, jnp.where(even, got_b, got_a), 0.0)
        from_after = jnp.where(has_after, jnp.where(even, got_a, got_b), 0.0)
        return (
            jnp.where(low, from_after, from_before),
            turned(jnp.where(low, from_before, from_after), 4, 0),
        )

    strip_halos = []
    for pair in range(5):
        rows = pl.ds(8 * pair, 8)
        strip_halos.extend(halos(ysa_ref[rows], ysb_ref[rows]))
    for k in range(9):
        ref = (now_out, old_out, static_out)[k // 3]
        ref[pl.ds(SOLID * (k % 3), OWN)] = full_ref[pl.ds(OWN * k, OWN)]
        ref[pl.ds(SOLID * (k % 3) + OWN, 8)] = strip_halos[k]
    for x in range(XS):
        for c in range(3):
            u_out[c, x, own] = un_ref[c, x]
            v_out[c, x, own] = up_ref[c, x]
        s_out[x, own] = s_ref[x]
        b_out[x, own] = b_ref[x]
        d_out[x, own] = d_ref[x]
        halo = []
        for k in range(4):
            halo.extend(halos(ya_ref[k, x], yb_ref[k, x]))
        contact_rows = jnp.zeros((8, DEPTH), F32)
        for c in range(3):
            v = halo[3 + c]
            contact_rows = jnp.where(sub == c, turned(v, c - 3, 0), contact_rows)
            contact_rows = jnp.where(sub == 5 + c, turned(v, 1 + c, 0), contact_rows)
        halo.append(contact_rows)
        for c in range(3):
            u_out[c, x, beyond] = halo[c]
            v_out[c, x, beyond] = halo[3 + c]
        s_out[x, beyond] = halo[6]
        b_out[x, beyond] = halo[7]
        d_out[x, beyond] = halo[8]
        pn_ref, pp_ref, c_ref = (pressures.at[k] for k in range(3))
        from_partner = low == (half == 0)

        def water_halo(at, natural):
            inner, beyond_it = partner_ref[pl.ds(8 * at, 8)], jnp.where(outer, wo_ref[at], 0.0)
            if not natural:
                inner, beyond_it = turned(inner, 4, 0), turned(beyond_it, 4, 0)
            return jnp.where(from_partner, inner, beyond_it)

        for ref, out, at, natural in (
            (pn_ref, p_out, x, True), (pp_ref, q_out, x, False), (c_ref, c_out, XS + x % 8, x < 8)
        ):
            out[x, pl.ds(0, 16)] = ref[x]
            out[x, pl.ds(16, 8)] = water_halo(at, natural)
    bottom, velocity = coupling(
        half,
        lambda x: velocity_of(u_out[2, x], v_out[2, x], d_out[x]),
        lambda x: p_out[x],
    )
    coupling_out[pl.ds(0, SOLID)] = bottom
    coupling_out[pl.ds(SOLID, SOLID)] = velocity
    strips = [now_out[pl.ds(SOLID * c, SOLID)] for c in range(3)]
    send_strip_faces(strips, xa_out, xb_out, pl.ds(FACE, SOLID))
    send_faces(lambda c, x: u_out[c, x], lambda x: p_out[x], xa_out, xb_out)


def step_kernel(last, lags, *refs):
    u_ref, v_ref, s_ref, b_ref, d_ref, p_ref, q_ref, c_ref = refs[0:8]
    now_ref, old_ref, static_ref, own_ref, got_ref, xa_ref, xb_ref = refs[8:15]
    strip_rows = pl.ds(FACE, SOLID)
    u_out, p_out = refs[15:17]
    more = refs[17:]
    gx, block, half = coordinates()
    low_half = half == 0
    shape = (SOLID, DEPTH)
    lane = iota(shape, 1)
    at_edge = lane == jnp.where(low_half, DEPTH - 1, 0)
    sub = iota((8, DEPTH), 0)
    bottom = own_ref[pl.ds(0, SOLID)] + got_ref[pl.ds(0, SOLID)]
    velocity = own_ref[pl.ds(SOLID, SOLID)] + got_ref[pl.ds(SOLID, SOLID)]
    strips = [now_ref[pl.ds(SOLID * c, SOLID)] for c in range(3)]
    strip_before, strip_after = [], []
    for value, out in zip(received(xa_ref, xb_ref, strip_rows), (strip_before, strip_after)):
        out.extend(turned(value, -8 * c, 1) if c else value for c in range(3))

    def of_half(value):
        return jnp.where(low_half, value, turned(value, 2, 1))

    ghosts = [[of_half(v) for v in group] for group in (strip_before, strips, strip_after)]

    def ghost(c, x):
        if x < 0:
            source, shift = ghosts[0][c], 123
        elif x >= XS:
            source, shift = ghosts[2][c], 123
        else:
            source, shift = ghosts[1][c], 123 - 8 * x
        return jnp.where(at_edge, turned(source, shift, 1), 0.0)

    faces = [received(xa_ref, xb_ref, pl.ds(SOLID * c, SOLID)) for c in range(3)]
    faces.append(received(xa_ref, xb_ref, pl.ds(3 * SOLID, WATER)))

    def solid(c, x):
        if x < 0:
            return faces[c][0]
        if x >= XS:
            return faces[c][1]
        return u_ref[c, x]

    def water(x):
        if x < 0:
            return faces[3][0]
        if x >= XS:
            return faces[3][1]
        return p_ref[x]

    def plane(x):
        uy, uz = solid(1, x), solid(2, x)
        gz = ghost(2, x)
        up, down = after_y(uy), before_y(uy)
        deep, shallow = after_z(uz, gz), before_z(uz, gz)
        return up - down, up + down, deep - shallow, deep + shallow

    behind = plane(-1)
    here = plane(0)
    ghost_x_behind, ghost_x_here = ghost(0, -1), ghost(0, 0)
    for x in range(XS):
        ahead = plane(x + 1)
        ghost_x_ahead = ghost(0, x + 1)
        qy, sy_y, qz, sz_z = here
        now = [solid(c, x) for c in range(3)]
        nxt = [solid(c, x + 1) for c in range(3)]
        prv = [solid(c, x - 1) for c in range(3)]
        qx = nxt[0] - prv[0]
        sum_x = [nxt[c] + prv[c] for c in range(3)]
        dx = (ahead[0] + ahead[2]) - (behind[0] + behind[2])
        wy = qx + qz
        dy = after_y(wy) - before_y(wy)
        gy_here = ghost(1, x)
        wz = qx + qy
        ghost_wz = (ghost_x_ahead - ghost_x_behind) + (after_y(gy_here) - before_y(gy_here))
        dz = after_z(wz, ghost_wz) - before_z(wz, ghost_wz)
        sum_y = [after_y(now[0]) + before_y(now[0]), sy_y, after_y(now[2]) + before_y(now[2])]
        sum_z = [
            after_z(now[0], ghost_x_here) + before_z(now[0], ghost_x_here),
            after_z(now[1], gy_here) + before_z(now[1], gy_here),
            sz_z,
        ]
        own_sums = [sum_x[0], sum_y[1], sum_z[2]]
        mixed = [dx, dy, dz]
        s, b = s_ref[x], b_ref[x]
        d = d_ref[x]
        contact = d == 1.0
        pb = jnp.broadcast_to(bottom[:, 8 * x : 8 * x + 1], shape)
        vn = jnp.broadcast_to(velocity[:, 8 * x : 8 * x + 1], shape)
        for c in range(3):
            u = now[c]
            two = u + u
            laplace = (sum_x[c] + sum_y[c] + sum_z[c]) - 6.0 * u
            grad = (own_sums[c] - two) + 0.25 * mixed[c]
            new = (two - v_ref[c, x]) + s * laplace + b * grad
            if c == 2:
                new = new - jnp.where(contact, LOAD * pb, 0.0)
            if last:
                u_out[c, x] = new[0:32]
            else:
                u_out[c, x] = new
        beyond = jnp.where(
            sub < 4,
            jnp.where(low_half, vn[16:24], vn[32:40]),
            jnp.where(low_half, vn[32:40], vn[8:16]),
        )
        vn_water = jnp.concatenate([jnp.where(low_half, vn[0:16], vn[16:32]), beyond], axis=0)
        p = water(x)
        lateral = water(x + 1) + water(x - 1) + after_y(p) + before_y(p)
        vertical = after_z(p, p - vn_water) + before_z(p, 0.0)
        p_new = (2.0 * p - q_ref[x]) + c_ref[x] * (lateral + vertical - 6.0 * p)
        if last:
            p_out[x] = p_new[0:16]
        else:
            p_out[x] = p_new
        behind, here = here, ahead
        ghost_x_behind, ghost_x_here = ghost_x_here, ghost_x_ahead
    if lags:
        lag_a, lag_b = more[-2:]
        even = gx % 2 == 0
        for n, ref in enumerate((u_ref, u_out)[2 - lags :]):
            for k in range(LAG):
                head = ref[2, k, pl.ds(0, 32)]
                tail = ref[2, k + XS - LAG, pl.ds(0, 32)]
                lag_a[n, k] = jnp.where(even, tail, head)
                lag_b[n, k] = jnp.where(even, head, tail)
    if last:
        for x in range(XS):
            more[0][x] = u_out[2, x]
        return
    strip_out, coupling_out, xa_out, xb_out = more[:4]
    static = [static_ref[pl.ds(SOLID * k, SOLID)] for k in range(3)]
    old = [old_ref[pl.ds(SOLID * c, SOLID)] for c in range(3)]
    strips = strip_step(
        strips, old, static[0], static[1], static[2] == 1.0, bottom, strip_before, strip_after
    )
    for c in range(3):
        strip_out[pl.ds(SOLID * c, SOLID)] = strips[c]
    send_strip_faces(strips, xa_out, xb_out, pl.ds(FACE, SOLID))
    send_faces(lambda c, x: u_out[c, x], lambda x: p_out[x], xa_out, xb_out)
    bottom, velocity = coupling(
        half,
        lambda x: velocity_of(u_out[2, x], u_ref[2, x], d_ref[x]),
        lambda x: p_out[x],
    )
    coupling_out[pl.ds(0, SOLID)] = bottom
    coupling_out[pl.ds(SOLID, SOLID)] = velocity


def own_range(lag):
    return max(0, LAG - lag), min(XS, XS + LAG - lag)


def open_pairs():
    pairs = []
    for lag in range(2 * LAG + 1):
        low, high = own_range(lag)
        pairs.extend((lag, x) for x in range(XS) if not low <= x < high)
    return {pair: at for at, pair in enumerate(pairs)}


def lag_halos(a, b):
    gx = lax.axis_index("gx")
    even = gx % 2 == 0
    before = jnp.where(gx > 0, jnp.where(even, b, a), 0.0)
    after = jnp.where(gx < lax.axis_size("gx") - 1, jnp.where(even, a, b), 0.0)
    return before, after


def image_kernel(
    u0, u1, u2, u3, first_a, first_b, third_a, third_b, recv_ref,
    out_hbm, open_ref, halo, weights, stage, sems,
):
    for t, (a_ref, b_ref, n) in enumerate(
        ((first_a, first_b, 0), (first_a, first_b, 1), (third_a, third_b, 0))
    ):
        for k in range(LAG):
            halo[t, k], halo[t, LAG + k] = lag_halos(a_ref[n, k], b_ref[n, k])
    for t in range(STEPS):
        for x in range(XS):
            weights[t, x] = recv_ref[t, x].astype(F32)

    def column(t, x):
        if x < 0:
            return halo[t, x + LAG]
        if x >= XS:
            return halo[t, x - XS + LAG]
        if t == STEPS - 1:
            return u3[x]
        return (u0, u1, u2)[t][2, x, pl.ds(0, OWN)]

    pairs = open_pairs()
    copies = []
    for lag in range(2 * LAG + 1):
        low, high = own_range(lag)
        for x in range(XS):
            at = x + lag - LAG
            total = column(0, at) * weights[0, x]
            total = total + column(1, at) * weights[1, x]
            total = total + column(2, at) * weights[2, x]
            if low <= x < high:
                total = total + column(3, at) * weights[3, x]
                stage[lag, x] = total.astype(jnp.bfloat16)
            else:
                open_ref[pairs[lag, x]] = total
        columns = pl.ds(low, high - low)
        copy = pltpu.make_async_copy(
            stage.at[lag, columns], out_hbm.at[lag, columns], sems.at[lag]
        )
        copy.start()
        copies.append(copy)
    for copy in copies:
        copy.wait()


def finish_kernel(open_ref, a_ref, b_ref, recv_ref, image_hbm, out_hbm, halo, stage, sems):
    for k in range(LAG):
        halo[k], halo[LAG + k] = lag_halos(a_ref[0, k], b_ref[0, k])
    pairs = open_pairs()
    copies = []
    for n, lag in enumerate(k for k in range(2 * LAG + 1) if k != LAG):
        low, high = own_range(lag)
        start, stop = (0, low) if lag < LAG else (high, XS)
        for x in range(start, stop):
            at = x + lag if lag < LAG else x + lag - XS
            total = open_ref[pairs[lag, x]] + halo[at] * recv_ref[STEPS - 1, x].astype(F32)
            stage[lag, x] = total.astype(jnp.bfloat16)
        columns = pl.ds(start, stop - start)
        copy = pltpu.make_async_copy(
            stage.at[lag, columns], out_hbm.at[lag, columns], sems.at[n]
        )
        copy.start()
        copies.append(copy)
    for copy in copies:
        copy.wait()


def call(body, outs, *args, specs=None, scratch=(), limit=40):
    return pl.pallas_call(
        body,
        out_shape=[jax.ShapeDtypeStruct(shape, F32) for shape in outs],
        in_specs=specs or [VMEM] * len(args),
        out_specs=[VMEM] * len(outs),
        scratch_shapes=list(scratch),
        compiler_params=pltpu.CompilerParams(vmem_limit_bytes=limit * 1024 * 1024),
    )(*args)


def swapped(size, width):
    return [(i, i ^ width) for i in range(size)]


def crossed(size, width):
    return [(i, (((i + width) % size ^ width) - width) % size) for i in range(size)]


def on_device(p_now, p_prev, water_coef, seafloor, u_now, u_prev, shear, bulk, recv_field):
    size_x = lax.axis_size("gx")
    size_y = lax.axis_size("gy")
    half = lax.axis_index("gy") % 2
    far = jnp.where(half == 0, 4 * DEPTH, -4 * DEPTH)
    levels = jnp.where(seafloor >= 0, seafloor, far)[:, :, None]
    depth = jnp.arange(1, DEPTH + 1, dtype=jnp.int32)[None, None, :]
    field = (depth - levels).astype(F32)
    pressures = jnp.stack([p_now, p_prev, water_coef])
    raw = (field, u_now, u_prev, jnp.stack([shear, bulk]), pressures)
    tile = (XS, 8, DEPTH)
    y_payload = (4,) + tile
    w_payload = (XS + XS // 2, 8, DEPTH)
    hbm = pl.BlockSpec(memory_space=pltpu.HBM)
    *masked, ya, yb, w_out, to_partner = call(
        pack_kernel,
        [u_now.shape, u_now.shape, shear.shape, shear.shape, y_payload, y_payload, w_payload, (INNER + 9 * OWN, DEPTH)],
        *raw,
        specs=[VMEM, hbm, hbm, VMEM, VMEM],
        scratch=[pltpu.SemaphoreType.DMA((2,))],
        limit=PACK_LIMIT,
    )

    def to_y(first, second):
        return (
            lax.ppermute(first, "gy", swapped(size_y, 2)),
            lax.ppermute(second, "gy", crossed(size_y, 2)),
        )

    partner = lax.ppermute(to_partner, "gy", swapped(size_y, 1))
    ya, yb = to_y(ya, yb)
    w_out = lax.ppermute(w_out, "gy", crossed(size_y, 1))
    y_strip = (SOLID, DEPTH)
    full, ysa, ysb = call(strip_kernel, [(9 * OWN, DEPTH), y_strip, y_strip], to_partner, partner)
    ysa, ysb = to_y(ysa, ysb)
    solid = (XS, SOLID, DEPTH)
    water = (XS, WATER, DEPTH)
    face = (FACE + SOLID, DEPTH)
    strip = (3 * SOLID, DEPTH)
    pair = (2 * SOLID, DEPTH)
    u, v, s, b, d, p, q, c, now, old, static, own, xa, xb = call(
        assemble_kernel,
        [(3,) + solid, (3,) + solid, solid, solid, solid, water, water, water,
         strip, strip, strip, pair, face, face],
        field, *masked, pressures, ya, yb, w_out, partner, full, ysa, ysb,
    )

    def to_x(first, second):
        return (
            lax.ppermute(first, "gx", swapped(size_x, 1)),
            lax.ppermute(second, "gx", crossed(size_x, 1)),
        )

    got = lax.ppermute(own, "gy", swapped(size_y, 1))
    faces = to_x(xa, xb)
    verticals, reaches = [], []
    for t in range(STEPS):
        last = t == STEPS - 1
        lags = (0, 2, 1, 1)[t]
        if last:
            outs = [(3, XS, 32, DEPTH), (XS, 16, DEPTH), (XS, 32, DEPTH)]
        else:
            outs = [(3,) + solid, water, strip, pair, face, face]
        outs = outs + [(lags, LAG, 32, DEPTH)] * (2 if lags else 0)

        def body(*refs, last=last, lags=lags):
            step_kernel(last, lags, *refs)

        u_new, p_new, *more = call(
            body, outs, u, v, s, b, d, p, q, c, now, old, static, own, got, *faces
        )
        v, u, q, p = u, u_new, p, p_new
        if last:
            verticals.append(more[0])
        else:
            verticals.append(u)
            old, now, own = now, more[0], more[1]
            faces = to_x(more[2], more[3])
            got = lax.ppermute(own, "gy", swapped(size_y, 1))
        if lags:
            reaches += to_x(more[-2], more[-1])
    lags = 2 * LAG + 1
    image_shape = jax.ShapeDtypeStruct((lags, XS, OWN, DEPTH), jnp.bfloat16)
    open_shape = jax.ShapeDtypeStruct((len(open_pairs()), OWN, DEPTH), F32)
    stage = pltpu.VMEM(image_shape.shape, jnp.bfloat16)
    image, unfinished = pl.pallas_call(
        image_kernel,
        out_shape=[image_shape, open_shape],
        in_specs=[VMEM] * 9,
        out_specs=[hbm, VMEM],
        scratch_shapes=[
            pltpu.VMEM((STEPS - 1, 2 * LAG, OWN, DEPTH), F32),
            pltpu.VMEM((STEPS, XS, OWN, DEPTH), F32),
            stage,
            pltpu.SemaphoreType.DMA((lags,)),
        ],
        compiler_params=PARAMS,
    )(*verticals, *reaches[0:4], recv_field)
    image = pl.pallas_call(
        finish_kernel,
        out_shape=image_shape,
        in_specs=[VMEM] * 4 + [hbm],
        out_specs=hbm,
        scratch_shapes=[
            pltpu.VMEM((2 * LAG, OWN, DEPTH), F32),
            stage,
            pltpu.SemaphoreType.DMA((lags - 1,)),
        ],
        input_output_aliases={4: 0},
        compiler_params=PARAMS,
    )(unfinished, *reaches[4:6], recv_field, image)
    return (p, u, image)


def solution(mesh):
    return jax.shard_map(
        on_device,
        mesh=mesh,
        in_specs=(
            P("gx", "gy", None),
            P("gx", "gy", None),
            P("gx", "gy", None),
            P("gx", "gy"),
            P(None, "gx", "gy", None),
            P(None, "gx", "gy", None),
            P("gx", "gy", None),
            P("gx", "gy", None),
            P(None, "gx", "gy", None),
        ),
        out_specs=(P("gx", "gy", None), P(None, "gx", "gy", None), P(None, "gx", "gy", None)),
        check_vma=False,
    )
```

time: 97.6 us -> 86.2 us (0.88)
  local copies, waits for them, and re-layouts: 8.02 us -> 1.14 us
  waiting for transfers between devices: 36.7 us -> 31.7 us
  other arithmetic: 0.91 us -> 2.96 us
  starting transfers between devices: 35.6 us -> 33.8 us
  Pallas kernels: 14.4 us -> 15.4 us
    unnamed x22 -> x4, local copies, waits for them, and re-layouts: 8.02 us -> 1.14 us
    ppermute x1, waiting for transfers between devices: 3.21 us -> 0.24 us  [on_device(): w_out = lax.ppermute(w_out, 'gy', crossed(size_y, 1))]
    another operation x0 -> x2, other arithmetic: none -> 2.13 us  [the longest x1 1.07 us: on_device(): raw = (field, u_now, u_prev, jnp.stack([shear, bulk]), pressures)]
    ppermute x21 -> x23, waiting for transfers between devices: 33.5 us -> 31.4 us  [the longest x7 12.1 us: to_x(): lax.ppermute(second, 'gx', crossed(size_x, 1))]
    ppermute x21 -> x23, starting transfers between devices: 35.6 us -> 33.8 us  [the longest x2 13.9 us: to_y(): lax.ppermute(second, 'gy', crossed(size_y, 2))]
    pallas_call x10 -> x7, Pallas kernels: 11.4 us -> 11.9 us  [call(): pl.pallas_call(body, out_shape=[jax.ShapeDtypeStruct(shape, F32) for shap...]
    pallas_call x1 -> x2, Pallas kernels: 3.02 us -> 3.49 us  [the longest x1 2.29 us: on_device(): pl.pallas_call(image_kernel, out_shape=[image_shape, open_shape], in_spec...]
  transfers between devices with their start and end apart: 22 -> 24, of which waited for: 13 -> 12; matrix products, arithmetic and copies ran while one was open for 0% -> 0% of each run, Pallas kernels for 5% -> 8%
where the time goes in v1:
time: 86.2 us; the launch traced here: 85.9 us
  starting transfers between devices  33.8 us (39%)
  waiting for transfers between devices  31.7 us (37%)
  Pallas kernels  15.4 us (18%)
  other arithmetic  2.96 us (3%)
  local copies, waits for them, and re-layouts  1.14 us (1%)
  between operations  0.99 us (1%)
    ppermute x2, starting transfers between devices, to_y(): lax.ppermute(second, 'gy', crossed(size_y, 2))  13.9 us
    ppermute x7, waiting for transfers between devices, to_x(): lax.ppermute(second, 'gx', crossed(size_x, 1))  12.1 us
    pallas_call x7, Pallas kernels, call(): pl.pallas_call(body, out_shape=[jax.ShapeDtypeStruct(shape, F32) for shap...  11.9 us
    ppermute x4, waiting for transfers between devices, on_device(): got = lax.ppermute(own, 'gy', swapped(size_y, 1))  11.7 us
    ppermute x7, starting transfers between devices, to_x(): lax.ppermute(second, 'gx', crossed(size_x, 1))  10.7 us
    ppermute x2, waiting for transfers between devices, to_y(): lax.ppermute(second, 'gy', crossed(size_y, 2))  6.1 us
    ppermute x2, starting transfers between devices, to_y(): lax.ppermute(first, 'gy', swapped(size_y, 2))  4.95 us
    pallas_call x1, Pallas kernels, on_device(): pl.pallas_call(image_kernel, out_shape=[image_shape, open_shape], in_spec...  2.29 us
  transfers between devices with their start and end apart: 24, of which 12 were waited for; matrix products, arithmetic and copies ran while one was open for 0% of the time, Pallas kernels for 8%

profile of v1, /device:TPU:8, one launch (start us, length us, event | category | flops | bytes accessed | tf_op | source)
XLA Modules:
  0.0 85.9 jit_solution(14520699986339590144)
XLA Ops:
  0.7 0.7 compare_select_fusion
  1.4 0.1 subtract_convert_fusion.d_ref
  1.5 1.1 %pad_maximum_fusion.elastic = f32[2,16,32,128]{3,2,1,0:T(8,128)S(1)} fusion(f32[1,16,32,128]{3,2,1,0:T(8,128)} %bitcast.5, f32[1,16,32,128]{3,2,1,0:T(8,128)} %bitcast.6), kind=kLoop, calls=%fused_computation | loop fusion | flops 131072 | bytes 1048576 | tf_op jit(solution)/shard_map/stack | solution.py:600
  2.6 1.1 %pad_maximum_fusion.1.pressures = f32[3,16,16,128]{3,2,1,0:T(8,128)S(1)} fusion(f32[1,16,16,128]{3,2,1,0:T(8,128)} %bitcast.7, f32[1,16,16,128]{3,2,1,0:T(8,128)} %bitcast.8, f32[1,16,16,128]{3,2,1,0:T(8,128)} %bitcast.9), kind=kLoop, calls=%fused_computation.1 | loop fusion | flops 196608 | bytes 786432 | tf_op jit(solution)/shard_map/stack | solution.py:599
  3.6 2.9 %shard_map.112 = (f32[3,16,32,128]{3,2,1,0:T(8,128)S(1)}, f32[3,16,32,128]{3,2,1,0:T(8,128)}, f32[16,32,128]{2,1,0:T(8,128)S(1)}, f32[16,32,128]{2,1,0:T(8,128)S...) custom-call(f32[16,32,128]{2,1,0:T(8,128)S(1)} %subtract_convert_fus, ...), custom_call_target="tpu_custom_call" | custom-call | tf_op jit(solution)/shard_map/pallas_call | solution.py:573
  6.6 2.3 %collective-permute-start.3 = (f32[480,128]{1,0:T(8,128)S(1)}, f32[480,128]{1,0:T(8,128)S(1)}, u32[]{:S(2)}, u32[]{:S(2)}) collective-permute-start(f32[480,128]{1,0:T(8,128)S(1)} %get-tuple-element.64.own_ref), channel_id=1, source_target_pairs={{0,1},{1,0},{2,3},{3,2},{4,5},{5,4},{6,7},{7,6},{8,9},{9,8},{10,11... | collective-permute-start | bytes 737288 | tf_op jit(solution)/shard_map/ppermute | solution.py:620
  8.8 0.9 collective-permute-start
  9.7 6.7 %collective-permute-start.1 = (f32[4,16,8,128]{3,2,1,0:T(8,128)S(1)}, f32[4,16,8,128]{3,2,1,0:T(8,128)S(1)}, u32[]{:S(2)}, u32[]{:S(2)}) collective-permute-start(f32[4,16,8,128]{3,2,1,0:T(8,128)S(1)} %get-tuple-element.62), channel_id=1, source_target_pairs={{0,14},{1,15},{2,4},{3,5},{4,2},{5,3},{6,8},{7,9},{8,6},{9,7},{10,... | collective-permute-start | bytes 786440 | tf_op jit(solution)/shard_map/ppermute | solution.py:617
  16.4 0.0 collective-permute-start.2
  16.4 1.4 %collective-permute-done.3.got_ref.partner_ref = f32[480,128]{1,0:T(8,128)S(1)} collective-permute-done((f32[480,128]{1,0:T(8,128)S(1)}, f32[480,128]{1,0:T(8,128)S(1)}, u32[]{:S(2)}, u32[]{:S(2)}) %collective-permute-start.3) | collective-permute-done | bytes 245792 | tf_op jit(solution)/shard_map/ppermute | solution.py:620
  17.8 4.1 %collective-permute-start.4 = (f32[40,128]{1,0:T(8,128)S(1)}, f32[40,128]{1,0:T(8,128)S(1)}, u32[]{:S(2)}, u32[]{:S(2)}) collective-permute-start(f32[40,128]{1,0:T(8,128)S(1)} %get-tuple-element.66), channel_id=1, source_target_pairs={{0,2},{1,3},{2,0},{3,1},{4,6},{5,7},{6,4},{7,5},{8,10},{9,11},{10,... | collective-permute-start | bytes 61448 | tf_op jit(solution)/shard_map/ppermute | solution.py:616
  21.9 7.2 %collective-permute-start.5 = (f32[40,128]{1,0:T(8,128)S(1)}, f32[40,128]{1,0:T(8,128)S(1)}, u32[]{:S(2)}, u32[]{:S(2)}) collective-permute-start(f32[40,128]{1,0:T(8,128)S(1)} %get-tuple-element.67), channel_id=1, source_target_pairs={{0,14},{1,15},{2,4},{3,5},{4,2},{5,3},{6,8},{7,9},{8,6},{9,7},{10,... | collective-permute-start | bytes 61448 | tf_op jit(solution)/shard_map/ppermute | solution.py:617
  29.1 0.2 collective-permute-done.2.wo_ref
  29.4 0.0 collective-permute-done.ya_ref
  29.4 0.0 collective-permute-done.1.yb_ref
  29.4 0.0 collective-permute-done.4.ysa_ref
  29.4 6.1 %collective-permute-done.5.ysb_ref = f32[40,128]{1,0:T(8,128)S(1)} collective-permute-done((f32[40,128]{1,0:T(8,128)S(1)}, f32[40,128]{1,0:T(8,128)S(1)}, u32[]{:S(2)}, u32[]{:S(2)}) %collective-permute-start.5) | collective-permute-done | bytes 20512 | tf_op jit(solution)/shard_map/ppermute | solution.py:617
  35.5 0.0 copy-start.1
  35.5 1.1 %copy-done.1 = f32[3,16,32,128]{3,2,1,0:T(8,128)S(1)} copy-done((f32[3,16,32,128]{3,2,1,0:T(8,128)S(1)}, f32[3,16,32,128]{3,2,1,0:T(8,128)}, u32[]{:S(2)}) %copy-start.1) | copy-done | bytes 786456
  36.6 0.4 shard_map.114
  37.0 0.1 collective-permute-start.7
  37.1 1.1 %collective-permute-start.8 = (f32[184,128]{1,0:T(8,128)S(1)}, f32[184,128]{1,0:T(8,128)S(1)}, u32[]{:S(2)}, u32[]{:S(2)}) collective-permute-start(f32[184,128]{1,0:T(8,128)S(1)} %get-tuple-element.81), channel_id=1, source_target_pairs={{0,240},{16,32},{32,16},{48,64},{64,48},{80,96},{96,80},{112,128},... | collective-permute-start | bytes 282632 | tf_op jit(solution)/shard_map/ppermute | solution.py:641
  38.2 0.8 collective-permute-start.6
  39.0 3.2 %collective-permute-done.6.refs_12_ = f32[80,128]{1,0:T(8,128)S(1)} collective-permute-done((f32[80,128]{1,0:T(8,128)S(1)}, f32[80,128]{1,0:T(8,128)S(1)}, u32[]{:S(2)}, u32[]{:S(2)}) %collective-permute-start.6) | collective-permute-done | bytes 40992 | tf_op jit(solution)/shard_map/ppermute | solution.py:644
  42.2 0.0 collective-permute-done.7.refs_13_
  42.2 1.5 %collective-permute-done.8.refs_14_ = f32[184,128]{1,0:T(8,128)S(1)} collective-permute-done((f32[184,128]{1,0:T(8,128)S(1)}, f32[184,128]{1,0:T(8,128)S(1)}, u32[]{:S(2)}, u32[]{:S(2)}) %collective-permute-start.8) | collective-permute-done | bytes 94240 | tf_op jit(solution)/shard_map/ppermute | solution.py:641
  43.7 2.1 %shard_map.115 = (f32[3,16,40,128]{3,2,1,0:T(8,128)S(1)}, f32[16,24,128]{2,1,0:T(8,128)S(1)}, f32[120,128]{1,0:T(8,128)S(1)}, f32[80,128]{1,0:T(8,128)S(1)}, f32...) custom-call(f32[3,16,40,128]{3,2,1,0:T(8,128)S(1)} %get-tuple-element.68.refs_0_.refs_1_, ...), custom_call_target="tpu_custom_call" | custom-call | tf_op jit(solution)/shard_map/pallas_call | solution.py:573
  45.8 0.1 collective-permute-start.10
  45.9 1.9 %collective-permute-start.11 = (f32[184,128]{1,0:T(8,128)S(1)}, f32[184,128]{1,0:T(8,128)S(1)}, u32[]{:S(2)}, u32[]{:S(2)}) collective-permute-start(f32[184,128]{1,0:T(8,128)S(1)} %get-tuple-element.87), channel_id=1, source_target_pairs={{0,240},{16,32},{32,16},{48,64},{64,48},{80,96},{96,80},{112,128},... | collective-permute-start | bytes 282632 | tf_op jit(solution)/shard_map/ppermute | solution.py:641
  47.7 0.0 collective-permute-start.9
  47.7 4.0 %collective-permute-done.9.refs_12_ = f32[80,128]{1,0:T(8,128)S(1)} collective-permute-done((f32[80,128]{1,0:T(8,128)S(1)}, f32[80,128]{1,0:T(8,128)S(1)}, u32[]{:S(2)}, u32[]{:S(2)}) %collective-permute-start.9) | collective-permute-done | bytes 40992 | tf_op jit(solution)/shard_map/ppermute | solution.py:669
  51.7 0.0 collective-permute-done.10.refs_13_
  51.8 1.3 %collective-permute-done.11.refs_14_ = f32[184,128]{1,0:T(8,128)S(1)} collective-permute-done((f32[184,128]{1,0:T(8,128)S(1)}, f32[184,128]{1,0:T(8,128)S(1)}, u32[]{:S(2)}, u32[]{:S(2)}) %collective-permute-start.11) | collective-permute-done | bytes 94240 | tf_op jit(solution)/shard_map/ppermute | solution.py:641
  53.0 2.1 %shard_map.116 = (f32[3,16,40,128]{3,2,1,0:T(8,128)S(1)}, f32[16,24,128]{2,1,0:T(8,128)S(1)}, f32[120,128]{1,0:T(8,128)S(1)}, f32[80,128]{1,0:T(8,128)S(1)}, f32...) custom-call(f32[3,16,40,128]{3,2,1,0:T(8,128)S(1)} %get-tuple-elemen, ...), custom_call_target="tpu_custom_call" | custom-call | tf_op jit(solution)/shard_map/pallas_call | solution.py:573
  55.1 0.3 collective-permute-start.13
  55.4 0.9 %collective-permute-start.14 = (f32[184,128]{1,0:T(8,128)S(1)}, f32[184,128]{1,0:T(8,128)S(1)}, u32[]{:S(2)}, u32[]{:S(2)}) collective-permute-start(f32[184,128]{1,0:T(8,128)S(1)} %get-tuple-element.93), channel_id=1, source_target_pairs={{0,240},{16,32},{32,16},{48,64},{64,48},{80,96},{96,80},{112,128},... | collective-permute-start | bytes 282632 | tf_op jit(solution)/shard_map/ppermute | solution.py:641
  56.3 0.2 collective-permute-start.12
  56.5 0.0 collective-permute-start.18
  56.5 2.9 %collective-permute-start.19 = (f32[2,10,32,128]{3,2,1,0:T(8,128)S(1)}, f32[2,10,32,128]{3,2,1,0:T(8,128)S(1)}, u32[]{:S(2)}, u32[]{:S(2)}) collective-permute-start(f32[2,10,32,128]{3,2,1,0:T(8,128)S(1)} %get-tuple-element.104), channel_id=1, source_target_pairs={{0,240},{16,32},{32,16},{48,64},{64,48},{80,96},{96,80},{112,128},... | collective-permute-start | bytes 983048 | tf_op jit(solution)/shard_map/ppermute | solution.py:641
  59.4 0.9 %collective-permute-done.12.refs_12_ = f32[80,128]{1,0:T(8,128)S(1)} collective-permute-done((f32[80,128]{1,0:T(8,128)S(1)}, f32[80,128]{1,0:T(8,128)S(1)}, u32[]{:S(2)}, u32[]{:S(2)}) %collective-permute-start.12) | collective-permute-done | bytes 40992 | tf_op jit(solution)/shard_map/ppermute | solution.py:669
  60.3 0.0 collective-permute-done.13.refs_13_
  60.3 1.6 %collective-permute-done.14.refs_14_ = f32[184,128]{1,0:T(8,128)S(1)} collective-permute-done((f32[184,128]{1,0:T(8,128)S(1)}, f32[184,128]{1,0:T(8,128)S(1)}, u32[]{:S(2)}, u32[]{:S(2)}) %collective-permute-start.14) | collective-permute-done | bytes 94240 | tf_op jit(solution)/shard_map/ppermute | solution.py:641
  62.0 2.1 %shard_map.117 = (f32[3,16,40,128]{3,2,1,0:T(8,128)S(1)}, f32[16,24,128]{2,1,0:T(8,128)S(1)}, f32[120,128]{1,0:T(8,128)S(1)}, f32[80,128]{1,0:T(8,128)S(1)}, f32...) custom-call(f32[3,16,40,128]{3,2,1,0:T(8,128)S(1)} %get-tuple-elemen, ...), custom_call_target="tpu_custom_call" | custom-call | tf_op jit(solution)/shard_map/pallas_call | solution.py:573
  64.1 0.0 copy-start
  64.1 0.1 collective-permute-start.20
  64.2 0.1 collective-permute-start.15
  64.3 0.4 collective-permute-start.16
  64.7 3.6 %collective-permute-done.15.refs_12_ = f32[80,128]{1,0:T(8,128)S(1)} collective-permute-done((f32[80,128]{1,0:T(8,128)S(1)}, f32[80,128]{1,0:T(8,128)S(1)}, u32[]{:S(2)}, u32[]{:S(2)}) %collective-permute-start.15) | collective-permute-done | bytes 40992 | tf_op jit(solution)/shard_map/ppermute | solution.py:669
  68.3 0.0 collective-permute-start.17
  68.3 0.0 collective-permute-done.16.refs_13_
  68.3 3.9 %collective-permute-start.21 = (f32[1,10,32,128]{3,2,1,0:T(8,128)S(1)}, f32[1,10,32,128]{3,2,1,0:T(8,128)S(1)}, u32[]{:S(2)}, u32[]{:S(2)}) collective-permute-start(f32[1,10,32,128]{3,2,1,0:T(8,128)S(1)} %get-tuple-element.106), channel_id=1, source_target_pairs={{0,240},{16,32},{32,16},{48,64},{64,48},{80,96},{96,80},{112,128},... | collective-permute-start | bytes 491528 | tf_op jit(solution)/shard_map/ppermute | solution.py:641
  72.2 3.2 %collective-permute-done.17.refs_14_ = f32[184,128]{1,0:T(8,128)S(1)} collective-permute-done((f32[184,128]{1,0:T(8,128)S(1)}, f32[184,128]{1,0:T(8,128)S(1)}, u32[]{:S(2)}, u32[]{:S(2)}) %collective-permute-start.17) | collective-permute-done | bytes 94240 | tf_op jit(solution)/shard_map/ppermute | solution.py:641
  75.4 2.3 %shard_map.118 = (f32[3,16,32,128]{3,2,1,0:T(8,128)}, f32[16,16,128]{2,1,0:T(8,128)}, f32[16,32,128]{2,1,0:T(8,128)S(1)}, f32[1,10,32,128]{3,2,1,0:T(8,128)S(1)}, f32[1,10,32,128]{3,2,1,0:T(8,128)S(1)}) custom-call(f32[3,16,40,128]{3,2,1,0:T(8,128)S(1)} %get-tuple-element.94.refs_0_.u2, f32[3,16,40,128]{3,2,1,0:T(8,128)S(1)} %get-tuple-element.88.refs_0_.refs_1_.u1, ...), custom_call_target="tpu_custom_call" | custom-call | tf_op jit(solution)/shard_map/pallas_call | solution.py:573
  77.6 0.0 collective-permute-start.22
  77.6 0.0 collective-permute-done.20.third_a
  77.6 0.1 collective-permute-start.23
  77.7 0.0 collective-permute-done.21.third_b
  77.7 0.0 collective-permute-done.18.first_a
  77.7 0.0 collective-permute-done.19.first_b
  77.8 0.0 copy-done
  77.8 2.3 %shard_map.119 = (bf16[21,16,32,128]{3,2,1,0:T(8,128)(2,1)}, f32[110,32,128]{2,1,0:T(8,128)S(1)}) custom-call(f32[3,16,40,128]{3,2,1,0:T(8,128)S(1)} %get-tuple-element.82.refs_0_.refs_1_.u0, f32[3,16,40,128]{3,2,1,0:T(8,128)S(1)} %get-tuple-element.88.refs_0_.refs_1_.u1, f32[3,16,40,128]{3,2,1,0:T(8,128)S(1)} %get-tuple-element.94.refs_0_.u2, ...), custom_call_target="tpu_custom_call" | custom-call | tf_op jit(solution)/shard_map/pallas_call | solution.py:676
  80.1 0.0 collective-permute-done.22.a_ref
  80.1 4.5 %collective-permute-done.23.b_ref = f32[1,10,32,128]{3,2,1,0:T(8,128)S(1)} collective-permute-done((f32[1,10,32,128]{3,2,1,0:T(8,128)S(1)}, f32[1,10,32,128]{3,2,1,0:T(8,128)S(1)}, u32[]{:S(2)}, u32[]{:S(2)}) %collective-permute-start.23) | collective-permute-done | bytes 163872 | tf_op jit(solution)/shard_map/ppermute | solution.py:641
  84.6 1.2 %shard_map.120 = bf16[21,16,32,128]{3,2,1,0:T(8,128)(2,1)} custom-call(f32[110,32,128]{2,1,0:T(8,128)S(1)} %get-tuple-element.107.open_ref, f32[1,10,32,128]{3,2,1,0:T(8,128)S(1)} %collective-permute-done.22.a_ref, f32[1,10,32,128]{3,2,1,0:T(8,128)S(1)} %collective-permute-done.23.b_ref, ...), custom_call_target="tpu_custom_call", output_to_operand_aliasing={{}: (4, {})} | custom-call | tf_op jit(solution)/shard_map/pallas_call | solution.py:689
  (2 shorter events, 0.0 us)
Async XLA Ops:
  6.6 11.2 %collective-permute-start.3 = (f32[480,128]{1,0:T(8,128)S(1)}, f32[480,128]{1,0:T(8,128)S(1)}, u32[]{:S(2)}, u32[]{:S(2)}) collective-permute-start(f32[480,128]{1,0:T(8,128)S(1)} %get-tuple-element.64.own_ref), channel_id=1, source_target_pairs={{0,1},{1,0},{2,3},{3,2},{4,5},{5,4},{6,7},{7,6},{8,9},{9,8},{10,11... | collective-permute-start | bytes 737288 | tf_op jit(solution)/shard_map/ppermute | solution.py:620
  8.8 20.5 %collective-permute-start = (f32[4,16,8,128]{3,2,1,0:T(8,128)S(1)}, f32[4,16,8,128]{3,2,1,0:T(8,128)S(1)}, u32[]{:S(2)}, u32[]{:S(2)}) collective-permute-start(f32[4,16,8,128]{3,2,1,0:T(8,128)S(1)} %get-tuple-element.61), channel_id=1, source_target_pairs={{0,2},{1,3},{2,0},{3,1},{4,6},{5,7},{6,4},{7,5},{8,10},{9,11},{10,... | collective-permute-start | bytes 786440 | tf_op jit(solution)/shard_map/ppermute | solution.py:616
  9.7 19.7 %collective-permute-start.1 = (f32[4,16,8,128]{3,2,1,0:T(8,128)S(1)}, f32[4,16,8,128]{3,2,1,0:T(8,128)S(1)}, u32[]{:S(2)}, u32[]{:S(2)}) collective-permute-start(f32[4,16,8,128]{3,2,1,0:T(8,128)S(1)} %get-tuple-element.62), channel_id=1, source_target_pairs={{0,14},{1,15},{2,4},{3,5},{4,2},{5,3},{6,8},{7,9},{8,6},{9,7},{10,... | collective-permute-start | bytes 786440 | tf_op jit(solution)/shard_map/ppermute | solution.py:617
  16.4 13.0 %collective-permute-start.2 = (f32[24,8,128]{2,1,0:T(8,128)S(1)}, f32[24,8,128]{2,1,0:T(8,128)S(1)}, u32[]{:S(2)}, u32[]{:S(2)}) collective-permute-start(f32[24,8,128]{2,1,0:T(8,128)S(1)} %get-tuple-element.63), channel_id=1, source_target_pairs={{0,15},{1,2},{2,1},{3,4},{4,3},{5,6},{6,5},{7,8},{8,7},{9,10},{10,... | collective-permute-start | bytes 294920 | tf_op jit(solution)/shard_map/ppermute | solution.py:622
  17.8 11.5 %collective-permute-start.4 = (f32[40,128]{1,0:T(8,128)S(1)}, f32[40,128]{1,0:T(8,128)S(1)}, u32[]{:S(2)}, u32[]{:S(2)}) collective-permute-start(f32[40,128]{1,0:T(8,128)S(1)} %get-tuple-element.66), channel_id=1, source_target_pairs={{0,2},{1,3},{2,0},{3,1},{4,6},{5,7},{6,4},{7,5},{8,10},{9,11},{10,... | collective-permute-start | bytes 61448 | tf_op jit(solution)/shard_map/ppermute | solution.py:616
  21.9 13.5 %collective-permute-start.5 = (f32[40,128]{1,0:T(8,128)S(1)}, f32[40,128]{1,0:T(8,128)S(1)}, u32[]{:S(2)}, u32[]{:S(2)}) collective-permute-start(f32[40,128]{1,0:T(8,128)S(1)} %get-tuple-element.67), channel_id=1, source_target_pairs={{0,14},{1,15},{2,4},{3,5},{4,2},{5,3},{6,8},{7,9},{8,6},{9,7},{10,... | collective-permute-start | bytes 61448 | tf_op jit(solution)/shard_map/ppermute | solution.py:617
  35.5 1.1 %copy-start.1 = (f32[3,16,32,128]{3,2,1,0:T(8,128)S(1)}, f32[3,16,32,128]{3,2,1,0:T(8,128)}, u32[]{:S(2)}) copy-start(f32[3,16,32,128]{3,2,1,0:T(8,128)} %get-tuple-element.58.up_ref) | copy-start | bytes 2359300
  37.0 5.2 %collective-permute-start.7 = (f32[184,128]{1,0:T(8,128)S(1)}, f32[184,128]{1,0:T(8,128)S(1)}, u32[]{:S(2)}, u32[]{:S(2)}) collective-permute-start(f32[184,128]{1,0:T(8,128)S(1)} %get-tuple-element.80), channel_id=1, source_target_pairs={{0,16},{16,0},{32,48},{48,32},{64,80},{80,64},{96,112},{112,96},{1... | collective-permute-start | bytes 282632 | tf_op jit(solution)/shard_map/ppermute | solution.py:640
  37.1 6.6 %collective-permute-start.8 = (f32[184,128]{1,0:T(8,128)S(1)}, f32[184,128]{1,0:T(8,128)S(1)}, u32[]{:S(2)}, u32[]{:S(2)}) collective-permute-start(f32[184,128]{1,0:T(8,128)S(1)} %get-tuple-element.81), channel_id=1, source_target_pairs={{0,240},{16,32},{32,16},{48,64},{64,48},{80,96},{96,80},{112,128},... | collective-permute-start | bytes 282632 | tf_op jit(solution)/shard_map/ppermute | solution.py:641
  38.2 4.0 %collective-permute-start.6 = (f32[80,128]{1,0:T(8,128)S(1)}, f32[80,128]{1,0:T(8,128)S(1)}, u32[]{:S(2)}, u32[]{:S(2)}) collective-permute-start(f32[80,128]{1,0:T(8,128)S(1)} %get-tuple-element.79.refs_11_), channel_id=1, source_target_pairs={{0,1},{1,0},{2,3},{3,2},{4,5},{5,4},{6,7},{7,6},{8,9},{9,8},{10,11... | collective-permute-start | bytes 122888 | tf_op jit(solution)/shard_map/ppermute | solution.py:644
  45.8 6.0 %collective-permute-start.10 = (f32[184,128]{1,0:T(8,128)S(1)}, f32[184,128]{1,0:T(8,128)S(1)}, u32[]{:S(2)}, u32[]{:S(2)}) collective-permute-start(f32[184,128]{1,0:T(8,128)S(1)} %get-tuple-element.86), channel_id=1, source_target_pairs={{0,16},{16,0},{32,48},{48,32},{64,80},{80,64},{96,112},{112,96},{1... | collective-permute-start | bytes 282632 | tf_op jit(solution)/shard_map/ppermute | solution.py:640
  45.9 7.2 %collective-permute-start.11 = (f32[184,128]{1,0:T(8,128)S(1)}, f32[184,128]{1,0:T(8,128)S(1)}, u32[]{:S(2)}, u32[]{:S(2)}) collective-permute-start(f32[184,128]{1,0:T(8,128)S(1)} %get-tuple-element.87), channel_id=1, source_target_pairs={{0,240},{16,32},{32,16},{48,64},{64,48},{80,96},{96,80},{112,128},... | collective-permute-start | bytes 282632 | tf_op jit(solution)/shard_map/ppermute | solution.py:641
  47.7 4.0 %collective-permute-start.9 = (f32[80,128]{1,0:T(8,128)S(1)}, f32[80,128]{1,0:T(8,128)S(1)}, u32[]{:S(2)}, u32[]{:S(2)}) collective-permute-start(f32[80,128]{1,0:T(8,128)S(1)} %get-tuple-element.85.refs_11_), channel_id=1, source_target_pairs={{0,1},{1,0},{2,3},{3,2},{4,5},{5,4},{6,7},{7,6},{8,9},{9,8},{10,11... | collective-permute-start | bytes 122888 | tf_op jit(solution)/shard_map/ppermute | solution.py:669
  55.1 5.2 %collective-permute-start.13 = (f32[184,128]{1,0:T(8,128)S(1)}, f32[184,128]{1,0:T(8,128)S(1)}, u32[]{:S(2)}, u32[]{:S(2)}) collective-permute-start(f32[184,128]{1,0:T(8,128)S(1)} %get-tuple-element.92), channel_id=1, source_target_pairs={{0,16},{16,0},{32,48},{48,32},{64,80},{80,64},{96,112},{112,96},{1... | collective-permute-start | bytes 282632 | tf_op jit(solution)/shard_map/ppermute | solution.py:640
  55.4 6.5 %collective-permute-start.14 = (f32[184,128]{1,0:T(8,128)S(1)}, f32[184,128]{1,0:T(8,128)S(1)}, u32[]{:S(2)}, u32[]{:S(2)}) collective-permute-start(f32[184,128]{1,0:T(8,128)S(1)} %get-tuple-element.93), channel_id=1, source_target_pairs={{0,240},{16,32},{32,16},{48,64},{64,48},{80,96},{96,80},{112,128},... | collective-permute-start | bytes 282632 | tf_op jit(solution)/shard_map/ppermute | solution.py:641
  56.3 4.0 %collective-permute-start.12 = (f32[80,128]{1,0:T(8,128)S(1)}, f32[80,128]{1,0:T(8,128)S(1)}, u32[]{:S(2)}, u32[]{:S(2)}) collective-permute-start(f32[80,128]{1,0:T(8,128)S(1)} %get-tuple-element.91.refs_11_), channel_id=1, source_target_pairs={{0,1},{1,0},{2,3},{3,2},{4,5},{5,4},{6,7},{7,6},{8,9},{9,8},{10,11... | collective-permute-start | bytes 122888 | tf_op jit(solution)/shard_map/ppermute | solution.py:669
  56.5 21.3 %collective-permute-start.18 = (f32[2,10,32,128]{3,2,1,0:T(8,128)S(1)}, f32[2,10,32,128]{3,2,1,0:T(8,128)S(1)}, u32[]{:S(2)}, u32[]{:S(2)}) collective-permute-start(f32[2,10,32,128]{3,2,1,0:T(8,128)S(1)} %get-tuple-element.103), channel_id=1, source_target_pairs={{0,16},{16,0},{32,48},{48,32},{64,80},{80,64},{96,112},{112,96},{1... | collective-permute-start | bytes 983048 | tf_op jit(solution)/shard_map/ppermute | solution.py:640
  56.5 21.3 %collective-permute-start.19 = (f32[2,10,32,128]{3,2,1,0:T(8,128)S(1)}, f32[2,10,32,128]{3,2,1,0:T(8,128)S(1)}, u32[]{:S(2)}, u32[]{:S(2)}) collective-permute-start(f32[2,10,32,128]{3,2,1,0:T(8,128)S(1)} %get-tuple-element.104), channel_id=1, source_target_pairs={{0,240},{16,32},{32,16},{48,64},{64,48},{80,96},{96,80},{112,128},... | collective-permute-start | bytes 983048 | tf_op jit(solution)/shard_map/ppermute | solution.py:641
  64.1 13.7 %copy-start = (bf16[4,16,32,128]{3,2,1,0:T(8,128)(2,1)S(1)}, bf16[4,16,32,128]{3,2,1,0:T(8,128)(2,1)}, u32[]{:S(2)}) copy-start(bf16[4,16,32,128]{3,2,1,0:T(8,128)(2,1)} %recv_ref.3) | copy-start | bytes 1572868
  64.1 13.5 %collective-permute-start.20 = (f32[1,10,32,128]{3,2,1,0:T(8,128)S(1)}, f32[1,10,32,128]{3,2,1,0:T(8,128)S(1)}, u32[]{:S(2)}, u32[]{:S(2)}) collective-permute-start(f32[1,10,32,128]{3,2,1,0:T(8,128)S(1)} %get-tuple-element.105), channel_id=1, source_target_pairs={{0,16},{16,0},{32,48},{48,32},{64,80},{80,64},{96,112},{112,96},{1... | collective-permute-start | bytes 491528 | tf_op jit(solution)/shard_map/ppermute | solution.py:640
  64.2 4.1 %collective-permute-start.15 = (f32[80,128]{1,0:T(8,128)S(1)}, f32[80,128]{1,0:T(8,128)S(1)}, u32[]{:S(2)}, u32[]{:S(2)}) collective-permute-start(f32[80,128]{1,0:T(8,128)S(1)} %get-tuple-element.97.refs_11_), channel_id=1, source_target_pairs={{0,1},{1,0},{2,3},{3,2},{4,5},{5,4},{6,7},{7,6},{8,9},{9,8},{10,11... | collective-permute-start | bytes 122888 | tf_op jit(solution)/shard_map/ppermute | solution.py:669
  64.3 4.0 %collective-permute-start.16 = (f32[184,128]{1,0:T(8,128)S(1)}, f32[184,128]{1,0:T(8,128)S(1)}, u32[]{:S(2)}, u32[]{:S(2)}) collective-permute-start(f32[184,128]{1,0:T(8,128)S(1)} %get-tuple-element.98), channel_id=1, source_target_pairs={{0,16},{16,0},{32,48},{48,32},{64,80},{80,64},{96,112},{112,96},{1... | collective-permute-start | bytes 282632 | tf_op jit(solution)/shard_map/ppermute | solution.py:640
  68.3 7.1 %collective-permute-start.17 = (f32[184,128]{1,0:T(8,128)S(1)}, f32[184,128]{1,0:T(8,128)S(1)}, u32[]{:S(2)}, u32[]{:S(2)}) collective-permute-start(f32[184,128]{1,0:T(8,128)S(1)} %get-tuple-element.99), channel_id=1, source_target_pairs={{0,240},{16,32},{32,16},{48,64},{64,48},{80,96},{96,80},{112,128},... | collective-permute-start | bytes 282632 | tf_op jit(solution)/shard_map/ppermute | solution.py:641
  68.3 9.4 %collective-permute-start.21 = (f32[1,10,32,128]{3,2,1,0:T(8,128)S(1)}, f32[1,10,32,128]{3,2,1,0:T(8,128)S(1)}, u32[]{:S(2)}, u32[]{:S(2)}) collective-permute-start(f32[1,10,32,128]{3,2,1,0:T(8,128)S(1)} %get-tuple-element.106), channel_id=1, source_target_pairs={{0,240},{16,32},{32,16},{48,64},{64,48},{80,96},{96,80},{112,128},... | collective-permute-start | bytes 491528 | tf_op jit(solution)/shard_map/ppermute | solution.py:641
  77.6 2.4 %collective-permute-start.22 = (f32[1,10,32,128]{3,2,1,0:T(8,128)S(1)}, f32[1,10,32,128]{3,2,1,0:T(8,128)S(1)}, u32[]{:S(2)}, u32[]{:S(2)}) collective-permute-start(f32[1,10,32,128]{3,2,1,0:T(8,128)S(1)} %get-tuple-element.108), channel_id=1, source_target_pairs={{0,16},{16,0},{32,48},{48,32},{64,80},{80,64},{96,112},{112,96},{1... | collective-permute-start | bytes 491528 | tf_op jit(solution)/shard_map/ppermute | solution.py:640
  77.6 6.9 %collective-permute-start.23 = (f32[1,10,32,128]{3,2,1,0:T(8,128)S(1)}, f32[1,10,32,128]{3,2,1,0:T(8,128)S(1)}, u32[]{:S(2)}, u32[]{:S(2)}) collective-permute-start(f32[1,10,32,128]{3,2,1,0:T(8,128)S(1)} %get-tuple-element.109), channel_id=1, source_target_pairs={{0,240},{16,32},{32,16},{48,64},{64,48},{80,96},{96,80},{112,128},... | collective-permute-start | bytes 491528 | tf_op jit(solution)/shard_map/ppermute | solution.py:641

commit v2 on v1

--- a/solution.py
+++ b/solution.py
@@ -17,7 +17,7 @@
 OWN = 32
 INNER = 192
 VMEM = pl.BlockSpec(memory_space=pltpu.VMEM)
-PACK_LIMIT = 50
+PACK_LIMIT = 49.5
 PARAMS = pltpu.CompilerParams(vmem_limit_bytes=40 * 1024 * 1024)
 
 
@@ -168,18 +168,35 @@
         copy = pltpu.make_async_copy(src, dst, sems.at[k])
         copy.start()
         copies.append(copy)
-    for copy in copies:
-        copy.wait()
     pn, pp, c_v = (pressures.at[k] for k in range(3))
     sub = iota((8, DEPTH), 0)
     low = sub < 4
+    for inner in (True, False):
+        keep = low == (upper != inner)
+
+        def pick(ref, at):
+            return jnp.where(upper == inner, ref[at, pl.ds(8, 8)], ref[at, pl.ds(0, 8)])
+
+        tiles = [paired(pick(pn, x), pick(pp, x), keep) for x in range(XS)]
+        tiles += [paired(pick(c_v, x), pick(c_v, x + 8), keep) for x in range(8)]
+        for at, tile in enumerate(tiles):
+            if inner:
+                partner_ref[pl.ds(8 * at, 8)] = tile
+            else:
+                wo_ref[at] = tile
+    for x in range(XS):
+        inside = d_ref[x] >= 1.0
+        s_v[x] = jnp.where(inside, elastic[0, x], 0.0)
+        b_v[x] = jnp.where(inside, elastic[1, x], 0.0)
+    for k, plane_of in enumerate((lambda x: s_v[x], lambda x: b_v[x], lambda x: d_ref[x])):
+        partner_ref[pl.ds(INNER + OWN * (6 + k), OWN)] = own_strip(half, plane_of)
+    for copy in copies:
+        copy.wait()
     for x in range(XS):
         inside = d_ref[x] >= 1.0
         for ref in (un, up):
             for c in range(3):
                 ref[c, x] = jnp.where(inside, ref[c, x], 0.0)
-        s_v[x] = jnp.where(inside, elastic[0, x], 0.0)
-        b_v[x] = jnp.where(inside, elastic[1, x], 0.0)
         sides = []
         for side, rows in ((0, pl.ds(0, 8)), (1, pl.ds(24, 8))):
             d = d_ref[x, rows]
@@ -198,22 +215,8 @@
             head, tail = sides[0][k], sides[1][k]
             ya_ref[k, x] = jnp.where(even, tail, head)
             yb_ref[k, x] = jnp.where(even, head, tail)
-    for inner in (True, False):
-        keep = low == (upper != inner)
-
-        def pick(ref, at):
-            return jnp.where(upper == inner, ref[at, pl.ds(8, 8)], ref[at, pl.ds(0, 8)])
-
-        tiles = [paired(pick(pn, x), pick(pp, x), keep) for x in range(XS)]
-        tiles += [paired(pick(c_v, x), pick(c_v, x + 8), keep) for x in range(8)]
-        for at, tile in enumerate(tiles):
-            if inner:
-                partner_ref[pl.ds(8 * at, 8)] = tile
-            else:
-                wo_ref[at] = tile
     planes = [lambda x, c=c: un[c, x] for c in range(3)]
     planes += [lambda x, c=c: up[c, x] for c in range(3)]
-    planes += [lambda x: s_v[x], lambda x: b_v[x], lambda x: d_ref[x]]
     for k, plane_of in enumerate(planes):
         partner_ref[pl.ds(INNER + OWN * k, OWN)] = own_strip(half, plane_of)
 
@@ -502,14 +505,12 @@
 
 
 def image_kernel(
-    u0, u1, u2, u3, first_a, first_b, third_a, third_b, recv_ref,
+    u0, u1, u2, u3, a_ref, b_ref, recv_ref,
     out_hbm, open_ref, halo, weights, stage, sems,
 ):
-    for t, (a_ref, b_ref, n) in enumerate(
-        ((first_a, first_b, 0), (first_a, first_b, 1), (third_a, third_b, 0))
-    ):
+    for t in range(2):
         for k in range(LAG):
-            halo[t, k], halo[t, LAG + k] = lag_halos(a_ref[n, k], b_ref[n, k])
+            halo[t, k], halo[t, LAG + k] = lag_halos(a_ref[t, k], b_ref[t, k])
     for t in range(STEPS):
         for x in range(XS):
             weights[t, x] = recv_ref[t, x].astype(F32)
@@ -531,8 +532,8 @@
             at = x + lag - LAG
             total = column(0, at) * weights[0, x]
             total = total + column(1, at) * weights[1, x]
-            total = total + column(2, at) * weights[2, x]
             if low <= x < high:
+                total = total + column(2, at) * weights[2, x]
                 total = total + column(3, at) * weights[3, x]
                 stage[lag, x] = total.astype(jnp.bfloat16)
             else:
@@ -548,8 +549,9 @@
 
 
 def finish_kernel(open_ref, a_ref, b_ref, recv_ref, image_hbm, out_hbm, halo, stage, sems):
-    for k in range(LAG):
-        halo[k], halo[LAG + k] = lag_halos(a_ref[0, k], b_ref[0, k])
+    for t in range(2):
+        for k in range(LAG):
+            halo[t, k], halo[t, LAG + k] = lag_halos(a_ref[t, k], b_ref[t, k])
     pairs = open_pairs()
     copies = []
     for n, lag in enumerate(k for k in range(2 * LAG + 1) if k != LAG):
@@ -557,7 +559,8 @@
         start, stop = (0, low) if lag < LAG else (high, XS)
         for x in range(start, stop):
             at = x + lag if lag < LAG else x + lag - XS
-            total = open_ref[pairs[lag, x]] + halo[at] * recv_ref[STEPS - 1, x].astype(F32)
+            total = open_ref[pairs[lag, x]] + halo[0, at] * recv_ref[2, x].astype(F32)
+            total = total + halo[1, at] * recv_ref[3, x].astype(F32)
             stage[lag, x] = total.astype(jnp.bfloat16)
         columns = pl.ds(start, stop - start)
         copy = pltpu.make_async_copy(
@@ -576,7 +579,7 @@
         in_specs=specs or [VMEM] * len(args),
         out_specs=[VMEM] * len(outs),
         scratch_shapes=list(scratch),
-        compiler_params=pltpu.CompilerParams(vmem_limit_bytes=limit * 1024 * 1024),
+        compiler_params=pltpu.CompilerParams(vmem_limit_bytes=int(limit * 1024 * 1024)),
     )(*args)
 
 
@@ -646,7 +649,7 @@
     verticals, reaches = [], []
     for t in range(STEPS):
         last = t == STEPS - 1
-        lags = (0, 2, 1, 1)[t]
+        lags = (0, 2, 0, 2)[t]
         if last:
             outs = [(3, XS, 32, DEPTH), (XS, 16, DEPTH), (XS, 32, DEPTH)]
         else:
@@ -676,29 +679,29 @@
     image, unfinished = pl.pallas_call(
         image_kernel,
         out_shape=[image_shape, open_shape],
-        in_specs=[VMEM] * 9,
+        in_specs=[VMEM] * 7,
         out_specs=[hbm, VMEM],
         scratch_shapes=[
-            pltpu.VMEM((STEPS - 1, 2 * LAG, OWN, DEPTH), F32),
+            pltpu.VMEM((2, 2 * LAG, OWN, DEPTH), F32),
             pltpu.VMEM((STEPS, XS, OWN, DEPTH), F32),
             stage,
             pltpu.SemaphoreType.DMA((lags,)),
         ],
         compiler_params=PARAMS,
-    )(*verticals, *reaches[0:4], recv_field)
+    )(*verticals, *reaches[0:2], recv_field)
     image = pl.pallas_call(
         finish_kernel,
         out_shape=image_shape,
         in_specs=[VMEM] * 4 + [hbm],
         out_specs=hbm,
         scratch_shapes=[
-            pltpu.VMEM((2 * LAG, OWN, DEPTH), F32),
+            pltpu.VMEM((2, 2 * LAG, OWN, DEPTH), F32),
             stage,
             pltpu.SemaphoreType.DMA((lags - 1,)),
         ],
         input_output_aliases={4: 0},
         compiler_params=PARAMS,
-    )(unfinished, *reaches[4:6], recv_field, image)
+    )(unfinished, *reaches[2:4], recv_field, image)
     return (p, u, image)
 
 

time: 86.2 us -> 84.1 us (0.976)
  starting transfers between devices: 33.8 us -> 31.2 us
  waiting for transfers between devices: 31.7 us -> 33.8 us
  local copies, waits for them, and re-layouts: 1.14 us -> 0.01 us
    ppermute x7 -> x6, starting transfers between devices: 10.7 us -> 8.47 us  [to_x(): lax.ppermute(second, 'gx', crossed(size_x, 1))]
    ppermute x7 -> x6, waiting for transfers between devices: 12.1 us -> 14 us  [to_x(): lax.ppermute(second, 'gx', crossed(size_x, 1))]
    unnamed x4 -> x2, local copies, waits for them, and re-layouts: 1.14 us -> 0.01 us
    pallas_call x7, Pallas kernels: 11.9 us -> 10.9 us  [call(): pl.pallas_call(body, out_shape=[jax.ShapeDtypeStruct(shape, F32) for shap...]
  transfers between devices with their start and end apart: 24 -> 22, of which waited for: 12 -> 13; matrix products, arithmetic and copies ran while one was open for 0% -> 0% of each run, Pallas kernels for 8% -> 5%
where the time goes in v2:
time: 84.1 us; the launch traced here: 83.5 us
  waiting for transfers between devices  33.8 us (40%)
  starting transfers between devices  31.2 us (37%)
  Pallas kernels  14.6 us (17%)
  other arithmetic  2.96 us (4%)
  between operations  0.95 us (1%)
    ppermute x6, waiting for transfers between devices, to_x(): lax.ppermute(second, 'gx', crossed(size_x, 1))  14 us
    ppermute x2, starting transfers between devices, to_y(): lax.ppermute(second, 'gy', crossed(size_y, 2))  13.9 us
    ppermute x4, waiting for transfers between devices, on_device(): got = lax.ppermute(own, 'gy', swapped(size_y, 1))  12 us
    pallas_call x7, Pallas kernels, call(): pl.pallas_call(body, out_shape=[jax.ShapeDtypeStruct(shape, F32) for shap...  10.9 us
    ppermute x6, starting transfers between devices, to_x(): lax.ppermute(second, 'gx', crossed(size_x, 1))  8.47 us
    ppermute x2, waiting for transfers between devices, to_y(): lax.ppermute(second, 'gy', crossed(size_y, 2))  6.1 us
    ppermute x2, starting transfers between devices, to_y(): lax.ppermute(first, 'gy', swapped(size_y, 2))  4.95 us
    pallas_call x1, Pallas kernels, on_device(): pl.pallas_call(image_kernel, out_shape=[image_shape, open_shape], in_spec...  2.29 us
  transfers between devices with their start and end apart: 22, of which 13 were waited for; matrix products, arithmetic and copies ran while one was open for 0% of the time, Pallas kernels for 5%

profile of v2, /device:TPU:8, one launch (start us, length us, event | category | flops | bytes accessed | tf_op | source)
XLA Modules:
  0.0 83.5 jit_solution(9866842170227557324)
XLA Ops:
  0.7 0.7 compare_select_fusion
  1.4 0.1 subtract_convert_fusion.d_ref
  1.5 1.1 %pad_maximum_fusion.elastic = f32[2,16,32,128]{3,2,1,0:T(8,128)S(1)} fusion(f32[1,16,32,128]{3,2,1,0:T(8,128)} %bitcast.5, f32[1,16,32,128]{3,2,1,0:T(8,128)} %bitcast.6), kind=kLoop, calls=%fused_computation | loop fusion | flops 131072 | bytes 1048576 | tf_op jit(solution)/shard_map/stack | solution.py:603
  2.6 1.1 %pad_maximum_fusion.1.pressures = f32[3,16,16,128]{3,2,1,0:T(8,128)S(1)} fusion(f32[1,16,16,128]{3,2,1,0:T(8,128)} %bitcast.7, f32[1,16,16,128]{3,2,1,0:T(8,128)} %bitcast.8, f32[1,16,16,128]{3,2,1,0:T(8,128)} %bitcast.9), kind=kLoop, calls=%fused_computation.1 | loop fusion | flops 196608 | bytes 786432 | tf_op jit(solution)/shard_map/stack | solution.py:602
  3.6 2.0 %shard_map.112 = (f32[3,16,32,128]{3,2,1,0:T(8,128)S(1)}, f32[3,16,32,128]{3,2,1,0:T(8,128)S(1)}, f32[16,32,128]{2,1,0:T(8,128)S(1)}, f32[16,32,128]{2,1,0:T(8,1...) custom-call(f32[16,32,128]{2,1,0:T(8,128)S(1)} %subtract_convert_fus, ...), custom_call_target="tpu_custom_call" | custom-call | tf_op jit(solution)/shard_map/pallas_call | solution.py:576
  5.7 2.3 %collective-permute-start.3 = (f32[480,128]{1,0:T(8,128)S(1)}, f32[480,128]{1,0:T(8,128)S(1)}, u32[]{:S(2)}, u32[]{:S(2)}) collective-permute-start(f32[480,128]{1,0:T(8,128)S(1)} %get-tuple-element.62.own_ref), channel_id=1, source_target_pairs={{0,1},{1,0},{2,3},{3,2},{4,5},{5,4},{6,7},{7,6},{8,9},{9,8},{10,11... | collective-permute-start | bytes 737288 | tf_op jit(solution)/shard_map/ppermute | solution.py:623
  7.9 0.9 %collective-permute-start = (f32[4,16,8,128]{3,2,1,0:T(8,128)S(1)}, f32[4,16,8,128]{3,2,1,0:T(8,128)S(1)}, u32[]{:S(2)}, u32[]{:S(2)}) collective-permute-start(f32[4,16,8,128]{3,2,1,0:T(8,128)S(1)} %get-tuple-element.59), channel_id=1, source_target_pairs={{0,2},{1,3},{2,0},{3,1},{4,6},{5,7},{6,4},{7,5},{8,10},{9,11},{10,... | collective-permute-start | bytes 786440 | tf_op jit(solution)/shard_map/ppermute | solution.py:619
  8.8 6.7 %collective-permute-start.1 = (f32[4,16,8,128]{3,2,1,0:T(8,128)S(1)}, f32[4,16,8,128]{3,2,1,0:T(8,128)S(1)}, u32[]{:S(2)}, u32[]{:S(2)}) collective-permute-start(f32[4,16,8,128]{3,2,1,0:T(8,128)S(1)} %get-tuple-element.60), channel_id=1, source_target_pairs={{0,14},{1,15},{2,4},{3,5},{4,2},{5,3},{6,8},{7,9},{8,6},{9,7},{10,... | collective-permute-start | bytes 786440 | tf_op jit(solution)/shard_map/ppermute | solution.py:620
  15.5 0.0 collective-permute-start.2
  15.5 1.4 %collective-permute-done.3.got_ref.partner_ref = f32[480,128]{1,0:T(8,128)S(1)} collective-permute-done((f32[480,128]{1,0:T(8,128)S(1)}, f32[480,128]{1,0:T(8,128)S(1)}, u32[]{:S(2)}, u32[]{:S(2)}) %collective-permute-start.3) | collective-permute-done | bytes 245792 | tf_op jit(solution)/shard_map/ppermute | solution.py:623
  16.9 4.1 %collective-permute-start.4 = (f32[40,128]{1,0:T(8,128)S(1)}, f32[40,128]{1,0:T(8,128)S(1)}, u32[]{:S(2)}, u32[]{:S(2)}) collective-permute-start(f32[40,128]{1,0:T(8,128)S(1)} %get-tuple-element.64), channel_id=1, source_target_pairs={{0,2},{1,3},{2,0},{3,1},{4,6},{5,7},{6,4},{7,5},{8,10},{9,11},{10,... | collective-permute-start | bytes 61448 | tf_op jit(solution)/shard_map/ppermute | solution.py:619
  21.0 7.2 %collective-permute-start.5 = (f32[40,128]{1,0:T(8,128)S(1)}, f32[40,128]{1,0:T(8,128)S(1)}, u32[]{:S(2)}, u32[]{:S(2)}) collective-permute-start(f32[40,128]{1,0:T(8,128)S(1)} %get-tuple-element.65), channel_id=1, source_target_pairs={{0,14},{1,15},{2,4},{3,5},{4,2},{5,3},{6,8},{7,9},{8,6},{9,7},{10,... | collective-permute-start | bytes 61448 | tf_op jit(solution)/shard_map/ppermute | solution.py:620
  28.2 0.2 collective-permute-done.2.wo_ref
  28.4 0.0 collective-permute-done.ya_ref
  28.4 0.0 collective-permute-done.1.yb_ref
  28.5 0.0 collective-permute-done.4.ysa_ref
  28.5 6.1 %collective-permute-done.5.ysb_ref = f32[40,128]{1,0:T(8,128)S(1)} collective-permute-done((f32[40,128]{1,0:T(8,128)S(1)}, f32[40,128]{1,0:T(8,128)S(1)}, u32[]{:S(2)}, u32[]{:S(2)}) %collective-permute-start.5) | collective-permute-done | bytes 20512 | tf_op jit(solution)/shard_map/ppermute | solution.py:620
  34.6 0.4 shard_map.114
  35.0 0.1 collective-permute-start.7
  35.1 1.1 %collective-permute-start.8 = (f32[184,128]{1,0:T(8,128)S(1)}, f32[184,128]{1,0:T(8,128)S(1)}, u32[]{:S(2)}, u32[]{:S(2)}) collective-permute-start(f32[184,128]{1,0:T(8,128)S(1)} %get-tuple-element.79), channel_id=1, source_target_pairs={{0,240},{16,32},{32,16},{48,64},{64,48},{80,96},{96,80},{112,128},... | collective-permute-start | bytes 282632 | tf_op jit(solution)/shard_map/ppermute | solution.py:644
  36.2 0.8 collective-permute-start.6
  37.0 3.2 %collective-permute-done.6.refs_12_ = f32[80,128]{1,0:T(8,128)S(1)} collective-permute-done((f32[80,128]{1,0:T(8,128)S(1)}, f32[80,128]{1,0:T(8,128)S(1)}, u32[]{:S(2)}, u32[]{:S(2)}) %collective-permute-start.6) | collective-permute-done | bytes 40992 | tf_op jit(solution)/shard_map/ppermute | solution.py:647
  40.2 0.0 collective-permute-done.7.refs_13_
  40.2 1.5 %collective-permute-done.8.refs_14_ = f32[184,128]{1,0:T(8,128)S(1)} collective-permute-done((f32[184,128]{1,0:T(8,128)S(1)}, f32[184,128]{1,0:T(8,128)S(1)}, u32[]{:S(2)}, u32[]{:S(2)}) %collective-permute-start.8) | collective-permute-done | bytes 94240 | tf_op jit(solution)/shard_map/ppermute | solution.py:644
  41.7 2.1 %shard_map.115 = (f32[3,16,40,128]{3,2,1,0:T(8,128)S(1)}, f32[16,24,128]{2,1,0:T(8,128)S(1)}, f32[120,128]{1,0:T(8,128)S(1)}, f32[80,128]{1,0:T(8,128)S(1)}, f32...) custom-call(f32[3,16,40,128]{3,2,1,0:T(8,128)S(1)} %get-tuple-element.66.refs_0_.refs_1_, ...), custom_call_target="tpu_custom_call" | custom-call | tf_op jit(solution)/shard_map/pallas_call | solution.py:576
  43.8 0.1 collective-permute-start.10
  43.9 1.9 %collective-permute-start.11 = (f32[184,128]{1,0:T(8,128)S(1)}, f32[184,128]{1,0:T(8,128)S(1)}, u32[]{:S(2)}, u32[]{:S(2)}) collective-permute-start(f32[184,128]{1,0:T(8,128)S(1)} %get-tuple-element.85), channel_id=1, source_target_pairs={{0,240},{16,32},{32,16},{48,64},{64,48},{80,96},{96,80},{112,128},... | collective-permute-start | bytes 282632 | tf_op jit(solution)/shard_map/ppermute | solution.py:644
  45.7 0.0 collective-permute-start.9
  45.7 4.0 %collective-permute-done.9.refs_12_ = f32[80,128]{1,0:T(8,128)S(1)} collective-permute-done((f32[80,128]{1,0:T(8,128)S(1)}, f32[80,128]{1,0:T(8,128)S(1)}, u32[]{:S(2)}, u32[]{:S(2)}) %collective-permute-start.9) | collective-permute-done | bytes 40992 | tf_op jit(solution)/shard_map/ppermute | solution.py:672
  49.7 0.0 collective-permute-done.10.refs_13_
  49.7 1.3 %collective-permute-done.11.refs_14_ = f32[184,128]{1,0:T(8,128)S(1)} collective-permute-done((f32[184,128]{1,0:T(8,128)S(1)}, f32[184,128]{1,0:T(8,128)S(1)}, u32[]{:S(2)}, u32[]{:S(2)}) %collective-permute-start.11) | collective-permute-done | bytes 94240 | tf_op jit(solution)/shard_map/ppermute | solution.py:644
  51.0 2.1 %shard_map.116 = (f32[3,16,40,128]{3,2,1,0:T(8,128)S(1)}, f32[16,24,128]{2,1,0:T(8,128)S(1)}, f32[120,128]{1,0:T(8,128)S(1)}, f32[80,128]{1,0:T(8,128)S(1)}, f32...) custom-call(f32[3,16,40,128]{3,2,1,0:T(8,128)S(1)} %get-tuple-elemen, ...), custom_call_target="tpu_custom_call" | custom-call | tf_op jit(solution)/shard_map/pallas_call | solution.py:576
  53.1 0.3 collective-permute-start.13
  53.4 0.9 %collective-permute-start.14 = (f32[184,128]{1,0:T(8,128)S(1)}, f32[184,128]{1,0:T(8,128)S(1)}, u32[]{:S(2)}, u32[]{:S(2)}) collective-permute-start(f32[184,128]{1,0:T(8,128)S(1)} %get-tuple-element.91), channel_id=1, source_target_pairs={{0,240},{16,32},{32,16},{48,64},{64,48},{80,96},{96,80},{112,128},... | collective-permute-start | bytes 282632 | tf_op jit(solution)/shard_map/ppermute | solution.py:644
  54.3 0.2 collective-permute-start.12
  54.4 3.8 %collective-permute-done.12.refs_12_ = f32[80,128]{1,0:T(8,128)S(1)} collective-permute-done((f32[80,128]{1,0:T(8,128)S(1)}, f32[80,128]{1,0:T(8,128)S(1)}, u32[]{:S(2)}, u32[]{:S(2)}) %collective-permute-start.12) | collective-permute-done | bytes 40992 | tf_op jit(solution)/shard_map/ppermute | solution.py:672
  58.3 0.0 collective-permute-done.13.refs_13_
  58.3 1.3 %collective-permute-done.14.refs_14_ = f32[184,128]{1,0:T(8,128)S(1)} collective-permute-done((f32[184,128]{1,0:T(8,128)S(1)}, f32[184,128]{1,0:T(8,128)S(1)}, u32[]{:S(2)}, u32[]{:S(2)}) %collective-permute-start.14) | collective-permute-done | bytes 94240 | tf_op jit(solution)/shard_map/ppermute | solution.py:644
  59.6 2.1 %shard_map.117 = (f32[3,16,40,128]{3,2,1,0:T(8,128)S(1)}, f32[16,24,128]{2,1,0:T(8,128)S(1)}, f32[120,128]{1,0:T(8,128)S(1)}, f32[80,128]{1,0:T(8,128)S(1)}, f32...) custom-call(f32[3,16,40,128]{3,2,1,0:T(8,128)S(1)} %get-tuple-element.86.refs_0_.refs_1_.u1, ...), custom_call_target="tpu_custom_call" | custom-call | tf_op jit(solution)/shard_map/pallas_call | solution.py:576
  61.7 0.0 copy-start
  61.7 0.1 collective-permute-start.16
  61.8 0.9 %collective-permute-start.17 = (f32[184,128]{1,0:T(8,128)S(1)}, f32[184,128]{1,0:T(8,128)S(1)}, u32[]{:S(2)}, u32[]{:S(2)}) collective-permute-start(f32[184,128]{1,0:T(8,128)S(1)} %get-tuple-element.97), channel_id=1, source_target_pairs={{0,240},{16,32},{32,16},{48,64},{64,48},{80,96},{96,80},{112,128},... | collective-permute-start | bytes 282632 | tf_op jit(solution)/shard_map/ppermute | solution.py:644
  62.7 0.2 collective-permute-start.15
  62.8 0.0 collective-permute-start.18
  62.8 2.9 %collective-permute-start.19 = (f32[2,10,32,128]{3,2,1,0:T(8,128)S(1)}, f32[2,10,32,128]{3,2,1,0:T(8,128)S(1)}, u32[]{:S(2)}, u32[]{:S(2)}) collective-permute-start(f32[2,10,32,128]{3,2,1,0:T(8,128)S(1)} %get-tuple-element.102), channel_id=1, source_target_pairs={{0,240},{16,32},{32,16},{48,64},{64,48},{80,96},{96,80},{112,128},... | collective-permute-start | bytes 983048 | tf_op jit(solution)/shard_map/ppermute | solution.py:644
  65.7 0.9 %collective-permute-done.15.refs_12_ = f32[80,128]{1,0:T(8,128)S(1)} collective-permute-done((f32[80,128]{1,0:T(8,128)S(1)}, f32[80,128]{1,0:T(8,128)S(1)}, u32[]{:S(2)}, u32[]{:S(2)}) %collective-permute-start.15) | collective-permute-done | bytes 40992 | tf_op jit(solution)/shard_map/ppermute | solution.py:672
  66.7 0.0 collective-permute-done.16.refs_13_
  66.7 1.6 %collective-permute-done.17.refs_14_ = f32[184,128]{1,0:T(8,128)S(1)} collective-permute-done((f32[184,128]{1,0:T(8,128)S(1)}, f32[184,128]{1,0:T(8,128)S(1)}, u32[]{:S(2)}, u32[]{:S(2)}) %collective-permute-start.17) | collective-permute-done | bytes 94240 | tf_op jit(solution)/shard_map/ppermute | solution.py:644
  68.3 2.3 %shard_map.118 = (f32[3,16,32,128]{3,2,1,0:T(8,128)}, f32[16,16,128]{2,1,0:T(8,128)}, f32[16,32,128]{2,1,0:T(8,128)S(1)}, f32[2,10,32,128]{3,2,1,0:T(8,128)S(1)}, f32[2,10,32,128]{3,2,1,0:T(8,128)S(1)}) custom-call(f32[3,16,40,128]{3,2,1,0:T(8,128)S(1)} %get-tuple-element.92.refs_0_.u2, f32[3,16,40,128]{3,2,1,0:T(8,128)S(1)} %get-tuple-element.86.refs_0_.refs_1_.u1, ...), custom_call_target="tpu_custom_call" | custom-call | tf_op jit(solution)/shard_map/pallas_call | solution.py:576
  70.6 0.0 collective-permute-start.20
  70.6 0.8 %collective-permute-start.21 = (f32[2,10,32,128]{3,2,1,0:T(8,128)S(1)}, f32[2,10,32,128]{3,2,1,0:T(8,128)S(1)}, u32[]{:S(2)}, u32[]{:S(2)}) collective-permute-start(f32[2,10,32,128]{3,2,1,0:T(8,128)S(1)} %get-tuple-element.105), channel_id=1, source_target_pairs={{0,240},{16,32},{32,16},{48,64},{64,48},{80,96},{96,80},{112,128},... | collective-permute-start | bytes 983048 | tf_op jit(solution)/shard_map/ppermute | solution.py:644
  71.4 0.0 collective-permute-done.18.a_ref
  71.4 3.9 %collective-permute-done.19.b_ref = f32[2,10,32,128]{3,2,1,0:T(8,128)S(1)} collective-permute-done((f32[2,10,32,128]{3,2,1,0:T(8,128)S(1)}, f32[2,10,32,128]{3,2,1,0:T(8,128)S(1)}, u32[]{:S(2)}, u32[]{:S(2)}) %collective-permute-start.19) | collective-permute-done | bytes 327712 | tf_op jit(solution)/shard_map/ppermute | solution.py:644
  75.3 0.0 copy-done
  75.3 2.3 %shard_map.119 = (bf16[21,16,32,128]{3,2,1,0:T(8,128)(2,1)}, f32[110,32,128]{2,1,0:T(8,128)S(1)}) custom-call(f32[3,16,40,128]{3,2,1,0:T(8,128)S(1)} %get-tuple-element.80.refs_0_.refs_1_.u0, f32[3,16,40,128]{3,2,1,0:T(8,128)S(1)} %get-tuple-element.86.refs_0_.refs_1_.u1, f32[3,16,40,128]{3,2,1,0:T(8,128)S(1)} %get-tuple-element.92.refs_0_.u2, ...), custom_call_target="tpu_custom_call" | custom-call | tf_op jit(solution)/shard_map/pallas_call | solution.py:679
  77.6 0.0 collective-permute-done.20.a_ref
  77.6 4.4 %collective-permute-done.21.b_ref = f32[2,10,32,128]{3,2,1,0:T(8,128)S(1)} collective-permute-done((f32[2,10,32,128]{3,2,1,0:T(8,128)S(1)}, f32[2,10,32,128]{3,2,1,0:T(8,128)S(1)}, u32[]{:S(2)}, u32[]{:S(2)}) %collective-permute-start.21) | collective-permute-done | bytes 327712 | tf_op jit(solution)/shard_map/ppermute | solution.py:644
  82.0 1.4 %shard_map.120 = bf16[21,16,32,128]{3,2,1,0:T(8,128)(2,1)} custom-call(f32[110,32,128]{2,1,0:T(8,128)S(1)} %get-tuple-element.103.open_ref, f32[2,10,32,128]{3,2,1,0:T(8,128)S(1)} %collective-permute-done.20.a_ref, f32[2,10,32,128]{3,2,1,0:T(8,128)S(1)} %collective-permute-done.21.b_ref, ...), custom_call_target="tpu_custom_call", output_to_operand_aliasing={{}: (4, {})} | custom-call | tf_op jit(solution)/shard_map/pallas_call | solution.py:692
  (2 shorter events, 0.0 us)
Async XLA Ops:
  5.7 11.2 %collective-permute-start.3 = (f32[480,128]{1,0:T(8,128)S(1)}, f32[480,128]{1,0:T(8,128)S(1)}, u32[]{:S(2)}, u32[]{:S(2)}) collective-permute-start(f32[480,128]{1,0:T(8,128)S(1)} %get-tuple-element.62.own_ref), channel_id=1, source_target_pairs={{0,1},{1,0},{2,3},{3,2},{4,5},{5,4},{6,7},{7,6},{8,9},{9,8},{10,11... | collective-permute-start | bytes 737288 | tf_op jit(solution)/shard_map/ppermute | solution.py:623
  7.9 20.5 %collective-permute-start = (f32[4,16,8,128]{3,2,1,0:T(8,128)S(1)}, f32[4,16,8,128]{3,2,1,0:T(8,128)S(1)}, u32[]{:S(2)}, u32[]{:S(2)}) collective-permute-start(f32[4,16,8,128]{3,2,1,0:T(8,128)S(1)} %get-tuple-element.59), channel_id=1, source_target_pairs={{0,2},{1,3},{2,0},{3,1},{4,6},{5,7},{6,4},{7,5},{8,10},{9,11},{10,... | collective-permute-start | bytes 786440 | tf_op jit(solution)/shard_map/ppermute | solution.py:619
  8.8 19.7 %collective-permute-start.1 = (f32[4,16,8,128]{3,2,1,0:T(8,128)S(1)}, f32[4,16,8,128]{3,2,1,0:T(8,128)S(1)}, u32[]{:S(2)}, u32[]{:S(2)}) collective-permute-start(f32[4,16,8,128]{3,2,1,0:T(8,128)S(1)} %get-tuple-element.60), channel_id=1, source_target_pairs={{0,14},{1,15},{2,4},{3,5},{4,2},{5,3},{6,8},{7,9},{8,6},{9,7},{10,... | collective-permute-start | bytes 786440 | tf_op jit(solution)/shard_map/ppermute | solution.py:620
  15.5 13.0 %collective-permute-start.2 = (f32[24,8,128]{2,1,0:T(8,128)S(1)}, f32[24,8,128]{2,1,0:T(8,128)S(1)}, u32[]{:S(2)}, u32[]{:S(2)}) collective-permute-start(f32[24,8,128]{2,1,0:T(8,128)S(1)} %get-tuple-element.61), channel_id=1, source_target_pairs={{0,15},{1,2},{2,1},{3,4},{4,3},{5,6},{6,5},{7,8},{8,7},{9,10},{10,... | collective-permute-start | bytes 294920 | tf_op jit(solution)/shard_map/ppermute | solution.py:625
  16.9 11.5 %collective-permute-start.4 = (f32[40,128]{1,0:T(8,128)S(1)}, f32[40,128]{1,0:T(8,128)S(1)}, u32[]{:S(2)}, u32[]{:S(2)}) collective-permute-start(f32[40,128]{1,0:T(8,128)S(1)} %get-tuple-element.64), channel_id=1, source_target_pairs={{0,2},{1,3},{2,0},{3,1},{4,6},{5,7},{6,4},{7,5},{8,10},{9,11},{10,... | collective-permute-start | bytes 61448 | tf_op jit(solution)/shard_map/ppermute | solution.py:619
  21.0 13.5 %collective-permute-start.5 = (f32[40,128]{1,0:T(8,128)S(1)}, f32[40,128]{1,0:T(8,128)S(1)}, u32[]{:S(2)}, u32[]{:S(2)}) collective-permute-start(f32[40,128]{1,0:T(8,128)S(1)} %get-tuple-element.65), channel_id=1, source_target_pairs={{0,14},{1,15},{2,4},{3,5},{4,2},{5,3},{6,8},{7,9},{8,6},{9,7},{10,... | collective-permute-start | bytes 61448 | tf_op jit(solution)/shard_map/ppermute | solution.py:620
  35.0 5.2 %collective-permute-start.7 = (f32[184,128]{1,0:T(8,128)S(1)}, f32[184,128]{1,0:T(8,128)S(1)}, u32[]{:S(2)}, u32[]{:S(2)}) collective-permute-start(f32[184,128]{1,0:T(8,128)S(1)} %get-tuple-element.78), channel_id=1, source_target_pairs={{0,16},{16,0},{32,48},{48,32},{64,80},{80,64},{96,112},{112,96},{1... | collective-permute-start | bytes 282632 | tf_op jit(solution)/shard_map/ppermute | solution.py:643
  35.1 6.6 %collective-permute-start.8 = (f32[184,128]{1,0:T(8,128)S(1)}, f32[184,128]{1,0:T(8,128)S(1)}, u32[]{:S(2)}, u32[]{:S(2)}) collective-permute-start(f32[184,128]{1,0:T(8,128)S(1)} %get-tuple-element.79), channel_id=1, source_target_pairs={{0,240},{16,32},{32,16},{48,64},{64,48},{80,96},{96,80},{112,128},... | collective-permute-start | bytes 282632 | tf_op jit(solution)/shard_map/ppermute | solution.py:644
  36.2 4.0 %collective-permute-start.6 = (f32[80,128]{1,0:T(8,128)S(1)}, f32[80,128]{1,0:T(8,128)S(1)}, u32[]{:S(2)}, u32[]{:S(2)}) collective-permute-start(f32[80,128]{1,0:T(8,128)S(1)} %get-tuple-element.77.refs_11_), channel_id=1, source_target_pairs={{0,1},{1,0},{2,3},{3,2},{4,5},{5,4},{6,7},{7,6},{8,9},{9,8},{10,11... | collective-permute-start | bytes 122888 | tf_op jit(solution)/shard_map/ppermute | solution.py:647
  43.8 6.0 %collective-permute-start.10 = (f32[184,128]{1,0:T(8,128)S(1)}, f32[184,128]{1,0:T(8,128)S(1)}, u32[]{:S(2)}, u32[]{:S(2)}) collective-permute-start(f32[184,128]{1,0:T(8,128)S(1)} %get-tuple-element.84), channel_id=1, source_target_pairs={{0,16},{16,0},{32,48},{48,32},{64,80},{80,64},{96,112},{112,96},{1... | collective-permute-start | bytes 282632 | tf_op jit(solution)/shard_map/ppermute | solution.py:643
  43.9 7.2 %collective-permute-start.11 = (f32[184,128]{1,0:T(8,128)S(1)}, f32[184,128]{1,0:T(8,128)S(1)}, u32[]{:S(2)}, u32[]{:S(2)}) collective-permute-start(f32[184,128]{1,0:T(8,128)S(1)} %get-tuple-element.85), channel_id=1, source_target_pairs={{0,240},{16,32},{32,16},{48,64},{64,48},{80,96},{96,80},{112,128},... | collective-permute-start | bytes 282632 | tf_op jit(solution)/shard_map/ppermute | solution.py:644
  45.7 4.0 %collective-permute-start.9 = (f32[80,128]{1,0:T(8,128)S(1)}, f32[80,128]{1,0:T(8,128)S(1)}, u32[]{:S(2)}, u32[]{:S(2)}) collective-permute-start(f32[80,128]{1,0:T(8,128)S(1)} %get-tuple-element.83.refs_11_), channel_id=1, source_target_pairs={{0,1},{1,0},{2,3},{3,2},{4,5},{5,4},{6,7},{7,6},{8,9},{9,8},{10,11... | collective-permute-start | bytes 122888 | tf_op jit(solution)/shard_map/ppermute | solution.py:672
  53.1 5.2 %collective-permute-start.13 = (f32[184,128]{1,0:T(8,128)S(1)}, f32[184,128]{1,0:T(8,128)S(1)}, u32[]{:S(2)}, u32[]{:S(2)}) collective-permute-start(f32[184,128]{1,0:T(8,128)S(1)} %get-tuple-element.90), channel_id=1, source_target_pairs={{0,16},{16,0},{32,48},{48,32},{64,80},{80,64},{96,112},{112,96},{1... | collective-permute-start | bytes 282632 | tf_op jit(solution)/shard_map/ppermute | solution.py:643
  53.4 6.2 %collective-permute-start.14 = (f32[184,128]{1,0:T(8,128)S(1)}, f32[184,128]{1,0:T(8,128)S(1)}, u32[]{:S(2)}, u32[]{:S(2)}) collective-permute-start(f32[184,128]{1,0:T(8,128)S(1)} %get-tuple-element.91), channel_id=1, source_target_pairs={{0,240},{16,32},{32,16},{48,64},{64,48},{80,96},{96,80},{112,128},... | collective-permute-start | bytes 282632 | tf_op jit(solution)/shard_map/ppermute | solution.py:644
  54.3 4.0 %collective-permute-start.12 = (f32[80,128]{1,0:T(8,128)S(1)}, f32[80,128]{1,0:T(8,128)S(1)}, u32[]{:S(2)}, u32[]{:S(2)}) collective-permute-start(f32[80,128]{1,0:T(8,128)S(1)} %get-tuple-element.89.refs_11_), channel_id=1, source_target_pairs={{0,1},{1,0},{2,3},{3,2},{4,5},{5,4},{6,7},{7,6},{8,9},{9,8},{10,11... | collective-permute-start | bytes 122888 | tf_op jit(solution)/shard_map/ppermute | solution.py:672
  61.7 13.7 %copy-start = (bf16[4,16,32,128]{3,2,1,0:T(8,128)(2,1)S(1)}, bf16[4,16,32,128]{3,2,1,0:T(8,128)(2,1)}, u32[]{:S(2)}) copy-start(bf16[4,16,32,128]{3,2,1,0:T(8,128)(2,1)} %recv_ref.3) | copy-start | bytes 1572868
  61.7 5.0 %collective-permute-start.16 = (f32[184,128]{1,0:T(8,128)S(1)}, f32[184,128]{1,0:T(8,128)S(1)}, u32[]{:S(2)}, u32[]{:S(2)}) collective-permute-start(f32[184,128]{1,0:T(8,128)S(1)} %get-tuple-element.96), channel_id=1, source_target_pairs={{0,16},{16,0},{32,48},{48,32},{64,80},{80,64},{96,112},{112,96},{1... | collective-permute-start | bytes 282632 | tf_op jit(solution)/shard_map/ppermute | solution.py:643
  61.8 6.5 %collective-permute-start.17 = (f32[184,128]{1,0:T(8,128)S(1)}, f32[184,128]{1,0:T(8,128)S(1)}, u32[]{:S(2)}, u32[]{:S(2)}) collective-permute-start(f32[184,128]{1,0:T(8,128)S(1)} %get-tuple-element.97), channel_id=1, source_target_pairs={{0,240},{16,32},{32,16},{48,64},{64,48},{80,96},{96,80},{112,128},... | collective-permute-start | bytes 282632 | tf_op jit(solution)/shard_map/ppermute | solution.py:644
  62.7 4.0 %collective-permute-start.15 = (f32[80,128]{1,0:T(8,128)S(1)}, f32[80,128]{1,0:T(8,128)S(1)}, u32[]{:S(2)}, u32[]{:S(2)}) collective-permute-start(f32[80,128]{1,0:T(8,128)S(1)} %get-tuple-element.95.refs_11_), channel_id=1, source_target_pairs={{0,1},{1,0},{2,3},{3,2},{4,5},{5,4},{6,7},{7,6},{8,9},{9,8},{10,11... | collective-permute-start | bytes 122888 | tf_op jit(solution)/shard_map/ppermute | solution.py:672
  62.8 8.6 %collective-permute-start.18 = (f32[2,10,32,128]{3,2,1,0:T(8,128)S(1)}, f32[2,10,32,128]{3,2,1,0:T(8,128)S(1)}, u32[]{:S(2)}, u32[]{:S(2)}) collective-permute-start(f32[2,10,32,128]{3,2,1,0:T(8,128)S(1)} %get-tuple-element.101), channel_id=1, source_target_pairs={{0,16},{16,0},{32,48},{48,32},{64,80},{80,64},{96,112},{112,96},{1... | collective-permute-start | bytes 983048 | tf_op jit(solution)/shard_map/ppermute | solution.py:643
  62.8 12.5 %collective-permute-start.19 = (f32[2,10,32,128]{3,2,1,0:T(8,128)S(1)}, f32[2,10,32,128]{3,2,1,0:T(8,128)S(1)}, u32[]{:S(2)}, u32[]{:S(2)}) collective-permute-start(f32[2,10,32,128]{3,2,1,0:T(8,128)S(1)} %get-tuple-element.102), channel_id=1, source_target_pairs={{0,240},{16,32},{32,16},{48,64},{64,48},{80,96},{96,80},{112,128},... | collective-permute-start | bytes 983048 | tf_op jit(solution)/shard_map/ppermute | solution.py:644
  70.6 7.1 %collective-permute-start.20 = (f32[2,10,32,128]{3,2,1,0:T(8,128)S(1)}, f32[2,10,32,128]{3,2,1,0:T(8,128)S(1)}, u32[]{:S(2)}, u32[]{:S(2)}) collective-permute-start(f32[2,10,32,128]{3,2,1,0:T(8,128)S(1)} %get-tuple-element.104), channel_id=1, source_target_pairs={{0,16},{16,0},{32,48},{48,32},{64,80},{80,64},{96,112},{112,96},{1... | collective-permute-start | bytes 983048 | tf_op jit(solution)/shard_map/ppermute | solution.py:643
  70.6 11.4 %collective-permute-start.21 = (f32[2,10,32,128]{3,2,1,0:T(8,128)S(1)}, f32[2,10,32,128]{3,2,1,0:T(8,128)S(1)}, u32[]{:S(2)}, u32[]{:S(2)}) collective-permute-start(f32[2,10,32,128]{3,2,1,0:T(8,128)S(1)} %get-tuple-element.105), channel_id=1, source_target_pairs={{0,240},{16,32},{32,16},{48,64},{64,48},{80,96},{96,80},{112,128},... | collective-permute-start | bytes 983048 | tf_op jit(solution)/shard_map/ppermute | solution.py:644

commit v3 on v2

--- a/solution.py
+++ b/solution.py
@@ -345,7 +345,7 @@
     low_half = half == 0
     shape = (SOLID, DEPTH)
     lane = iota(shape, 1)
-    at_edge = lane == jnp.where(low_half, DEPTH - 1, 0)
+    facing = lane % 8 == jnp.where(low_half, 4, 5)
     sub = iota((8, DEPTH), 0)
     bottom = own_ref[pl.ds(0, SOLID)] + got_ref[pl.ds(0, SOLID)]
     velocity = own_ref[pl.ds(SOLID, SOLID)] + got_ref[pl.ds(SOLID, SOLID)]
@@ -355,7 +355,7 @@
         out.extend(turned(value, -8 * c, 1) if c else value for c in range(3))
 
     def of_half(value):
-        return jnp.where(low_half, value, turned(value, 2, 1))
+        return jnp.where(facing, jnp.where(low_half, value, turned(value, 2, 1)), 0.0)
 
     ghosts = [[of_half(v) for v in group] for group in (strip_before, strips, strip_after)]
 
@@ -366,7 +366,7 @@
             source, shift = ghosts[2][c], 123
         else:
             source, shift = ghosts[1][c], 123 - 8 * x
-        return jnp.where(at_edge, turned(source, shift, 1), 0.0)
+        return turned(source, shift, 1)
 
     faces = [received(xa_ref, xb_ref, pl.ds(SOLID * c, SOLID)) for c in range(3)]
     faces.append(received(xa_ref, xb_ref, pl.ds(3 * SOLID, WATER)))
@@ -505,12 +505,14 @@
 
 
 def image_kernel(
-    u0, u1, u2, u3, a_ref, b_ref, recv_ref,
+    u0, u1, u2, u3, first_a, first_b, third_a, third_b, recv_ref,
     out_hbm, open_ref, halo, weights, stage, sems,
 ):
-    for t in range(2):
+    for t, (a_ref, b_ref, n) in enumerate(
+        ((first_a, first_b, 0), (first_a, first_b, 1), (third_a, third_b, 0))
+    ):
         for k in range(LAG):
-            halo[t, k], halo[t, LAG + k] = lag_halos(a_ref[t, k], b_ref[t, k])
+            halo[t, k], halo[t, LAG + k] = lag_halos(a_ref[n, k], b_ref[n, k])
     for t in range(STEPS):
         for x in range(XS):
             weights[t, x] = recv_ref[t, x].astype(F32)
@@ -532,8 +534,8 @@
             at = x + lag - LAG
             total = column(0, at) * weights[0, x]
             total = total + column(1, at) * weights[1, x]
+            total = total + column(2, at) * weights[2, x]
             if low <= x < high:
-                total = total + column(2, at) * weights[2, x]
                 total = total + column(3, at) * weights[3, x]
                 stage[lag, x] = total.astype(jnp.bfloat16)
             else:
@@ -548,28 +550,34 @@
         copy.wait()
 
 
-def finish_kernel(open_ref, a_ref, b_ref, recv_ref, image_hbm, out_hbm, halo, stage, sems):
-    for t in range(2):
-        for k in range(LAG):
-            halo[t, k], halo[t, LAG + k] = lag_halos(a_ref[t, k], b_ref[t, k])
+def finish_kernel(with_a, open_ref, got_ref, recv_ref, image_hbm, out_hbm, stage, sems):
+    gx = lax.axis_index("gx")
+    beyond = (gx % 2 == 0) == with_a
     pairs = open_pairs()
-    copies = []
-    for n, lag in enumerate(k for k in range(2 * LAG + 1) if k != LAG):
-        low, high = own_range(lag)
-        start, stop = (0, low) if lag < LAG else (high, XS)
-        for x in range(start, stop):
-            at = x + lag if lag < LAG else x + lag - XS
-            total = open_ref[pairs[lag, x]] + halo[0, at] * recv_ref[2, x].astype(F32)
-            total = total + halo[1, at] * recv_ref[3, x].astype(F32)
-            stage[lag, x] = total.astype(jnp.bfloat16)
-        columns = pl.ds(start, stop - start)
-        copy = pltpu.make_async_copy(
-            stage.at[lag, columns], out_hbm.at[lag, columns], sems.at[n]
-        )
-        copy.start()
-        copies.append(copy)
-    for copy in copies:
-        copy.wait()
+
+    def finish(after):
+        present = gx < lax.axis_size("gx") - 1 if after else gx > 0
+        copies = []
+        for n in range(LAG):
+            lag = LAG + 1 + n if after else n
+            low, high = own_range(lag)
+            start, stop = (high, XS) if after else (0, low)
+            for x in range(start, stop):
+                plane = got_ref[0, x + lag - LAG - XS if after else x + lag]
+                plane = jnp.where(present, plane, 0.0)
+                total = open_ref[pairs[lag, x]] + plane * recv_ref[STEPS - 1, x].astype(F32)
+                stage[n, x] = total.astype(jnp.bfloat16)
+            columns = pl.ds(start, stop - start)
+            copy = pltpu.make_async_copy(
+                stage.at[n, columns], out_hbm.at[lag, columns], sems.at[n]
+            )
+            copy.start()
+            copies.append(copy)
+        for copy in copies:
+            copy.wait()
+
+    pl.when(beyond)(lambda: finish(True))
+    pl.when(jnp.logical_not(beyond))(lambda: finish(False))
 
 
 def call(body, outs, *args, specs=None, scratch=(), limit=40):
@@ -649,7 +657,7 @@
     verticals, reaches = [], []
     for t in range(STEPS):
         last = t == STEPS - 1
-        lags = (0, 2, 0, 2)[t]
+        lags = (0, 2, 1, 1)[t]
         if last:
             outs = [(3, XS, 32, DEPTH), (XS, 16, DEPTH), (XS, 32, DEPTH)]
         else:
@@ -679,29 +687,33 @@
     image, unfinished = pl.pallas_call(
         image_kernel,
         out_shape=[image_shape, open_shape],
-        in_specs=[VMEM] * 7,
+        in_specs=[VMEM] * 9,
         out_specs=[hbm, VMEM],
         scratch_shapes=[
-            pltpu.VMEM((2, 2 * LAG, OWN, DEPTH), F32),
+            pltpu.VMEM((STEPS - 1, 2 * LAG, OWN, DEPTH), F32),
             pltpu.VMEM((STEPS, XS, OWN, DEPTH), F32),
             stage,
             pltpu.SemaphoreType.DMA((lags,)),
         ],
         compiler_params=PARAMS,
-    )(*verticals, *reaches[0:2], recv_field)
-    image = pl.pallas_call(
-        finish_kernel,
-        out_shape=image_shape,
-        in_specs=[VMEM] * 4 + [hbm],
-        out_specs=hbm,
-        scratch_shapes=[
-            pltpu.VMEM((2, 2 * LAG, OWN, DEPTH), F32),
-            stage,
-            pltpu.SemaphoreType.DMA((lags - 1,)),
-        ],
-        input_output_aliases={4: 0},
-        compiler_params=PARAMS,
-    )(unfinished, *reaches[2:4], recv_field, image)
+    )(*verticals, *reaches[0:4], recv_field)
+    for with_a, got in ((True, reaches[4]), (False, reaches[5])):
+
+        def finish(*refs, with_a=with_a):
+            finish_kernel(with_a, *refs)
+
+        image = pl.pallas_call(
+            finish,
+            out_shape=image_shape,
+            in_specs=[VMEM] * 3 + [hbm],
+            out_specs=hbm,
+            scratch_shapes=[
+                pltpu.VMEM((LAG, XS, OWN, DEPTH), jnp.bfloat16),
+                pltpu.SemaphoreType.DMA((LAG,)),
+            ],
+            input_output_aliases={3: 0},
+            compiler_params=PARAMS,
+        )(unfinished, got, recv_field, image)
     return (p, u, image)
 
 

time: 84.1 us -> 83.7 us (level)
  waiting for transfers between devices: 33.8 us -> 30.8 us
  starting transfers between devices: 31.2 us -> 33.8 us
    ppermute x6 -> x7, waiting for transfers between devices: 14 us -> 11.3 us  [to_x(): lax.ppermute(second, 'gx', crossed(size_x, 1))]
    ppermute x6 -> x7, starting transfers between devices: 8.47 us -> 10.7 us  [to_x(): lax.ppermute(second, 'gx', crossed(size_x, 1))]
    pallas_call x1 -> x2, Pallas kernels: 1.36 us -> 1.74 us  [on_device(): pl.pallas_call(finish, out_shape=image_shape, in_specs=[VMEM] * 3 + [hbm]...]
  transfers between devices with their start and end apart: 22 -> 24, of which waited for: 13 -> 12; matrix products, arithmetic and copies ran while one was open for 0% -> 0% of each run, Pallas kernels for 5% -> 9%
where the time goes in v3:
time: 83.7 us; the launch traced here: 83.5 us
  starting transfers between devices  33.8 us (40%)
  waiting for transfers between devices  30.8 us (37%)
  Pallas kernels  15 us (18%)
  other arithmetic  2.96 us (4%)
  between operations  1 us (1%)
    ppermute x2, starting transfers between devices, to_y(): lax.ppermute(second, 'gy', crossed(size_y, 2))  13.9 us
    ppermute x4, waiting for transfers between devices, on_device(): got = lax.ppermute(own, 'gy', swapped(size_y, 1))  11.7 us
    ppermute x7, waiting for transfers between devices, to_x(): lax.ppermute(second, 'gx', crossed(size_x, 1))  11.3 us
    pallas_call x7, Pallas kernels, call(): pl.pallas_call(body, out_shape=[jax.ShapeDtypeStruct(shape, F32) for shap...  11 us
    ppermute x7, starting transfers between devices, to_x(): lax.ppermute(second, 'gx', crossed(size_x, 1))  10.7 us
    ppermute x2, waiting for transfers between devices, to_y(): lax.ppermute(second, 'gy', crossed(size_y, 2))  6.11 us
    ppermute x2, starting transfers between devices, to_y(): lax.ppermute(first, 'gy', swapped(size_y, 2))  4.95 us
    pallas_call x1, Pallas kernels, on_device(): pl.pallas_call(image_kernel, out_shape=[image_shape, open_shape], in_spec...  2.28 us
  transfers between devices with their start and end apart: 24, of which 12 were waited for; matrix products, arithmetic and copies ran while one was open for 0% of the time, Pallas kernels for 9%

profile of v3, /device:TPU:8, one launch (start us, length us, event | category | flops | bytes accessed | tf_op | source)
XLA Modules:
  0.0 83.5 jit_solution(16901541785018868323)
XLA Ops:
  0.7 0.7 compare_select_fusion
  1.4 0.1 subtract_convert_fusion.d_ref
  1.5 1.1 %pad_maximum_fusion.elastic = f32[2,16,32,128]{3,2,1,0:T(8,128)S(1)} fusion(f32[1,16,32,128]{3,2,1,0:T(8,128)} %bitcast.5, f32[1,16,32,128]{3,2,1,0:T(8,128)} %bitcast.6), kind=kLoop, calls=%fused_computation | loop fusion | flops 131072 | bytes 1048576 | tf_op jit(solution)/shard_map/stack | solution.py:611
  2.6 1.1 %pad_maximum_fusion.1.pressures = f32[3,16,16,128]{3,2,1,0:T(8,128)S(1)} fusion(f32[1,16,16,128]{3,2,1,0:T(8,128)} %bitcast.7, f32[1,16,16,128]{3,2,1,0:T(8,128)} %bitcast.8, f32[1,16,16,128]{3,2,1,0:T(8,128)} %bitcast.9), kind=kLoop, calls=%fused_computation.1 | loop fusion | flops 196608 | bytes 786432 | tf_op jit(solution)/shard_map/stack | solution.py:610
  3.6 2.0 %shard_map.112 = (f32[3,16,32,128]{3,2,1,0:T(8,128)S(1)}, f32[3,16,32,128]{3,2,1,0:T(8,128)S(1)}, f32[16,32,128]{2,1,0:T(8,128)S(1)}, f32[16,32,128]{2,1,0:T(8,1...) custom-call(f32[16,32,128]{2,1,0:T(8,128)S(1)} %subtract_convert_fus, ...), custom_call_target="tpu_custom_call" | custom-call | tf_op jit(solution)/shard_map/pallas_call | solution.py:584
  5.7 2.3 %collective-permute-start.3 = (f32[480,128]{1,0:T(8,128)S(1)}, f32[480,128]{1,0:T(8,128)S(1)}, u32[]{:S(2)}, u32[]{:S(2)}) collective-permute-start(f32[480,128]{1,0:T(8,128)S(1)} %get-tuple-element.64.own_ref), channel_id=1, source_target_pairs={{0,1},{1,0},{2,3},{3,2},{4,5},{5,4},{6,7},{7,6},{8,9},{9,8},{10,11... | collective-permute-start | bytes 737288 | tf_op jit(solution)/shard_map/ppermute | solution.py:631
  7.9 0.9 %collective-permute-start = (f32[4,16,8,128]{3,2,1,0:T(8,128)S(1)}, f32[4,16,8,128]{3,2,1,0:T(8,128)S(1)}, u32[]{:S(2)}, u32[]{:S(2)}) collective-permute-start(f32[4,16,8,128]{3,2,1,0:T(8,128)S(1)} %get-tuple-element.61), channel_id=1, source_target_pairs={{0,2},{1,3},{2,0},{3,1},{4,6},{5,7},{6,4},{7,5},{8,10},{9,11},{10,... | collective-permute-start | bytes 786440 | tf_op jit(solution)/shard_map/ppermute | solution.py:627
  8.8 6.7 %collective-permute-start.1 = (f32[4,16,8,128]{3,2,1,0:T(8,128)S(1)}, f32[4,16,8,128]{3,2,1,0:T(8,128)S(1)}, u32[]{:S(2)}, u32[]{:S(2)}) collective-permute-start(f32[4,16,8,128]{3,2,1,0:T(8,128)S(1)} %get-tuple-element.62), channel_id=1, source_target_pairs={{0,14},{1,15},{2,4},{3,5},{4,2},{5,3},{6,8},{7,9},{8,6},{9,7},{10,... | collective-permute-start | bytes 786440 | tf_op jit(solution)/shard_map/ppermute | solution.py:628
  15.5 0.0 collective-permute-start.2
  15.5 1.4 %collective-permute-done.3.got_ref.partner_ref = f32[480,128]{1,0:T(8,128)S(1)} collective-permute-done((f32[480,128]{1,0:T(8,128)S(1)}, f32[480,128]{1,0:T(8,128)S(1)}, u32[]{:S(2)}, u32[]{:S(2)}) %collective-permute-start.3) | collective-permute-done | bytes 245792 | tf_op jit(solution)/shard_map/ppermute | solution.py:631
  16.9 4.1 %collective-permute-start.4 = (f32[40,128]{1,0:T(8,128)S(1)}, f32[40,128]{1,0:T(8,128)S(1)}, u32[]{:S(2)}, u32[]{:S(2)}) collective-permute-start(f32[40,128]{1,0:T(8,128)S(1)} %get-tuple-element.66), channel_id=1, source_target_pairs={{0,2},{1,3},{2,0},{3,1},{4,6},{5,7},{6,4},{7,5},{8,10},{9,11},{10,... | collective-permute-start | bytes 61448 | tf_op jit(solution)/shard_map/ppermute | solution.py:627
  21.0 7.2 %collective-permute-start.5 = (f32[40,128]{1,0:T(8,128)S(1)}, f32[40,128]{1,0:T(8,128)S(1)}, u32[]{:S(2)}, u32[]{:S(2)}) collective-permute-start(f32[40,128]{1,0:T(8,128)S(1)} %get-tuple-element.67), channel_id=1, source_target_pairs={{0,14},{1,15},{2,4},{3,5},{4,2},{5,3},{6,8},{7,9},{8,6},{9,7},{10,... | collective-permute-start | bytes 61448 | tf_op jit(solution)/shard_map/ppermute | solution.py:628
  28.2 0.2 collective-permute-done.2.wo_ref
  28.4 0.0 collective-permute-done.ya_ref
  28.4 0.0 collective-permute-done.1.yb_ref
  28.5 0.0 collective-permute-done.4.ysa_ref
  28.5 6.1 %collective-permute-done.5.ysb_ref = f32[40,128]{1,0:T(8,128)S(1)} collective-permute-done((f32[40,128]{1,0:T(8,128)S(1)}, f32[40,128]{1,0:T(8,128)S(1)}, u32[]{:S(2)}, u32[]{:S(2)}) %collective-permute-start.5) | collective-permute-done | bytes 20512 | tf_op jit(solution)/shard_map/ppermute | solution.py:628
  34.6 0.4 shard_map.114
  35.0 0.1 collective-permute-start.7
  35.1 1.1 %collective-permute-start.8 = (f32[184,128]{1,0:T(8,128)S(1)}, f32[184,128]{1,0:T(8,128)S(1)}, u32[]{:S(2)}, u32[]{:S(2)}) collective-permute-start(f32[184,128]{1,0:T(8,128)S(1)} %get-tuple-element.81), channel_id=1, source_target_pairs={{0,240},{16,32},{32,16},{48,64},{64,48},{80,96},{96,80},{112,128},... | collective-permute-start | bytes 282632 | tf_op jit(solution)/shard_map/ppermute | solution.py:652
  36.2 0.8 collective-permute-start.6
  37.0 3.2 %collective-permute-done.6.refs_12_ = f32[80,128]{1,0:T(8,128)S(1)} collective-permute-done((f32[80,128]{1,0:T(8,128)S(1)}, f32[80,128]{1,0:T(8,128)S(1)}, u32[]{:S(2)}, u32[]{:S(2)}) %collective-permute-start.6) | collective-permute-done | bytes 40992 | tf_op jit(solution)/shard_map/ppermute | solution.py:655
  40.2 0.0 collective-permute-done.7.refs_13_
  40.2 1.5 %collective-permute-done.8.refs_14_ = f32[184,128]{1,0:T(8,128)S(1)} collective-permute-done((f32[184,128]{1,0:T(8,128)S(1)}, f32[184,128]{1,0:T(8,128)S(1)}, u32[]{:S(2)}, u32[]{:S(2)}) %collective-permute-start.8) | collective-permute-done | bytes 94240 | tf_op jit(solution)/shard_map/ppermute | solution.py:652
  41.7 2.1 %shard_map.115 = (f32[3,16,40,128]{3,2,1,0:T(8,128)S(1)}, f32[16,24,128]{2,1,0:T(8,128)S(1)}, f32[120,128]{1,0:T(8,128)S(1)}, f32[80,128]{1,0:T(8,128)S(1)}, f32...) custom-call(f32[3,16,40,128]{3,2,1,0:T(8,128)S(1)} %get-tuple-element.68.refs_0_.refs_1_, ...), custom_call_target="tpu_custom_call" | custom-call | tf_op jit(solution)/shard_map/pallas_call | solution.py:584
  43.7 0.1 collective-permute-start.10
  43.8 1.9 %collective-permute-start.11 = (f32[184,128]{1,0:T(8,128)S(1)}, f32[184,128]{1,0:T(8,128)S(1)}, u32[]{:S(2)}, u32[]{:S(2)}) collective-permute-start(f32[184,128]{1,0:T(8,128)S(1)} %get-tuple-element.87), channel_id=1, source_target_pairs={{0,240},{16,32},{32,16},{48,64},{64,48},{80,96},{96,80},{112,128},... | collective-permute-start | bytes 282632 | tf_op jit(solution)/shard_map/ppermute | solution.py:652
  45.7 0.0 collective-permute-start.9
  45.7 4.0 %collective-permute-done.9.refs_12_ = f32[80,128]{1,0:T(8,128)S(1)} collective-permute-done((f32[80,128]{1,0:T(8,128)S(1)}, f32[80,128]{1,0:T(8,128)S(1)}, u32[]{:S(2)}, u32[]{:S(2)}) %collective-permute-start.9) | collective-permute-done | bytes 40992 | tf_op jit(solution)/shard_map/ppermute | solution.py:680
  49.7 0.0 collective-permute-done.10.refs_13_
  49.7 1.3 %collective-permute-done.11.refs_14_ = f32[184,128]{1,0:T(8,128)S(1)} collective-permute-done((f32[184,128]{1,0:T(8,128)S(1)}, f32[184,128]{1,0:T(8,128)S(1)}, u32[]{:S(2)}, u32[]{:S(2)}) %collective-permute-start.11) | collective-permute-done | bytes 94240 | tf_op jit(solution)/shard_map/ppermute | solution.py:652
  51.0 2.1 %shard_map.116 = (f32[3,16,40,128]{3,2,1,0:T(8,128)S(1)}, f32[16,24,128]{2,1,0:T(8,128)S(1)}, f32[120,128]{1,0:T(8,128)S(1)}, f32[80,128]{1,0:T(8,128)S(1)}, f32...) custom-call(f32[3,16,40,128]{3,2,1,0:T(8,128)S(1)} %get-tuple-elemen, ...), custom_call_target="tpu_custom_call" | custom-call | tf_op jit(solution)/shard_map/pallas_call | solution.py:584
  53.1 0.3 collective-permute-start.13
  53.4 0.9 %collective-permute-start.14 = (f32[184,128]{1,0:T(8,128)S(1)}, f32[184,128]{1,0:T(8,128)S(1)}, u32[]{:S(2)}, u32[]{:S(2)}) collective-permute-start(f32[184,128]{1,0:T(8,128)S(1)} %get-tuple-element.93), channel_id=1, source_target_pairs={{0,240},{16,32},{32,16},{48,64},{64,48},{80,96},{96,80},{112,128},... | collective-permute-start | bytes 282632 | tf_op jit(solution)/shard_map/ppermute | solution.py:652
  54.3 0.2 collective-permute-start.12
  54.4 0.0 collective-permute-start.18
  54.4 2.9 %collective-permute-start.19 = (f32[2,10,32,128]{3,2,1,0:T(8,128)S(1)}, f32[2,10,32,128]{3,2,1,0:T(8,128)S(1)}, u32[]{:S(2)}, u32[]{:S(2)}) collective-permute-start(f32[2,10,32,128]{3,2,1,0:T(8,128)S(1)} %get-tuple-element.104), channel_id=1, source_target_pairs={{0,240},{16,32},{32,16},{48,64},{64,48},{80,96},{96,80},{112,128},... | collective-permute-start | bytes 983048 | tf_op jit(solution)/shard_map/ppermute | solution.py:652
  57.3 0.9 %collective-permute-done.12.refs_12_ = f32[80,128]{1,0:T(8,128)S(1)} collective-permute-done((f32[80,128]{1,0:T(8,128)S(1)}, f32[80,128]{1,0:T(8,128)S(1)}, u32[]{:S(2)}, u32[]{:S(2)}) %collective-permute-start.12) | collective-permute-done | bytes 40992 | tf_op jit(solution)/shard_map/ppermute | solution.py:680
  58.3 0.0 collective-permute-done.13.refs_13_
  58.3 1.6 %collective-permute-done.14.refs_14_ = f32[184,128]{1,0:T(8,128)S(1)} collective-permute-done((f32[184,128]{1,0:T(8,128)S(1)}, f32[184,128]{1,0:T(8,128)S(1)}, u32[]{:S(2)}, u32[]{:S(2)}) %collective-permute-start.14) | collective-permute-done | bytes 94240 | tf_op jit(solution)/shard_map/ppermute | solution.py:652
  59.9 2.1 %shard_map.117 = (f32[3,16,40,128]{3,2,1,0:T(8,128)S(1)}, f32[16,24,128]{2,1,0:T(8,128)S(1)}, f32[120,128]{1,0:T(8,128)S(1)}, f32[80,128]{1,0:T(8,128)S(1)}, f32...) custom-call(f32[3,16,40,128]{3,2,1,0:T(8,128)S(1)} %get-tuple-elemen, ...), custom_call_target="tpu_custom_call" | custom-call | tf_op jit(solution)/shard_map/pallas_call | solution.py:584
  62.1 0.0 copy-start
  62.1 0.1 collective-permute-start.20
  62.2 0.1 collective-permute-start.15
  62.3 0.4 collective-permute-start.16
  62.7 3.6 %collective-permute-done.15.refs_12_ = f32[80,128]{1,0:T(8,128)S(1)} collective-permute-done((f32[80,128]{1,0:T(8,128)S(1)}, f32[80,128]{1,0:T(8,128)S(1)}, u32[]{:S(2)}, u32[]{:S(2)}) %collective-permute-start.15) | collective-permute-done | bytes 40992 | tf_op jit(solution)/shard_map/ppermute | solution.py:680
  66.3 0.0 collective-permute-start.17
  66.3 0.0 collective-permute-done.16.refs_13_
  66.3 3.9 %collective-permute-start.21 = (f32[1,10,32,128]{3,2,1,0:T(8,128)S(1)}, f32[1,10,32,128]{3,2,1,0:T(8,128)S(1)}, u32[]{:S(2)}, u32[]{:S(2)}) collective-permute-start(f32[1,10,32,128]{3,2,1,0:T(8,128)S(1)} %get-tuple-element.106), channel_id=1, source_target_pairs={{0,240},{16,32},{32,16},{48,64},{64,48},{80,96},{96,80},{112,128},... | collective-permute-start | bytes 491528 | tf_op jit(solution)/shard_map/ppermute | solution.py:652
  70.1 3.2 %collective-permute-done.17.refs_14_ = f32[184,128]{1,0:T(8,128)S(1)} collective-permute-done((f32[184,128]{1,0:T(8,128)S(1)}, f32[184,128]{1,0:T(8,128)S(1)}, u32[]{:S(2)}, u32[]{:S(2)}) %collective-permute-start.17) | collective-permute-done | bytes 94240 | tf_op jit(solution)/shard_map/ppermute | solution.py:652
  73.3 2.3 %shard_map.118 = (f32[3,16,32,128]{3,2,1,0:T(8,128)}, f32[16,16,128]{2,1,0:T(8,128)}, f32[16,32,128]{2,1,0:T(8,128)S(1)}, f32[1,10,32,128]{3,2,1,0:T(8,128)S(1)}, f32[1,10,32,128]{3,2,1,0:T(8,128)S(1)}) custom-call(f32[3,16,40,128]{3,2,1,0:T(8,128)S(1)} %get-tuple-element.94.refs_0_.u2, f32[3,16,40,128]{3,2,1,0:T(8,128)S(1)} %get-tuple-element.88.refs_0_.refs_1_.u1, ...), custom_call_target="tpu_custom_call" | custom-call | tf_op jit(solution)/shard_map/pallas_call | solution.py:584
  75.6 0.0 collective-permute-start.23
  75.6 0.0 collective-permute-done.20.third_a
  75.6 0.1 collective-permute-start.22
  75.7 0.0 collective-permute-done.21.third_b
  75.7 0.0 collective-permute-done.18.first_a
  75.7 0.0 collective-permute-done.19.first_b
  75.7 0.0 copy-done
  75.7 2.3 %shard_map.119 = (bf16[21,16,32,128]{3,2,1,0:T(8,128)(2,1)}, f32[110,32,128]{2,1,0:T(8,128)S(1)}) custom-call(f32[3,16,40,128]{3,2,1,0:T(8,128)S(1)} %get-tuple-element.82.refs_0_.refs_1_.u0, f32[3,16,40,128]{3,2,1,0:T(8,128)S(1)} %get-tuple-element.88.refs_0_.refs_1_.u1, f32[3,16,40,128]{3,2,1,0:T(8,128)S(1)} %get-tuple-element.94.refs_0_.u2, ...), custom_call_target="tpu_custom_call" | custom-call | tf_op jit(solution)/shard_map/pallas_call | solution.py:687
  78.0 0.0 collective-permute-done.23.refs_1_
  78.0 0.9 %shard_map.120.refs_3_ = bf16[21,16,32,128]{3,2,1,0:T(8,128)(2,1)} custom-call(f32[110,32,128]{2,1,0:T(8,128)S(1)} %get-tuple-element.107.refs_0_, f32[1,10,32,128]{3,2,1,0:T(8,128)S(1)} %collective-permute-done.23.refs_1_, bf16[4,16,32,128]{3,2,1,0:T(8,128)(2,1)S(1)} %copy-done, ...), custom_call_target="tpu_custom_call", output_to_operand_aliasing={{}: (3, {})} | custom-call | tf_op jit(solution)/shard_map/pallas_call | solution.py:705
  78.9 3.6 %collective-permute-done.22.refs_1_ = f32[1,10,32,128]{3,2,1,0:T(8,128)S(1)} collective-permute-done((f32[1,10,32,128]{3,2,1,0:T(8,128)S(1)}, f32[1,10,32,128]{3,2,1,0:T(8,128)S(1)}, u32[]{:S(2)}, u32[]{:S(2)}) %collective-permute-start.22) | collective-permute-done | bytes 163872 | tf_op jit(solution)/shard_map/ppermute | solution.py:652
  82.5 0.9 %shard_map.121 = bf16[21,16,32,128]{3,2,1,0:T(8,128)(2,1)} custom-call(f32[110,32,128]{2,1,0:T(8,128)S(1)} %get-tuple-element.107.refs_0_, f32[1,10,32,128]{3,2,1,0:T(8,128)S(1)} %collective-permute-done.22.refs_1_, bf16[4,16,32,128]{3,2,1,0:T(8,128)(2,1)S(1)} %copy-done, bf16[21,16,32,128]{3,2,1,0:T(8,128)(2,1)} %shard_map.120.refs_3_), custom_call_target="tpu_custom_call", output_to_operand_aliasing={{}: (3, {})} | custom-call | tf_op jit(solution)/shard_map/pallas_call | solution.py:705
  (2 shorter events, 0.0 us)
Async XLA Ops:
  5.7 11.2 %collective-permute-start.3 = (f32[480,128]{1,0:T(8,128)S(1)}, f32[480,128]{1,0:T(8,128)S(1)}, u32[]{:S(2)}, u32[]{:S(2)}) collective-permute-start(f32[480,128]{1,0:T(8,128)S(1)} %get-tuple-element.64.own_ref), channel_id=1, source_target_pairs={{0,1},{1,0},{2,3},{3,2},{4,5},{5,4},{6,7},{7,6},{8,9},{9,8},{10,11... | collective-permute-start | bytes 737288 | tf_op jit(solution)/shard_map/ppermute | solution.py:631
  7.9 20.5 %collective-permute-start = (f32[4,16,8,128]{3,2,1,0:T(8,128)S(1)}, f32[4,16,8,128]{3,2,1,0:T(8,128)S(1)}, u32[]{:S(2)}, u32[]{:S(2)}) collective-permute-start(f32[4,16,8,128]{3,2,1,0:T(8,128)S(1)} %get-tuple-element.61), channel_id=1, source_target_pairs={{0,2},{1,3},{2,0},{3,1},{4,6},{5,7},{6,4},{7,5},{8,10},{9,11},{10,... | collective-permute-start | bytes 786440 | tf_op jit(solution)/shard_map/ppermute | solution.py:627
  8.8 19.7 %collective-permute-start.1 = (f32[4,16,8,128]{3,2,1,0:T(8,128)S(1)}, f32[4,16,8,128]{3,2,1,0:T(8,128)S(1)}, u32[]{:S(2)}, u32[]{:S(2)}) collective-permute-start(f32[4,16,8,128]{3,2,1,0:T(8,128)S(1)} %get-tuple-element.62), channel_id=1, source_target_pairs={{0,14},{1,15},{2,4},{3,5},{4,2},{5,3},{6,8},{7,9},{8,6},{9,7},{10,... | collective-permute-start | bytes 786440 | tf_op jit(solution)/shard_map/ppermute | solution.py:628
  15.5 13.0 %collective-permute-start.2 = (f32[24,8,128]{2,1,0:T(8,128)S(1)}, f32[24,8,128]{2,1,0:T(8,128)S(1)}, u32[]{:S(2)}, u32[]{:S(2)}) collective-permute-start(f32[24,8,128]{2,1,0:T(8,128)S(1)} %get-tuple-element.63), channel_id=1, source_target_pairs={{0,15},{1,2},{2,1},{3,4},{4,3},{5,6},{6,5},{7,8},{8,7},{9,10},{10,... | collective-permute-start | bytes 294920 | tf_op jit(solution)/shard_map/ppermute | solution.py:633
  16.9 11.5 %collective-permute-start.4 = (f32[40,128]{1,0:T(8,128)S(1)}, f32[40,128]{1,0:T(8,128)S(1)}, u32[]{:S(2)}, u32[]{:S(2)}) collective-permute-start(f32[40,128]{1,0:T(8,128)S(1)} %get-tuple-element.66), channel_id=1, source_target_pairs={{0,2},{1,3},{2,0},{3,1},{4,6},{5,7},{6,4},{7,5},{8,10},{9,11},{10,... | collective-permute-start | bytes 61448 | tf_op jit(solution)/shard_map/ppermute | solution.py:627
  21.0 13.5 %collective-permute-start.5 = (f32[40,128]{1,0:T(8,128)S(1)}, f32[40,128]{1,0:T(8,128)S(1)}, u32[]{:S(2)}, u32[]{:S(2)}) collective-permute-start(f32[40,128]{1,0:T(8,128)S(1)} %get-tuple-element.67), channel_id=1, source_target_pairs={{0,14},{1,15},{2,4},{3,5},{4,2},{5,3},{6,8},{7,9},{8,6},{9,7},{10,... | collective-permute-start | bytes 61448 | tf_op jit(solution)/shard_map/ppermute | solution.py:628
  35.0 5.2 %collective-permute-start.7 = (f32[184,128]{1,0:T(8,128)S(1)}, f32[184,128]{1,0:T(8,128)S(1)}, u32[]{:S(2)}, u32[]{:S(2)}) collective-permute-start(f32[184,128]{1,0:T(8,128)S(1)} %get-tuple-element.80), channel_id=1, source_target_pairs={{0,16},{16,0},{32,48},{48,32},{64,80},{80,64},{96,112},{112,96},{1... | collective-permute-start | bytes 282632 | tf_op jit(solution)/shard_map/ppermute | solution.py:651
  35.1 6.6 %collective-permute-start.8 = (f32[184,128]{1,0:T(8,128)S(1)}, f32[184,128]{1,0:T(8,128)S(1)}, u32[]{:S(2)}, u32[]{:S(2)}) collective-permute-start(f32[184,128]{1,0:T(8,128)S(1)} %get-tuple-element.81), channel_id=1, source_target_pairs={{0,240},{16,32},{32,16},{48,64},{64,48},{80,96},{96,80},{112,128},... | collective-permute-start | bytes 282632 | tf_op jit(solution)/shard_map/ppermute | solution.py:652
  36.2 4.0 %collective-permute-start.6 = (f32[80,128]{1,0:T(8,128)S(1)}, f32[80,128]{1,0:T(8,128)S(1)}, u32[]{:S(2)}, u32[]{:S(2)}) collective-permute-start(f32[80,128]{1,0:T(8,128)S(1)} %get-tuple-element.79.refs_11_), channel_id=1, source_target_pairs={{0,1},{1,0},{2,3},{3,2},{4,5},{5,4},{6,7},{7,6},{8,9},{9,8},{10,11... | collective-permute-start | bytes 122888 | tf_op jit(solution)/shard_map/ppermute | solution.py:655
  43.7 6.0 %collective-permute-start.10 = (f32[184,128]{1,0:T(8,128)S(1)}, f32[184,128]{1,0:T(8,128)S(1)}, u32[]{:S(2)}, u32[]{:S(2)}) collective-permute-start(f32[184,128]{1,0:T(8,128)S(1)} %get-tuple-element.86), channel_id=1, source_target_pairs={{0,16},{16,0},{32,48},{48,32},{64,80},{80,64},{96,112},{112,96},{1... | collective-permute-start | bytes 282632 | tf_op jit(solution)/shard_map/ppermute | solution.py:651
  43.8 7.2 %collective-permute-start.11 = (f32[184,128]{1,0:T(8,128)S(1)}, f32[184,128]{1,0:T(8,128)S(1)}, u32[]{:S(2)}, u32[]{:S(2)}) collective-permute-start(f32[184,128]{1,0:T(8,128)S(1)} %get-tuple-element.87), channel_id=1, source_target_pairs={{0,240},{16,32},{32,16},{48,64},{64,48},{80,96},{96,80},{112,128},... | collective-permute-start | bytes 282632 | tf_op jit(solution)/shard_map/ppermute | solution.py:652
  45.7 4.0 %collective-permute-start.9 = (f32[80,128]{1,0:T(8,128)S(1)}, f32[80,128]{1,0:T(8,128)S(1)}, u32[]{:S(2)}, u32[]{:S(2)}) collective-permute-start(f32[80,128]{1,0:T(8,128)S(1)} %get-tuple-element.85.refs_11_), channel_id=1, source_target_pairs={{0,1},{1,0},{2,3},{3,2},{4,5},{5,4},{6,7},{7,6},{8,9},{9,8},{10,11... | collective-permute-start | bytes 122888 | tf_op jit(solution)/shard_map/ppermute | solution.py:680
  53.1 5.2 %collective-permute-start.13 = (f32[184,128]{1,0:T(8,128)S(1)}, f32[184,128]{1,0:T(8,128)S(1)}, u32[]{:S(2)}, u32[]{:S(2)}) collective-permute-start(f32[184,128]{1,0:T(8,128)S(1)} %get-tuple-element.92), channel_id=1, source_target_pairs={{0,16},{16,0},{32,48},{48,32},{64,80},{80,64},{96,112},{112,96},{1... | collective-permute-start | bytes 282632 | tf_op jit(solution)/shard_map/ppermute | solution.py:651
  53.4 6.5 %collective-permute-start.14 = (f32[184,128]{1,0:T(8,128)S(1)}, f32[184,128]{1,0:T(8,128)S(1)}, u32[]{:S(2)}, u32[]{:S(2)}) collective-permute-start(f32[184,128]{1,0:T(8,128)S(1)} %get-tuple-element.93), channel_id=1, source_target_pairs={{0,240},{16,32},{32,16},{48,64},{64,48},{80,96},{96,80},{112,128},... | collective-permute-start | bytes 282632 | tf_op jit(solution)/shard_map/ppermute | solution.py:652
  54.3 4.0 %collective-permute-start.12 = (f32[80,128]{1,0:T(8,128)S(1)}, f32[80,128]{1,0:T(8,128)S(1)}, u32[]{:S(2)}, u32[]{:S(2)}) collective-permute-start(f32[80,128]{1,0:T(8,128)S(1)} %get-tuple-element.91.refs_11_), channel_id=1, source_target_pairs={{0,1},{1,0},{2,3},{3,2},{4,5},{5,4},{6,7},{7,6},{8,9},{9,8},{10,11... | collective-permute-start | bytes 122888 | tf_op jit(solution)/shard_map/ppermute | solution.py:680
  54.4 21.3 %collective-permute-start.18 = (f32[2,10,32,128]{3,2,1,0:T(8,128)S(1)}, f32[2,10,32,128]{3,2,1,0:T(8,128)S(1)}, u32[]{:S(2)}, u32[]{:S(2)}) collective-permute-start(f32[2,10,32,128]{3,2,1,0:T(8,128)S(1)} %get-tuple-element.103), channel_id=1, source_target_pairs={{0,16},{16,0},{32,48},{48,32},{64,80},{80,64},{96,112},{112,96},{1... | collective-permute-start | bytes 983048 | tf_op jit(solution)/shard_map/ppermute | solution.py:651
  54.4 21.3 %collective-permute-start.19 = (f32[2,10,32,128]{3,2,1,0:T(8,128)S(1)}, f32[2,10,32,128]{3,2,1,0:T(8,128)S(1)}, u32[]{:S(2)}, u32[]{:S(2)}) collective-permute-start(f32[2,10,32,128]{3,2,1,0:T(8,128)S(1)} %get-tuple-element.104), channel_id=1, source_target_pairs={{0,240},{16,32},{32,16},{48,64},{64,48},{80,96},{96,80},{112,128},... | collective-permute-start | bytes 983048 | tf_op jit(solution)/shard_map/ppermute | solution.py:652
  62.1 13.7 %copy-start = (bf16[4,16,32,128]{3,2,1,0:T(8,128)(2,1)S(1)}, bf16[4,16,32,128]{3,2,1,0:T(8,128)(2,1)}, u32[]{:S(2)}) copy-start(bf16[4,16,32,128]{3,2,1,0:T(8,128)(2,1)} %refs_2_.3) | copy-start | bytes 1572868
  62.1 13.5 %collective-permute-start.20 = (f32[1,10,32,128]{3,2,1,0:T(8,128)S(1)}, f32[1,10,32,128]{3,2,1,0:T(8,128)S(1)}, u32[]{:S(2)}, u32[]{:S(2)}) collective-permute-start(f32[1,10,32,128]{3,2,1,0:T(8,128)S(1)} %get-tuple-element.105), channel_id=1, source_target_pairs={{0,16},{16,0},{32,48},{48,32},{64,80},{80,64},{96,112},{112,96},{1... | collective-permute-start | bytes 491528 | tf_op jit(solution)/shard_map/ppermute | solution.py:651
  62.2 4.1 %collective-permute-start.15 = (f32[80,128]{1,0:T(8,128)S(1)}, f32[80,128]{1,0:T(8,128)S(1)}, u32[]{:S(2)}, u32[]{:S(2)}) collective-permute-start(f32[80,128]{1,0:T(8,128)S(1)} %get-tuple-element.97.refs_11_), channel_id=1, source_target_pairs={{0,1},{1,0},{2,3},{3,2},{4,5},{5,4},{6,7},{7,6},{8,9},{9,8},{10,11... | collective-permute-start | bytes 122888 | tf_op jit(solution)/shard_map/ppermute | solution.py:680
  62.3 4.0 %collective-permute-start.16 = (f32[184,128]{1,0:T(8,128)S(1)}, f32[184,128]{1,0:T(8,128)S(1)}, u32[]{:S(2)}, u32[]{:S(2)}) collective-permute-start(f32[184,128]{1,0:T(8,128)S(1)} %get-tuple-element.98), channel_id=1, source_target_pairs={{0,16},{16,0},{32,48},{48,32},{64,80},{80,64},{96,112},{112,96},{1... | collective-permute-start | bytes 282632 | tf_op jit(solution)/shard_map/ppermute | solution.py:651
  66.3 7.1 %collective-permute-start.17 = (f32[184,128]{1,0:T(8,128)S(1)}, f32[184,128]{1,0:T(8,128)S(1)}, u32[]{:S(2)}, u32[]{:S(2)}) collective-permute-start(f32[184,128]{1,0:T(8,128)S(1)} %get-tuple-element.99), channel_id=1, source_target_pairs={{0,240},{16,32},{32,16},{48,64},{64,48},{80,96},{96,80},{112,128},... | collective-permute-start | bytes 282632 | tf_op jit(solution)/shard_map/ppermute | solution.py:652
  66.3 9.4 %collective-permute-start.21 = (f32[1,10,32,128]{3,2,1,0:T(8,128)S(1)}, f32[1,10,32,128]{3,2,1,0:T(8,128)S(1)}, u32[]{:S(2)}, u32[]{:S(2)}) collective-permute-start(f32[1,10,32,128]{3,2,1,0:T(8,128)S(1)} %get-tuple-element.106), channel_id=1, source_target_pairs={{0,240},{16,32},{32,16},{48,64},{64,48},{80,96},{96,80},{112,128},... | collective-permute-start | bytes 491528 | tf_op jit(solution)/shard_map/ppermute | solution.py:652
  75.6 2.4 %collective-permute-start.23 = (f32[1,10,32,128]{3,2,1,0:T(8,128)S(1)}, f32[1,10,32,128]{3,2,1,0:T(8,128)S(1)}, u32[]{:S(2)}, u32[]{:S(2)}) collective-permute-start(f32[1,10,32,128]{3,2,1,0:T(8,128)S(1)} %get-tuple-element.109), channel_id=1, source_target_pairs={{0,16},{16,0},{32,48},{48,32},{64,80},{80,64},{96,112},{112,96},{1... | collective-permute-start | bytes 491528 | tf_op jit(solution)/shard_map/ppermute | solution.py:651
  75.6 6.9 %collective-permute-start.22 = (f32[1,10,32,128]{3,2,1,0:T(8,128)S(1)}, f32[1,10,32,128]{3,2,1,0:T(8,128)S(1)}, u32[]{:S(2)}, u32[]{:S(2)}) collective-permute-start(f32[1,10,32,128]{3,2,1,0:T(8,128)S(1)} %get-tuple-element.108), channel_id=1, source_target_pairs={{0,240},{16,32},{32,16},{48,64},{64,48},{80,96},{96,80},{112,128},... | collective-permute-start | bytes 491528 | tf_op jit(solution)/shard_map/ppermute | solution.py:652

commit v4 on v3

--- a/solution.py
+++ b/solution.py
@@ -335,12 +335,12 @@
     send_faces(lambda c, x: u_out[c, x], lambda x: p_out[x], xa_out, xb_out)
 
 
-def step_kernel(last, lags, *refs):
+def step_kernel(last, lags, early, *refs):
     u_ref, v_ref, s_ref, b_ref, d_ref, p_ref, q_ref, c_ref = refs[0:8]
     now_ref, old_ref, static_ref, own_ref, got_ref, xa_ref, xb_ref = refs[8:15]
     strip_rows = pl.ds(FACE, SOLID)
-    u_out, p_out = refs[15:17]
-    more = refs[17:]
+    u_out, p_out = refs[15 + early : 17 + early]
+    more = refs[17 + early :]
     gx, block, half = coordinates()
     low_half = half == 0
     shape = (SOLID, DEPTH)
@@ -664,11 +664,13 @@
             outs = [(3,) + solid, water, strip, pair, face, face]
         outs = outs + [(lags, LAG, 32, DEPTH)] * (2 if lags else 0)
 
-        def body(*refs, last=last, lags=lags):
-            step_kernel(last, lags, *refs)
+        arrived = reaches[0:1] if t == 2 else []
+
+        def body(*refs, last=last, lags=lags, early=len(arrived)):
+            step_kernel(last, lags, early, *refs)
 
         u_new, p_new, *more = call(
-            body, outs, u, v, s, b, d, p, q, c, now, old, static, own, got, *faces
+            body, outs, u, v, s, b, d, p, q, c, now, old, static, own, got, *faces, *arrived
         )
         v, u, q, p = u, u_new, p, p_new
         if last:

time: 83.7 us -> 81.1 us (0.969)
  waiting for transfers between devices: 30.8 us -> 27.9 us
    ppermute x7, waiting for transfers between devices: 11.3 us -> 5.18 us  [to_x(): lax.ppermute(second, 'gx', crossed(size_x, 1))]
    ppermute x4, waiting for transfers between devices: 11.7 us -> 14.9 us  [on_device(): got = lax.ppermute(own, 'gy', swapped(size_y, 1))]
  transfers between devices with their start and end apart: 24 -> 24, of which waited for: 12 -> 11; matrix products, arithmetic and copies ran while one was open for 0% -> 0% of each run, Pallas kernels for 9% -> 9%
where the time goes in v4:
time: 81.1 us; the launch traced here: 80.9 us
  starting transfers between devices  34.1 us (42%)
  waiting for transfers between devices  27.9 us (34%)
  Pallas kernels  15.1 us (19%)
  other arithmetic  2.96 us (4%)
  between operations  0.97 us (1%)
    ppermute x4, waiting for transfers between devices, on_device(): got = lax.ppermute(own, 'gy', swapped(size_y, 1))  14.9 us
    ppermute x2, starting transfers between devices, to_y(): lax.ppermute(second, 'gy', crossed(size_y, 2))  13.9 us
    pallas_call x7, Pallas kernels, call(): pl.pallas_call(body, out_shape=[jax.ShapeDtypeStruct(shape, F32) for shap...  11 us
    ppermute x7, starting transfers between devices, to_x(): lax.ppermute(second, 'gx', crossed(size_x, 1))  10.7 us
    ppermute x2, waiting for transfers between devices, to_y(): lax.ppermute(second, 'gy', crossed(size_y, 2))  6.11 us
    ppermute x7, waiting for transfers between devices, to_x(): lax.ppermute(second, 'gx', crossed(size_x, 1))  5.18 us
    ppermute x2, starting transfers between devices, to_y(): lax.ppermute(first, 'gy', swapped(size_y, 2))  4.95 us
    pallas_call x1, Pallas kernels, on_device(): pl.pallas_call(image_kernel, out_shape=[image_shape, open_shape], in_spec...  2.3 us
  transfers between devices with their start and end apart: 24, of which 11 were waited for; matrix products, arithmetic and copies ran while one was open for 0% of the time, Pallas kernels for 9%

profile of v4, /device:TPU:8, one launch (start us, length us, event | category | flops | bytes accessed | tf_op | source)
XLA Modules:
  0.0 80.9 jit_solution(13459092447678540505)
XLA Ops:
  0.7 0.7 compare_select_fusion
  1.4 0.1 subtract_convert_fusion.d_ref
  1.5 1.1 %pad_maximum_fusion.elastic = f32[2,16,32,128]{3,2,1,0:T(8,128)S(1)} fusion(f32[1,16,32,128]{3,2,1,0:T(8,128)} %bitcast.5, f32[1,16,32,128]{3,2,1,0:T(8,128)} %bitcast.6), kind=kLoop, calls=%fused_computation | loop fusion | flops 131072 | bytes 1048576 | tf_op jit(solution)/shard_map/stack | solution.py:611
  2.6 1.1 %pad_maximum_fusion.1.pressures = f32[3,16,16,128]{3,2,1,0:T(8,128)S(1)} fusion(f32[1,16,16,128]{3,2,1,0:T(8,128)} %bitcast.7, f32[1,16,16,128]{3,2,1,0:T(8,128)} %bitcast.8, f32[1,16,16,128]{3,2,1,0:T(8,128)} %bitcast.9), kind=kLoop, calls=%fused_computation.1 | loop fusion | flops 196608 | bytes 786432 | tf_op jit(solution)/shard_map/stack | solution.py:610
  3.6 2.0 %shard_map.112 = (f32[3,16,32,128]{3,2,1,0:T(8,128)S(1)}, f32[3,16,32,128]{3,2,1,0:T(8,128)S(1)}, f32[16,32,128]{2,1,0:T(8,128)S(1)}, f32[16,32,128]{2,1,0:T(8,1...) custom-call(f32[16,32,128]{2,1,0:T(8,128)S(1)} %subtract_convert_fus, ...), custom_call_target="tpu_custom_call" | custom-call | tf_op jit(solution)/shard_map/pallas_call | solution.py:584
  5.7 2.3 %collective-permute-start.3 = (f32[480,128]{1,0:T(8,128)S(1)}, f32[480,128]{1,0:T(8,128)S(1)}, u32[]{:S(2)}, u32[]{:S(2)}) collective-permute-start(f32[480,128]{1,0:T(8,128)S(1)} %get-tuple-element.64.own_ref), channel_id=1, source_target_pairs={{0,1},{1,0},{2,3},{3,2},{4,5},{5,4},{6,7},{7,6},{8,9},{9,8},{10,11... | collective-permute-start | bytes 737288 | tf_op jit(solution)/shard_map/ppermute | solution.py:631
  7.9 0.9 %collective-permute-start = (f32[4,16,8,128]{3,2,1,0:T(8,128)S(1)}, f32[4,16,8,128]{3,2,1,0:T(8,128)S(1)}, u32[]{:S(2)}, u32[]{:S(2)}) collective-permute-start(f32[4,16,8,128]{3,2,1,0:T(8,128)S(1)} %get-tuple-element.61), channel_id=1, source_target_pairs={{0,2},{1,3},{2,0},{3,1},{4,6},{5,7},{6,4},{7,5},{8,10},{9,11},{10,... | collective-permute-start | bytes 786440 | tf_op jit(solution)/shard_map/ppermute | solution.py:627
  8.8 6.7 %collective-permute-start.1 = (f32[4,16,8,128]{3,2,1,0:T(8,128)S(1)}, f32[4,16,8,128]{3,2,1,0:T(8,128)S(1)}, u32[]{:S(2)}, u32[]{:S(2)}) collective-permute-start(f32[4,16,8,128]{3,2,1,0:T(8,128)S(1)} %get-tuple-element.62), channel_id=1, source_target_pairs={{0,14},{1,15},{2,4},{3,5},{4,2},{5,3},{6,8},{7,9},{8,6},{9,7},{10,... | collective-permute-start | bytes 786440 | tf_op jit(solution)/shard_map/ppermute | solution.py:628
  15.5 0.0 collective-permute-start.2
  15.5 1.4 %collective-permute-done.3.got_ref.partner_ref = f32[480,128]{1,0:T(8,128)S(1)} collective-permute-done((f32[480,128]{1,0:T(8,128)S(1)}, f32[480,128]{1,0:T(8,128)S(1)}, u32[]{:S(2)}, u32[]{:S(2)}) %collective-permute-start.3) | collective-permute-done | bytes 245792 | tf_op jit(solution)/shard_map/ppermute | solution.py:631
  16.9 4.1 %collective-permute-start.4 = (f32[40,128]{1,0:T(8,128)S(1)}, f32[40,128]{1,0:T(8,128)S(1)}, u32[]{:S(2)}, u32[]{:S(2)}) collective-permute-start(f32[40,128]{1,0:T(8,128)S(1)} %get-tuple-element.66), channel_id=1, source_target_pairs={{0,2},{1,3},{2,0},{3,1},{4,6},{5,7},{6,4},{7,5},{8,10},{9,11},{10,... | collective-permute-start | bytes 61448 | tf_op jit(solution)/shard_map/ppermute | solution.py:627
  21.0 7.2 %collective-permute-start.5 = (f32[40,128]{1,0:T(8,128)S(1)}, f32[40,128]{1,0:T(8,128)S(1)}, u32[]{:S(2)}, u32[]{:S(2)}) collective-permute-start(f32[40,128]{1,0:T(8,128)S(1)} %get-tuple-element.67), channel_id=1, source_target_pairs={{0,14},{1,15},{2,4},{3,5},{4,2},{5,3},{6,8},{7,9},{8,6},{9,7},{10,... | collective-permute-start | bytes 61448 | tf_op jit(solution)/shard_map/ppermute | solution.py:628
  28.2 0.2 collective-permute-done.2.wo_ref
  28.4 0.0 collective-permute-done.ya_ref
  28.4 0.0 collective-permute-done.1.yb_ref
  28.5 0.0 collective-permute-done.4.ysa_ref
  28.5 6.1 %collective-permute-done.5.ysb_ref = f32[40,128]{1,0:T(8,128)S(1)} collective-permute-done((f32[40,128]{1,0:T(8,128)S(1)}, f32[40,128]{1,0:T(8,128)S(1)}, u32[]{:S(2)}, u32[]{:S(2)}) %collective-permute-start.5) | collective-permute-done | bytes 20512 | tf_op jit(solution)/shard_map/ppermute | solution.py:628
  34.6 0.4 shard_map.114
  35.0 0.1 collective-permute-start.7
  35.1 1.1 %collective-permute-start.8 = (f32[184,128]{1,0:T(8,128)S(1)}, f32[184,128]{1,0:T(8,128)S(1)}, u32[]{:S(2)}, u32[]{:S(2)}) collective-permute-start(f32[184,128]{1,0:T(8,128)S(1)} %get-tuple-element.81), channel_id=1, source_target_pairs={{0,240},{16,32},{32,16},{48,64},{64,48},{80,96},{96,80},{112,128},... | collective-permute-start | bytes 282632 | tf_op jit(solution)/shard_map/ppermute | solution.py:652
  36.2 0.8 %collective-permute-start.6 = (f32[80,128]{1,0:T(8,128)S(1)}, f32[80,128]{1,0:T(8,128)S(1)}, u32[]{:S(2)}, u32[]{:S(2)}) collective-permute-start(f32[80,128]{1,0:T(8,128)S(1)} %get-tuple-element.79.refs_11_), channel_id=1, source_target_pairs={{0,1},{1,0},{2,3},{3,2},{4,5},{5,4},{6,7},{7,6},{8,9},{9,8},{10,11... | collective-permute-start | bytes 122888 | tf_op jit(solution)/shard_map/ppermute | solution.py:655
  37.0 3.2 %collective-permute-done.6.refs_12_ = f32[80,128]{1,0:T(8,128)S(1)} collective-permute-done((f32[80,128]{1,0:T(8,128)S(1)}, f32[80,128]{1,0:T(8,128)S(1)}, u32[]{:S(2)}, u32[]{:S(2)}) %collective-permute-start.6) | collective-permute-done | bytes 40992 | tf_op jit(solution)/shard_map/ppermute | solution.py:655
  40.2 0.0 collective-permute-done.7.refs_13_
  40.2 1.5 %collective-permute-done.8.refs_14_ = f32[184,128]{1,0:T(8,128)S(1)} collective-permute-done((f32[184,128]{1,0:T(8,128)S(1)}, f32[184,128]{1,0:T(8,128)S(1)}, u32[]{:S(2)}, u32[]{:S(2)}) %collective-permute-start.8) | collective-permute-done | bytes 94240 | tf_op jit(solution)/shard_map/ppermute | solution.py:652
  41.7 2.1 %shard_map.115 = (f32[3,16,40,128]{3,2,1,0:T(8,128)S(1)}, f32[16,24,128]{2,1,0:T(8,128)S(1)}, f32[120,128]{1,0:T(8,128)S(1)}, f32[80,128]{1,0:T(8,128)S(1)}, f32...) custom-call(f32[3,16,40,128]{3,2,1,0:T(8,128)S(1)} %get-tuple-element.68.refs_0_.refs_1_, ...), custom_call_target="tpu_custom_call" | custom-call | tf_op jit(solution)/shard_map/pallas_call | solution.py:584
  43.7 0.1 collective-permute-start.10
  43.8 1.9 %collective-permute-start.11 = (f32[184,128]{1,0:T(8,128)S(1)}, f32[184,128]{1,0:T(8,128)S(1)}, u32[]{:S(2)}, u32[]{:S(2)}) collective-permute-start(f32[184,128]{1,0:T(8,128)S(1)} %get-tuple-element.87), channel_id=1, source_target_pairs={{0,240},{16,32},{32,16},{48,64},{64,48},{80,96},{96,80},{112,128},... | collective-permute-start | bytes 282632 | tf_op jit(solution)/shard_map/ppermute | solution.py:652
  45.7 0.0 collective-permute-start.9
  45.7 4.0 %collective-permute-done.9.refs_12_ = f32[80,128]{1,0:T(8,128)S(1)} collective-permute-done((f32[80,128]{1,0:T(8,128)S(1)}, f32[80,128]{1,0:T(8,128)S(1)}, u32[]{:S(2)}, u32[]{:S(2)}) %collective-permute-start.9) | collective-permute-done | bytes 40992 | tf_op jit(solution)/shard_map/ppermute | solution.py:682
  49.7 0.0 collective-permute-done.10.refs_13_
  49.7 1.3 %collective-permute-done.11.refs_14_ = f32[184,128]{1,0:T(8,128)S(1)} collective-permute-done((f32[184,128]{1,0:T(8,128)S(1)}, f32[184,128]{1,0:T(8,128)S(1)}, u32[]{:S(2)}, u32[]{:S(2)}) %collective-permute-start.11) | collective-permute-done | bytes 94240 | tf_op jit(solution)/shard_map/ppermute | solution.py:652
  51.0 2.1 %shard_map.116 = (f32[3,16,40,128]{3,2,1,0:T(8,128)S(1)}, f32[16,24,128]{2,1,0:T(8,128)S(1)}, f32[120,128]{1,0:T(8,128)S(1)}, f32[80,128]{1,0:T(8,128)S(1)}, f32...) custom-call(f32[3,16,40,128]{3,2,1,0:T(8,128)S(1)} %get-tuple-elemen, ...), custom_call_target="tpu_custom_call" | custom-call | tf_op jit(solution)/shard_map/pallas_call | solution.py:584
  53.1 0.3 collective-permute-start.15
  53.4 0.5 collective-permute-start.13
  53.9 0.8 collective-permute-start.14
  54.7 3.0 %collective-permute-start.19 = (f32[2,10,32,128]{3,2,1,0:T(8,128)S(1)}, f32[2,10,32,128]{3,2,1,0:T(8,128)S(1)}, u32[]{:S(2)}, u32[]{:S(2)}) collective-permute-start(f32[2,10,32,128]{3,2,1,0:T(8,128)S(1)} %get-tuple-element.104), channel_id=1, source_target_pairs={{0,240},{16,32},{32,16},{48,64},{64,48},{80,96},{96,80},{112,128},... | collective-permute-start | bytes 983048 | tf_op jit(solution)/shard_map/ppermute | solution.py:652
  57.7 0.0 collective-permute-start.12
  57.7 4.0 %collective-permute-done.12.refs_12_ = f32[80,128]{1,0:T(8,128)S(1)} collective-permute-done((f32[80,128]{1,0:T(8,128)S(1)}, f32[80,128]{1,0:T(8,128)S(1)}, u32[]{:S(2)}, u32[]{:S(2)}) %collective-permute-start.12) | collective-permute-done | bytes 40992 | tf_op jit(solution)/shard_map/ppermute | solution.py:682
  61.7 0.0 collective-permute-done.13.refs_13_
  61.7 0.0 collective-permute-done.14.refs_14_
  61.8 0.0 collective-permute-done.15.refs_15_.first_a
  61.8 2.1 %shard_map.117 = (f32[3,16,40,128]{3,2,1,0:T(8,128)S(1)}, f32[16,24,128]{2,1,0:T(8,128)S(1)}, f32[120,128]{1,0:T(8,128)S(1)}, f32[80,128]{1,0:T(8,128)S(1)}, f32...) custom-call(f32[3,16,40,128]{3,2,1,0:T(8,128)S(1)} %get-tuple-elemen, ...), custom_call_target="tpu_custom_call" | custom-call | tf_op jit(solution)/shard_map/pallas_call | solution.py:584
  63.9 0.0 copy-start
  63.9 0.1 collective-permute-start.17
  64.0 0.1 collective-permute-start.18
  64.1 0.2 collective-permute-start.16
  64.3 0.2 collective-permute-start.20
  64.5 3.7 %collective-permute-done.16.refs_12_ = f32[80,128]{1,0:T(8,128)S(1)} collective-permute-done((f32[80,128]{1,0:T(8,128)S(1)}, f32[80,128]{1,0:T(8,128)S(1)}, u32[]{:S(2)}, u32[]{:S(2)}) %collective-permute-start.16) | collective-permute-done | bytes 40992 | tf_op jit(solution)/shard_map/ppermute | solution.py:682
  68.2 2.6 %collective-permute-start.21 = (f32[1,10,32,128]{3,2,1,0:T(8,128)S(1)}, f32[1,10,32,128]{3,2,1,0:T(8,128)S(1)}, u32[]{:S(2)}, u32[]{:S(2)}) collective-permute-start(f32[1,10,32,128]{3,2,1,0:T(8,128)S(1)} %get-tuple-element.106), channel_id=1, source_target_pairs={{0,240},{16,32},{32,16},{48,64},{64,48},{80,96},{96,80},{112,128},... | collective-permute-start | bytes 491528 | tf_op jit(solution)/shard_map/ppermute | solution.py:652
  70.8 0.0 collective-permute-done.17.refs_13_
  70.8 0.0 collective-permute-done.18.refs_14_
  70.8 2.3 %shard_map.118 = (f32[3,16,32,128]{3,2,1,0:T(8,128)}, f32[16,16,128]{2,1,0:T(8,128)}, f32[16,32,128]{2,1,0:T(8,128)S(1)}, f32[1,10,32,128]{3,2,1,0:T(8,128)S(1)}, f32[1,10,32,128]{3,2,1,0:T(8,128)S(1)}) custom-call(f32[3,16,40,128]{3,2,1,0:T(8,128)S(1)} %get-tuple-element.95.refs_0_.u2, f32[3,16,40,128]{3,2,1,0:T(8,128)S(1)} %get-tuple-element.88.refs_0_.refs_1_.u1, ...), custom_call_target="tpu_custom_call" | custom-call | tf_op jit(solution)/shard_map/pallas_call | solution.py:584
  73.1 0.0 collective-permute-start.23
  73.1 1.2 %collective-permute-start.22 = (f32[1,10,32,128]{3,2,1,0:T(8,128)S(1)}, f32[1,10,32,128]{3,2,1,0:T(8,128)S(1)}, u32[]{:S(2)}, u32[]{:S(2)}) collective-permute-start(f32[1,10,32,128]{3,2,1,0:T(8,128)S(1)} %get-tuple-element.108), channel_id=1, source_target_pairs={{0,240},{16,32},{32,16},{48,64},{64,48},{80,96},{96,80},{112,128},... | collective-permute-start | bytes 491528 | tf_op jit(solution)/shard_map/ppermute | solution.py:652
  74.3 0.0 collective-permute-done.19.first_b
  74.3 0.0 collective-permute-done.20.third_a
  74.3 0.7 collective-permute-done.21.third_b
  75.0 0.0 copy-done
  75.0 2.3 %shard_map.119 = (bf16[21,16,32,128]{3,2,1,0:T(8,128)(2,1)}, f32[110,32,128]{2,1,0:T(8,128)S(1)}) custom-call(f32[3,16,40,128]{3,2,1,0:T(8,128)S(1)} %get-tuple-element.82.refs_0_.refs_1_.u0, f32[3,16,40,128]{3,2,1,0:T(8,128)S(1)} %get-tuple-element.88.refs_0_.refs_1_.u1, f32[3,16,40,128]{3,2,1,0:T(8,128)S(1)} %get-tuple-element.95.refs_0_.u2, ...), custom_call_target="tpu_custom_call" | custom-call | tf_op jit(solution)/shard_map/pallas_call | solution.py:689
  77.4 0.0 collective-permute-done.23.refs_1_
  77.4 0.9 %shard_map.120.refs_3_ = bf16[21,16,32,128]{3,2,1,0:T(8,128)(2,1)} custom-call(f32[110,32,128]{2,1,0:T(8,128)S(1)} %get-tuple-element.107.refs_0_, f32[1,10,32,128]{3,2,1,0:T(8,128)S(1)} %collective-permute-done.23.refs_1_, bf16[4,16,32,128]{3,2,1,0:T(8,128)(2,1)S(1)} %copy-done, ...), custom_call_target="tpu_custom_call", output_to_operand_aliasing={{}: (3, {})} | custom-call | tf_op jit(solution)/shard_map/pallas_call | solution.py:707
  78.2 1.7 %collective-permute-done.22.refs_1_ = f32[1,10,32,128]{3,2,1,0:T(8,128)S(1)} collective-permute-done((f32[1,10,32,128]{3,2,1,0:T(8,128)S(1)}, f32[1,10,32,128]{3,2,1,0:T(8,128)S(1)}, u32[]{:S(2)}, u32[]{:S(2)}) %collective-permute-start.22) | collective-permute-done | bytes 163872 | tf_op jit(solution)/shard_map/ppermute | solution.py:652
  79.9 0.9 %shard_map.121 = bf16[21,16,32,128]{3,2,1,0:T(8,128)(2,1)} custom-call(f32[110,32,128]{2,1,0:T(8,128)S(1)} %get-tuple-element.107.refs_0_, f32[1,10,32,128]{3,2,1,0:T(8,128)S(1)} %collective-permute-done.22.refs_1_, bf16[4,16,32,128]{3,2,1,0:T(8,128)(2,1)S(1)} %copy-done, bf16[21,16,32,128]{3,2,1,0:T(8,128)(2,1)} %shard_map.120.refs_3_), custom_call_target="tpu_custom_call", output_to_operand_aliasing={{}: (3, {})} | custom-call | tf_op jit(solution)/shard_map/pallas_call | solution.py:707
  (2 shorter events, 0.0 us)
Async XLA Ops:
  5.7 11.2 %collective-permute-start.3 = (f32[480,128]{1,0:T(8,128)S(1)}, f32[480,128]{1,0:T(8,128)S(1)}, u32[]{:S(2)}, u32[]{:S(2)}) collective-permute-start(f32[480,128]{1,0:T(8,128)S(1)} %get-tuple-element.64.own_ref), channel_id=1, source_target_pairs={{0,1},{1,0},{2,3},{3,2},{4,5},{5,4},{6,7},{7,6},{8,9},{9,8},{10,11... | collective-permute-start | bytes 737288 | tf_op jit(solution)/shard_map/ppermute | solution.py:631
  7.9 20.5 %collective-permute-start = (f32[4,16,8,128]{3,2,1,0:T(8,128)S(1)}, f32[4,16,8,128]{3,2,1,0:T(8,128)S(1)}, u32[]{:S(2)}, u32[]{:S(2)}) collective-permute-start(f32[4,16,8,128]{3,2,1,0:T(8,128)S(1)} %get-tuple-element.61), channel_id=1, source_target_pairs={{0,2},{1,3},{2,0},{3,1},{4,6},{5,7},{6,4},{7,5},{8,10},{9,11},{10,... | collective-permute-start | bytes 786440 | tf_op jit(solution)/shard_map/ppermute | solution.py:627
  8.8 19.7 %collective-permute-start.1 = (f32[4,16,8,128]{3,2,1,0:T(8,128)S(1)}, f32[4,16,8,128]{3,2,1,0:T(8,128)S(1)}, u32[]{:S(2)}, u32[]{:S(2)}) collective-permute-start(f32[4,16,8,128]{3,2,1,0:T(8,128)S(1)} %get-tuple-element.62), channel_id=1, source_target_pairs={{0,14},{1,15},{2,4},{3,5},{4,2},{5,3},{6,8},{7,9},{8,6},{9,7},{10,... | collective-permute-start | bytes 786440 | tf_op jit(solution)/shard_map/ppermute | solution.py:628
  15.5 13.0 %collective-permute-start.2 = (f32[24,8,128]{2,1,0:T(8,128)S(1)}, f32[24,8,128]{2,1,0:T(8,128)S(1)}, u32[]{:S(2)}, u32[]{:S(2)}) collective-permute-start(f32[24,8,128]{2,1,0:T(8,128)S(1)} %get-tuple-element.63), channel_id=1, source_target_pairs={{0,15},{1,2},{2,1},{3,4},{4,3},{5,6},{6,5},{7,8},{8,7},{9,10},{10,... | collective-permute-start | bytes 294920 | tf_op jit(solution)/shard_map/ppermute | solution.py:633
  16.9 11.5 %collective-permute-start.4 = (f32[40,128]{1,0:T(8,128)S(1)}, f32[40,128]{1,0:T(8,128)S(1)}, u32[]{:S(2)}, u32[]{:S(2)}) collective-permute-start(f32[40,128]{1,0:T(8,128)S(1)} %get-tuple-element.66), channel_id=1, source_target_pairs={{0,2},{1,3},{2,0},{3,1},{4,6},{5,7},{6,4},{7,5},{8,10},{9,11},{10,... | collective-permute-start | bytes 61448 | tf_op jit(solution)/shard_map/ppermute | solution.py:627
  21.0 13.5 %collective-permute-start.5 = (f32[40,128]{1,0:T(8,128)S(1)}, f32[40,128]{1,0:T(8,128)S(1)}, u32[]{:S(2)}, u32[]{:S(2)}) collective-permute-start(f32[40,128]{1,0:T(8,128)S(1)} %get-tuple-element.67), channel_id=1, source_target_pairs={{0,14},{1,15},{2,4},{3,5},{4,2},{5,3},{6,8},{7,9},{8,6},{9,7},{10,... | collective-permute-start | bytes 61448 | tf_op jit(solution)/shard_map/ppermute | solution.py:628
  35.0 5.2 %collective-permute-start.7 = (f32[184,128]{1,0:T(8,128)S(1)}, f32[184,128]{1,0:T(8,128)S(1)}, u32[]{:S(2)}, u32[]{:S(2)}) collective-permute-start(f32[184,128]{1,0:T(8,128)S(1)} %get-tuple-element.80), channel_id=1, source_target_pairs={{0,16},{16,0},{32,48},{48,32},{64,80},{80,64},{96,112},{112,96},{1... | collective-permute-start | bytes 282632 | tf_op jit(solution)/shard_map/ppermute | solution.py:651
  35.1 6.6 %collective-permute-start.8 = (f32[184,128]{1,0:T(8,128)S(1)}, f32[184,128]{1,0:T(8,128)S(1)}, u32[]{:S(2)}, u32[]{:S(2)}) collective-permute-start(f32[184,128]{1,0:T(8,128)S(1)} %get-tuple-element.81), channel_id=1, source_target_pairs={{0,240},{16,32},{32,16},{48,64},{64,48},{80,96},{96,80},{112,128},... | collective-permute-start | bytes 282632 | tf_op jit(solution)/shard_map/ppermute | solution.py:652
  36.2 4.0 %collective-permute-start.6 = (f32[80,128]{1,0:T(8,128)S(1)}, f32[80,128]{1,0:T(8,128)S(1)}, u32[]{:S(2)}, u32[]{:S(2)}) collective-permute-start(f32[80,128]{1,0:T(8,128)S(1)} %get-tuple-element.79.refs_11_), channel_id=1, source_target_pairs={{0,1},{1,0},{2,3},{3,2},{4,5},{5,4},{6,7},{7,6},{8,9},{9,8},{10,11... | collective-permute-start | bytes 122888 | tf_op jit(solution)/shard_map/ppermute | solution.py:655
  43.7 6.0 %collective-permute-start.10 = (f32[184,128]{1,0:T(8,128)S(1)}, f32[184,128]{1,0:T(8,128)S(1)}, u32[]{:S(2)}, u32[]{:S(2)}) collective-permute-start(f32[184,128]{1,0:T(8,128)S(1)} %get-tuple-element.86), channel_id=1, source_target_pairs={{0,16},{16,0},{32,48},{48,32},{64,80},{80,64},{96,112},{112,96},{1... | collective-permute-start | bytes 282632 | tf_op jit(solution)/shard_map/ppermute | solution.py:651
  43.8 7.2 %collective-permute-start.11 = (f32[184,128]{1,0:T(8,128)S(1)}, f32[184,128]{1,0:T(8,128)S(1)}, u32[]{:S(2)}, u32[]{:S(2)}) collective-permute-start(f32[184,128]{1,0:T(8,128)S(1)} %get-tuple-element.87), channel_id=1, source_target_pairs={{0,240},{16,32},{32,16},{48,64},{64,48},{80,96},{96,80},{112,128},... | collective-permute-start | bytes 282632 | tf_op jit(solution)/shard_map/ppermute | solution.py:652
  45.7 4.0 %collective-permute-start.9 = (f32[80,128]{1,0:T(8,128)S(1)}, f32[80,128]{1,0:T(8,128)S(1)}, u32[]{:S(2)}, u32[]{:S(2)}) collective-permute-start(f32[80,128]{1,0:T(8,128)S(1)} %get-tuple-element.85.refs_11_), channel_id=1, source_target_pairs={{0,1},{1,0},{2,3},{3,2},{4,5},{5,4},{6,7},{7,6},{8,9},{9,8},{10,11... | collective-permute-start | bytes 122888 | tf_op jit(solution)/shard_map/ppermute | solution.py:682
  53.1 8.6 %collective-permute-start.15 = (f32[2,10,32,128]{3,2,1,0:T(8,128)S(1)}, f32[2,10,32,128]{3,2,1,0:T(8,128)S(1)}, u32[]{:S(2)}, u32[]{:S(2)}) collective-permute-start(f32[2,10,32,128]{3,2,1,0:T(8,128)S(1)} %get-tuple-element.94), channel_id=1, source_target_pairs={{0,16},{16,0},{32,48},{48,32},{64,80},{80,64},{96,112},{112,96},{1... | collective-permute-start | bytes 983048 | tf_op jit(solution)/shard_map/ppermute | solution.py:651
  53.4 8.4 %collective-permute-start.13 = (f32[184,128]{1,0:T(8,128)S(1)}, f32[184,128]{1,0:T(8,128)S(1)}, u32[]{:S(2)}, u32[]{:S(2)}) collective-permute-start(f32[184,128]{1,0:T(8,128)S(1)} %get-tuple-element.92), channel_id=1, source_target_pairs={{0,16},{16,0},{32,48},{48,32},{64,80},{80,64},{96,112},{112,96},{1... | collective-permute-start | bytes 282632 | tf_op jit(solution)/shard_map/ppermute | solution.py:651
  53.9 7.9 %collective-permute-start.14 = (f32[184,128]{1,0:T(8,128)S(1)}, f32[184,128]{1,0:T(8,128)S(1)}, u32[]{:S(2)}, u32[]{:S(2)}) collective-permute-start(f32[184,128]{1,0:T(8,128)S(1)} %get-tuple-element.93), channel_id=1, source_target_pairs={{0,240},{16,32},{32,16},{48,64},{64,48},{80,96},{96,80},{112,128},... | collective-permute-start | bytes 282632 | tf_op jit(solution)/shard_map/ppermute | solution.py:652
  54.7 19.6 %collective-permute-start.19 = (f32[2,10,32,128]{3,2,1,0:T(8,128)S(1)}, f32[2,10,32,128]{3,2,1,0:T(8,128)S(1)}, u32[]{:S(2)}, u32[]{:S(2)}) collective-permute-start(f32[2,10,32,128]{3,2,1,0:T(8,128)S(1)} %get-tuple-element.104), channel_id=1, source_target_pairs={{0,240},{16,32},{32,16},{48,64},{64,48},{80,96},{96,80},{112,128},... | collective-permute-start | bytes 983048 | tf_op jit(solution)/shard_map/ppermute | solution.py:652
  57.7 4.0 %collective-permute-start.12 = (f32[80,128]{1,0:T(8,128)S(1)}, f32[80,128]{1,0:T(8,128)S(1)}, u32[]{:S(2)}, u32[]{:S(2)}) collective-permute-start(f32[80,128]{1,0:T(8,128)S(1)} %get-tuple-element.91.refs_11_), channel_id=1, source_target_pairs={{0,1},{1,0},{2,3},{3,2},{4,5},{5,4},{6,7},{7,6},{8,9},{9,8},{10,11... | collective-permute-start | bytes 122888 | tf_op jit(solution)/shard_map/ppermute | solution.py:682
  63.9 11.2 %copy-start = (bf16[4,16,32,128]{3,2,1,0:T(8,128)(2,1)S(1)}, bf16[4,16,32,128]{3,2,1,0:T(8,128)(2,1)}, u32[]{:S(2)}) copy-start(bf16[4,16,32,128]{3,2,1,0:T(8,128)(2,1)} %refs_2_.3) | copy-start | bytes 1572868
  63.9 6.9 %collective-permute-start.17 = (f32[184,128]{1,0:T(8,128)S(1)}, f32[184,128]{1,0:T(8,128)S(1)}, u32[]{:S(2)}, u32[]{:S(2)}) collective-permute-start(f32[184,128]{1,0:T(8,128)S(1)} %get-tuple-element.99), channel_id=1, source_target_pairs={{0,16},{16,0},{32,48},{48,32},{64,80},{80,64},{96,112},{112,96},{1... | collective-permute-start | bytes 282632 | tf_op jit(solution)/shard_map/ppermute | solution.py:651
  64.0 6.8 %collective-permute-start.18 = (f32[184,128]{1,0:T(8,128)S(1)}, f32[184,128]{1,0:T(8,128)S(1)}, u32[]{:S(2)}, u32[]{:S(2)}) collective-permute-start(f32[184,128]{1,0:T(8,128)S(1)} %get-tuple-element.100), channel_id=1, source_target_pairs={{0,240},{16,32},{32,16},{48,64},{64,48},{80,96},{96,80},{112,128},... | collective-permute-start | bytes 282632 | tf_op jit(solution)/shard_map/ppermute | solution.py:652
  64.1 4.1 %collective-permute-start.16 = (f32[80,128]{1,0:T(8,128)S(1)}, f32[80,128]{1,0:T(8,128)S(1)}, u32[]{:S(2)}, u32[]{:S(2)}) collective-permute-start(f32[80,128]{1,0:T(8,128)S(1)} %get-tuple-element.98.refs_11_), channel_id=1, source_target_pairs={{0,1},{1,0},{2,3},{3,2},{4,5},{5,4},{6,7},{7,6},{8,9},{9,8},{10,11... | collective-permute-start | bytes 122888 | tf_op jit(solution)/shard_map/ppermute | solution.py:682
  64.3 10.0 %collective-permute-start.20 = (f32[1,10,32,128]{3,2,1,0:T(8,128)S(1)}, f32[1,10,32,128]{3,2,1,0:T(8,128)S(1)}, u32[]{:S(2)}, u32[]{:S(2)}) collective-permute-start(f32[1,10,32,128]{3,2,1,0:T(8,128)S(1)} %get-tuple-element.105), channel_id=1, source_target_pairs={{0,16},{16,0},{32,48},{48,32},{64,80},{80,64},{96,112},{112,96},{1... | collective-permute-start | bytes 491528 | tf_op jit(solution)/shard_map/ppermute | solution.py:651
  68.2 6.9 %collective-permute-start.21 = (f32[1,10,32,128]{3,2,1,0:T(8,128)S(1)}, f32[1,10,32,128]{3,2,1,0:T(8,128)S(1)}, u32[]{:S(2)}, u32[]{:S(2)}) collective-permute-start(f32[1,10,32,128]{3,2,1,0:T(8,128)S(1)} %get-tuple-element.106), channel_id=1, source_target_pairs={{0,240},{16,32},{32,16},{48,64},{64,48},{80,96},{96,80},{112,128},... | collective-permute-start | bytes 491528 | tf_op jit(solution)/shard_map/ppermute | solution.py:652
  73.1 4.3 %collective-permute-start.23 = (f32[1,10,32,128]{3,2,1,0:T(8,128)S(1)}, f32[1,10,32,128]{3,2,1,0:T(8,128)S(1)}, u32[]{:S(2)}, u32[]{:S(2)}) collective-permute-start(f32[1,10,32,128]{3,2,1,0:T(8,128)S(1)} %get-tuple-element.109), channel_id=1, source_target_pairs={{0,16},{16,0},{32,48},{48,32},{64,80},{80,64},{96,112},{112,96},{1... | collective-permute-start | bytes 491528 | tf_op jit(solution)/shard_map/ppermute | solution.py:651
  73.1 6.9 %collective-permute-start.22 = (f32[1,10,32,128]{3,2,1,0:T(8,128)S(1)}, f32[1,10,32,128]{3,2,1,0:T(8,128)S(1)}, u32[]{:S(2)}, u32[]{:S(2)}) collective-permute-start(f32[1,10,32,128]{3,2,1,0:T(8,128)S(1)} %get-tuple-element.108), channel_id=1, source_target_pairs={{0,240},{16,32},{32,16},{48,64},{64,48},{80,96},{96,80},{112,128},... | collective-permute-start | bytes 491528 | tf_op jit(solution)/shard_map/ppermute | solution.py:652
